TPU v7x, 256 devices: a whole 4x4x8 slice. The times are simulated.
256 devices in a mesh: stn: 128 (over y_lo, z, x, core), tpl: 2 (over y_hi).
Axes of the slice: x: 4, y: 4 (y_hi: 2, y_lo: 2; y = y_hi * 2 + y_lo), z: 8, core: 2. Of those that a mesh axis runs over, the one named last changes fastest.
Arguments:
- archive: bfloat16 [8192, 17408], P('stn'), may hold values from -400 to 400
- slot_of_row: int32 [8192], P('stn'), may hold values from 0 to 8191, as said below
- templates: bfloat16 [64, 30, 600], P('tpl'), may hold values from -5 to 5
- template_channels: int32 [64, 30], P('tpl'), may hold values from 0 to 8191, as said below
- moveouts: int32 [64, 30], P('tpl'), may hold values from 0 to 384, as said below
Outputs:
- grouped: bfloat16 [8192, 17408], P('stn')
- stack: float32 [64, 16384], P('tpl', 'stn')
Inputs may be any that keep to these rules, and one draw needn't show every extreme that they name: `slot_of_row`: A permutation: channel p in owner order belongs to index p // 64 of stn. Of the 64 rows held by one index of stn, at most 2 go to any one owner, and in every draw some owner receives exactly 2 of them. `template_channels`: among the templates of one index of tpl, at most 22 entries name channels of any one owner, and one owner is named exactly 22 times. `moveouts`: the first channel of every template has moveout 0; some entry equals 384.
All inputs are finite; a program needn't handle non-finite values.
Results may differ from a plain program's by a relative error of at most 0.001.
Values may be sent and summed in bfloat16 or wider, within the bound.
No kernel may reach another device: no remote copies, remote signals or barrier semaphores. Data moves between devices by JAX's collectives and lax.ppermute only.
A program may use at most 128 MiB of HBM per device.

v0:
```python
import math

import jax
import jax.numpy as jnp
from jax import lax
from jax.sharding import PartitionSpec as P

MVMAX = 384
L = 16384
TPAD = 640


EPSILON = 1e-06


def pack_rows(archive_part, slot_local, stations, capacity):
    row_count = archive_part.shape[0]
    target = slot_local // row_count
    position = slot_local % row_count
    onehot = (target[:, None] == jnp.arange(stations, dtype=jnp.int32)[None, :]).astype(jnp.int32)
    before = jnp.cumsum(onehot, axis=0) - onehot
    rank_in = jnp.sum(before * onehot, axis=1)
    where_to = target * capacity + rank_in
    buffer = (
        jnp.zeros((stations * capacity, archive_part.shape[1]), archive_part.dtype)
        .at[where_to]
        .set(archive_part)
    )
    places = jnp.full((stations * capacity,), -1, jnp.int32).at[where_to].set(position)
    return (buffer, places)


def unpack_rows(received, places, row_count):
    safe_places = jnp.where(places < 0, row_count, places)
    return (
        jnp.zeros((row_count, received.shape[1]), received.dtype)
        .at[safe_places]
        .set(received, mode="drop")
    )


def take_lags(series, lag_shift):
    return lax.dynamic_slice_in_dim(series, lag_shift, L)


def correlate(grouped, templates, template_channels, moveouts, my_index, stations):
    row_count, sample_count = grouped.shape
    local_templates, channels_per, length = templates.shape
    capacity_refs = max(4, 3 * local_templates * channels_per // stations)
    flat_channels = template_channels.reshape(-1)
    is_owned = flat_channels // row_count == my_index
    running = jnp.cumsum(is_owned.astype(jnp.int32)) - 1
    target = jnp.where(is_owned, running, capacity_refs)
    entries = jnp.arange(flat_channels.shape[0], dtype=jnp.int32)
    ref_entry = jnp.zeros((capacity_refs,), jnp.int32).at[target].set(entries, mode="drop")
    ref_valid = jnp.zeros((capacity_refs,), jnp.float32).at[target].set(1.0, mode="drop")
    ref_row = flat_channels[ref_entry] % row_count
    ref_shift = moveouts.reshape(-1)[ref_entry]
    ref_wave = templates.reshape(-1, length)[ref_entry]
    tile_count = (L + MVMAX) // 128
    spread = TPAD // 128
    tile_rows = grouped[ref_row].reshape(capacity_refs, sample_count // 128, 128)
    windows = jnp.concatenate(
        [tile_rows[:, offset_tile : offset_tile + tile_count] for offset_tile in range(spread + 1)],
        axis=2,
    )
    offsets = (
        jnp.arange(TPAD + 128, dtype=jnp.int32)[:, None] - jnp.arange(128, dtype=jnp.int32)[None, :]
    )
    inside = (offsets >= 0) & (offsets < length)
    clipped = jnp.clip(offsets, 0, length - 1)
    toeplitz = jnp.where(inside[None], ref_wave[:, clipped], jnp.zeros((), ref_wave.dtype))
    products = jnp.einsum("kbu,kuj->kbj", windows, toeplitz, preferred_element_type=jnp.float32)
    windows_full = windows.astype(jnp.float32)
    energy = jnp.einsum(
        "kbu,uj->kbj",
        windows_full * windows_full,
        inside.astype(jnp.float32),
        precision=lax.Precision.HIGHEST,
    )
    wave_full = ref_wave.astype(jnp.float32)
    template_power = jnp.sum(wave_full * wave_full, axis=1)
    normalized = (
        products.reshape(capacity_refs, -1)
        / length
        / jnp.sqrt(
            (energy.reshape(capacity_refs, -1) / length + EPSILON)
            * (template_power[:, None] / length + EPSILON)
        )
    )
    shifted = jax.vmap(take_lags)(normalized, ref_shift) * ref_valid[:, None]
    owner_of = ref_entry // channels_per
    selector = (owner_of[None, :] == jnp.arange(local_templates, dtype=jnp.int32)[:, None]).astype(
        jnp.float32
    ) * ref_valid[None, :]
    return jnp.dot(selector, shifted, precision=lax.Precision.HIGHEST) * math.sqrt(
        length / channels_per
    )


def shards(archive, slot_of_row, templates, template_channels, moveouts):
    stations = lax.axis_size("stn")
    my_index = lax.axis_index("stn")
    row_count, sample_count = archive.shape
    capacity = max(2, 2 * row_count // stations)
    buffer, places = pack_rows(archive, slot_of_row, stations, capacity)
    received, got_places = (
        lax.all_to_all(buffer, "stn", split_axis=0, concat_axis=0, tiled=True),
        lax.all_to_all(places, "stn", split_axis=0, concat_axis=0, tiled=True),
    )
    grouped = unpack_rows(received, got_places, row_count)
    local_stack = correlate(grouped, templates, template_channels, moveouts, my_index, stations)
    segment = L // stations
    summed = lax.psum(local_stack, "stn")
    stack_part = lax.dynamic_slice_in_dim(summed, my_index * segment, segment, 1)
    return (grouped, stack_part)


def solution(mesh):
    in_specs = (P("stn", None), P("stn"), P("tpl", None, None), P("tpl", None), P("tpl", None))
    out_specs = (P("stn", None), P("tpl", "stn"))
    return jax.shard_map(shards, mesh=mesh, in_specs=in_specs, out_specs=out_specs, check_vma=False)
```

profile of v0, /device:TPU:16, one launch (start us, length us, event | category | flops | bytes accessed | tf_op | source)
XLA Modules:
  0.0 1648.2 jit_solution(901367341670598744)
XLA Ops:
  9.7 13.9 all-to-all-start
  23.6 9.7 scatter_custom_fusion.1
  33.3 13.4 all_to_all.19
  46.8 20.2 %all-to-all-start.1 = ((bf16[128,2,17408]{2,1,0:T(2,128)(2,1)}), bf16[128,2,17408]{2,1,0:T(2,128)(2,1)}, u32[]{:S(2)}, u32[]{:S(2)}) async-start(bf16[128,2,17408]{2,1,0:T(2,128)(2,1)} %all_to_all.19), calls=%async_computation.1 | async-start | bytes 17825792 | tf_op jit(solution)/shard_map/all_to_all | solution.py:108
  67.8 5.2 scatter_custom_fusion.3
  75.6 340.7 %gather_fusion.3 = bf16[98304,22]{1,0:T(8,128)(2,1)} fusion(bf16[22,600]{0,1:T(8,128)(2,1)S(1)} %copy.15, s32[98304]{0:T(1024)S(1)} %fusion.20), kind=kCustom, calls=%fused_computation.3 | custom fusion | bytes 9043968 | tf_op jit(solution)/shard_map/gather | solution.py:72
  416.3 20.6 %copy.16 = bf16[768,128,22]{1,0,2:T(8,128)(2,1)} copy(bf16[768,128,22]{2,1,0:T(8,128)(2,1)} %bitcast.42) | data formatting | bytes 8650752 | tf_op jit(solution)/shard_map/gather | solution.py:72
  437.6 5.2 scatter_custom_fusion.4
  444.6 13.5 reshape.269
  458.1 15.1 scatter_custom_fusion.2
  476.5 4.8 multiply_add_fusion
  485.1 60.4 %while.1 = (s32[]{:T(128)}, f32[22,16768]{1,0:T(8,128)S(1)}, s32[22,2]{0,1:T(2,128)S(1)}, f32[22,16384]{1,0:T(8,128)S(1)}, s32[]{:T(128)}, /*index=5*/s32[]{:T(128)}) while((s32[]{:T(128)}, f32[22,16768]{1,0:T(8,128)S(1)}, s32[22,2]{0,1:T(2,128)S(1)}, f32[22,16384]{1,0:T(8,128)S(1)}, s32[]{:T(128)}, /*index=5*/s32[]{:T(128)}) %tuple.30), condition=%wide.while_cond, body=%wide.while_body.sunk | while | flops 2 | bytes 262257 | solution.py:43
  486.0 1.5 dynamic-slice.7
  488.8 1.5 dynamic-slice.7
  494.2 1.5 dynamic-slice.7
  497.0 1.5 dynamic-slice.7
  499.7 1.5 dynamic-slice.7
  502.5 1.5 dynamic-slice.7
  505.2 1.5 dynamic-slice.7
  507.9 1.5 dynamic-slice.7
  510.7 1.5 dynamic-slice.7
  513.4 1.5 dynamic-slice.7
  516.1 1.5 dynamic-slice.7
  518.9 1.5 dynamic-slice.7
  521.6 1.5 dynamic-slice.7
  524.3 1.5 dynamic-slice.7
  529.8 1.5 dynamic-slice.7
  532.5 1.5 dynamic-slice.7
  535.3 1.5 dynamic-slice.7
  538.0 1.5 dynamic-slice.7
  545.5 3.2 convolution_multiply_fusion
  548.7 1090.8 %all-reduce.3.cloned.1.call-done = f32[32,16384]{1,0:T(8,128)} async-done(((f32[32,16384]{1,0:T(8,128)}), f32[32,16384]{1,0:T(8,128)}) %all-reduce.3.cloned.1.call-update) | async-done | bytes 2097168 | tf_op jit(solution)/shard_map/psum | solution.py:114
  (146 shorter events, 48.3 us)
Async XLA Ops:
  9.7 37.0 %all-to-all-start = ((s32[128,2,1]{1,2,0:T(1,128)}), s32[128,2,1]{1,2,0:T(1,128)S(1)}, u32[]{:S(2)}, u32[]{:S(2)}) async-start(s32[128,2,1]{1,2,0:T(1,128)} %bitcast), calls=%async_computation | async-start | bytes 131072 | tf_op jit(solution)/shard_map/all_to_all | solution.py:109
  46.8 20.3 %copy-start.3 = (s32[32,30]{1,0:T(8,128)S(1)}, s32[32,30]{1,0:T(8,128)}, u32[]{:S(2)}) copy-start(s32[32,30]{1,0:T(8,128)} %param.8) | copy-start | bytes 11524
  46.8 27.0 %copy-start.2 = (bf16[32,30,600]{2,0,1:T(8,128)(2,1)S(1)}, bf16[32,30,600]{2,0,1:T(8,128)(2,1)}, u32[]{:S(2)}) copy-start(bf16[32,30,600]{2,0,1:T(8,128)(2,1)} %param.7) | copy-start | bytes 3456004
  46.8 397.8 %all-to-all-start.1 = ((bf16[128,2,17408]{2,1,0:T(2,128)(2,1)}), bf16[128,2,17408]{2,1,0:T(2,128)(2,1)}, u32[]{:S(2)}, u32[]{:S(2)}) async-start(bf16[128,2,17408]{2,1,0:T(2,128)(2,1)} %all_to_all.19), calls=%async_computation.1 | async-start | bytes 17825792 | tf_op jit(solution)/shard_map/all_to_all | solution.py:108
  67.0 1572.6 %all-reduce.3.cloned.1.call-start = ((), (), s32[]{:S(2)}) async-start(), calls=%async_computation.2 | async-start | bytes 4194304 | tf_op jit(solution)/shard_map/psum | solution.py:114
  416.3 20.6 %copy-start.4 = (s32[32,30]{1,0:T(8,128)S(1)}, s32[32,30]{1,0:T(8,128)}, u32[]{:S(2)}) copy-start(s32[32,30]{1,0:T(8,128)} %param.9) | copy-start | bytes 11524
  473.2 1.4 copy-start
  474.9 6.5 slice-start
  476.2 5.2 slice-start.1
  483.7 1.4 copy-start.1
Sparse Core Ops, SparseCore 0:
  548.8 1090.6 all-reduce.2
where the time goes:
time: 1660 us; the launch traced here: 1650 us
  waiting for transfers between devices  1090 us (66%)
  local copies, waits for them, and re-layouts  495 us (30%)
  starting transfers between devices  34.1 us (2%)
    psum x1, waiting for transfers between devices, shards(): summed = lax.psum(local_stack, 'stn')  1090 us
    gather x2, local copies, waits for them, and re-layouts, correlate(): ref_wave[:, clipped]  361 us
    gather x88, local copies, waits for them, and re-layouts  59.6 us
  transfers between devices with their start and end apart: 3, of which 1 were waited for; matrix products, arithmetic and copies ran while one was open for 23% of the time, Pallas kernels for 0%

commit v1 on v0

v1 whole, which is shorter than its diff:
```python
import functools
import math

import jax
import jax.numpy as jnp
from jax import lax
from jax.experimental import pallas as pl
from jax.experimental.pallas import tpu as pltpu
from jax.sharding import PartitionSpec as P

EPSILON = 1e-06
LANES = 128
KW = 7
SPAN = KW * LANES
VMEM_LIMIT = 60 * 1024 * 1024


def roll_half(x):
    return pltpu.roll(x, LANES // 2, 1)


def left_lanes(rows):
    return lax.broadcasted_iota(jnp.int32, (rows, LANES), 1) < LANES // 2


def pack_kernel(half_ref, base_ref, info_ref, archive_ref, out_ref, tail_ref, *, rows, tiles, tail_tiles):
    which = half_ref[0]
    half = rows // 2
    left = left_lanes(half)
    owners = out_ref.shape[0]
    tail_lines = 2 * tail_tiles
    tail_ref[...] = jnp.zeros_like(tail_ref)
    tail_start = 2 * tiles * LANES
    info = info_ref[...]
    for tile in range(tail_tiles):
        at = pl.multiple_of(tail_start + (which * tail_tiles + tile) * LANES, LANES)
        block = archive_ref[:, pl.ds(at, LANES)].astype(jnp.float32)
        for row in range(rows):
            tail_ref[pl.ds(base_ref[row] * tail_tiles + tile, 1), :] = block[row : row + 1, :]

    def one(tile, carry):
        at = pl.multiple_of((which * tiles + tile) * LANES, LANES)
        block = archive_ref[:, pl.ds(at, LANES)].astype(jnp.float32)
        upper, lower = block[:half], block[half:]
        even = jnp.where(left, upper, roll_half(lower))
        odd = jnp.where(left, roll_half(upper), lower)
        for side, lines in ((0, even), (1, odd)):
            owner = 2 * tile + side
            tail = tail_ref[pl.ds(pl.multiple_of(owner * tail_lines, 8), tail_lines), :]
            out_ref[owner] = jnp.concatenate([lines, tail, info], axis=0).astype(jnp.bfloat16)
        return carry

    lax.fori_loop(0, owners // 2, one, 0, unroll=8)


def permute_kernel(
    owner_ref, got_ref, out_ref, tail_out_ref,
    plain_ref, placed_ref, tail_ref, tail_rows_ref, info_ref, route_ref, keep_ref,
    route_smem, keep_smem, route_sem, keep_sem, *, rows, tail_tiles,
):
    stations = got_ref.shape[0]
    half = rows // 2
    left = left_lanes(half)
    tail_lines = 2 * tail_tiles
    swapped = stations * half

    def note(station, carry):
        info_ref[pl.ds(station, 1), :] = got_ref[station][half + tail_lines : half + tail_lines + 8].astype(
            jnp.float32
        )[:1]
        return carry

    lax.fori_loop(0, stations, note, 0, unroll=8)
    info = info_ref[...].astype(jnp.int32)
    other = pltpu.roll(info_ref[...], rows, 1).astype(jnp.int32)
    lane = lax.broadcasted_iota(jnp.int32, info.shape, 1)
    station = lax.broadcasted_iota(jnp.int32, info.shape, 0)
    on_left = lane < rows
    target = jnp.where(on_left, info, other)
    packed = jnp.where(on_left, other, info)
    place, rank = packed % rows, packed // rows
    row = lane % rows
    crossed = (place // half) != (row // half)
    source = station * half + row % half + jnp.where(crossed, swapped, 0)
    route_ref[...] = jnp.where(on_left, target * rows + place, source)
    mine = target == owner_ref[0]
    side = jnp.where(on_left, 0, 1)
    first = jnp.max(jnp.where(mine & (rank == 0), place, -1), axis=1, keepdims=True)
    second = jnp.max(jnp.where(mine & (rank == 1), place, -1), axis=1, keepdims=True)
    kept = jnp.where(side == 0, first, second)
    keep_ref[...] = jnp.where(kept < 0, rows, kept)
    route_copy = pltpu.make_async_copy(route_ref, route_smem, route_sem)
    keep_copy = pltpu.make_async_copy(keep_ref, keep_smem, keep_sem)
    route_copy.start()
    keep_copy.start()

    def expand(station, carry):
        block = got_ref[station].astype(jnp.float32)
        lines = block[:half]
        at = pl.multiple_of(station * half, 8)
        plain_ref[pl.ds(at, half), :] = lines
        plain_ref[pl.ds(swapped + at, half), :] = roll_half(lines)
        tail_ref[pl.ds(pl.multiple_of(station * tail_lines, 8), tail_lines), :] = block[half : half + tail_lines]
        return carry

    lax.fori_loop(0, stations, expand, 0, unroll=8)
    route_copy.wait()
    keep_copy.wait()

    def move(station, carry):
        for row in range(rows):
            placed_ref[pl.ds(route_smem[station, row], 1), :] = plain_ref[
                pl.ds(route_smem[station, rows + row], 1), :
            ]
        return carry

    lax.fori_loop(0, stations, move, 0)

    def keep(station, carry):
        for rank in range(2):
            row = keep_smem[station, rank * rows]
            for tile in range(tail_tiles):
                line = station * tail_lines + rank * tail_tiles + tile
                tail_rows_ref[tile, pl.ds(row, 1), :] = tail_ref[pl.ds(line, 1), :]
        return carry

    lax.fori_loop(0, stations, keep, 0, unroll=8)
    for tile in range(tail_tiles):
        tail_out_ref[:, tile * LANES : (tile + 1) * LANES] = tail_rows_ref[tile, :rows, :].astype(jnp.bfloat16)

    def join(station, carry):
        at = pl.multiple_of(station * rows, 8)
        lines = jnp.where(left, placed_ref[pl.ds(at, half), :], placed_ref[pl.ds(at + half, half), :])
        lines = lines.astype(jnp.bfloat16)
        out_ref[2 * station] = lines
        out_ref[2 * station + 1] = lines
        return carry

    lax.fori_loop(0, stations, join, 0, unroll=8)


def assemble_kernel(got_ref, tail_low_ref, tail_high_ref, out_ref, *, tiles):
    half = got_ref.shape[1]
    left = left_lanes(half)
    for which in range(2):

        def one(tile, carry, which=which):
            even = got_ref[4 * tile + which].astype(jnp.float32)
            odd = got_ref[4 * tile + 2 + which].astype(jnp.float32)
            upper = jnp.where(left, even, roll_half(odd))
            lower = jnp.where(left, roll_half(even), odd)
            at = pl.multiple_of((which * tiles + tile) * LANES, LANES)
            out_ref[:, pl.ds(at, LANES)] = jnp.concatenate([upper, lower], axis=0).astype(jnp.bfloat16)
            return carry

        lax.fori_loop(0, tiles, one, 0, unroll=8)
    at = 2 * tiles * LANES
    width = tail_low_ref.shape[1]
    out_ref[:, at : at + width] = tail_low_ref[...]
    out_ref[:, at + width : at + 2 * width] = tail_high_ref[...]


def halving_bits(sizes):
    ys, zs, xs, cores = (size.bit_length() - 1 for size in sizes)
    x_from, z_from, y_from = cores, cores + xs, cores + xs + zs
    return (
        list(range(cores))
        + list(range(y_from, y_from + ys))
        + list(range(x_from, z_from))
        + list(reversed(range(z_from, y_from)))
    )


def place_of(index, bits):
    place = 0
    for at, bit in enumerate(bits):
        place = place + ((index >> bit) & 1) * (1 << (len(bits) - 1 - at))
    return place


def correlate_kernel(
    count_ref, entry_ref, row_ref, shift_ref, place_ref, archive_ref, wave_ref, out_ref,
    series_ref, line_ref, high_ref, low_ref, *, length, channels, bits,
):
    rows = archive_ref.shape[0]
    tiles = archive_ref.shape[1] // LANES
    blocks = LANES
    padded = series_ref.shape[0]

    def widen(tile, carry):
        at = pl.multiple_of(tile * LANES, LANES)
        series_ref[tile] = archive_ref[:, pl.ds(at, LANES)].astype(jnp.float32)
        return carry

    lax.fori_loop(0, tiles, widen, 0, unroll=8)
    for tile in range(tiles, padded):
        series_ref[tile] = jnp.zeros((rows, LANES), jnp.float32)
    out_ref[...] = jnp.zeros_like(out_ref)
    line_ref[...] = jnp.zeros_like(line_ref)
    my_place = place_ref[0]
    lag = lax.broadcasted_iota(jnp.int32, (LANES, SPAN), 1) - lax.broadcasted_iota(jnp.int32, (LANES, SPAN), 0)
    contract = (((1,), (1,)), ((), ()))

    def one(step, carry):
        entry = entry_ref[step]
        row = row_ref[entry]
        shift = shift_ref[entry]
        skip, fine = shift // LANES, shift % LANES
        for tile in range(blocks + KW - 1):
            line_ref[tile : tile + 1, :] = series_ref[skip + tile, pl.ds(row, 1), :]
        lines = line_ref[...]
        squares = lines * lines
        high = squares.astype(jnp.bfloat16).astype(jnp.float32)
        high_ref[...] = high
        low_ref[...] = squares - high
        def windows(ref):
            return jnp.concatenate(
                [ref[k : k + blocks, :].astype(jnp.bfloat16) for k in range(KW)], axis=1
            )

        wave = wave_ref[pl.ds(entry, 1), :]
        power = jnp.sum(wave * wave, axis=1, keepdims=True)
        base = pltpu.roll(jnp.broadcast_to(wave, (8, SPAN)), fine, 1)
        banded = pltpu.roll(
            jnp.concatenate([base] * (LANES // 8), axis=0), 0, 1, stride=1, stride_axis=0
        ).astype(jnp.bfloat16)
        inside = (lag >= fine) & (lag < fine + length)
        mask = jnp.where(inside, 1.0, 0.0).astype(jnp.bfloat16)
        product = lax.dot_general(windows(line_ref), banded, contract, preferred_element_type=jnp.float32)
        energy = lax.dot_general(
            windows(high_ref), mask, contract, preferred_element_type=jnp.float32
        ) + lax.dot_general(windows(low_ref), mask, contract, preferred_element_type=jnp.float32)
        scale = (energy / length + EPSILON) * (power / length + EPSILON)
        normalized = product / length / jnp.sqrt(scale)
        template = entry // channels
        for block in range(blocks):
            at = (place_of(block, bits) ^ my_place, pl.ds(template, 1), slice(None))
            out_ref[at] = out_ref[at] + normalized[block : block + 1, :]
        return carry

    lax.fori_loop(0, count_ref[0], one, 0)


VMEM_SPEC = pl.BlockSpec(memory_space=pltpu.VMEM)
SMEM_SPEC = pl.BlockSpec(memory_space=pltpu.SMEM)


def kernel_call(body, scalars, arrays, outs, scratch, flops, moved):
    return pl.pallas_call(
        body,
        out_shape=outs,
        in_specs=[SMEM_SPEC] * len(scalars) + [VMEM_SPEC] * len(arrays),
        out_specs=jax.tree.map(lambda _: VMEM_SPEC, outs),
        scratch_shapes=scratch,
        compiler_params=pltpu.CompilerParams(vmem_limit_bytes=VMEM_LIMIT),
        cost_estimate=pl.CostEstimate(flops=flops, bytes_accessed=moved, transcendentals=0),
    )(*scalars, *arrays)


def reduce_stack(partial, bits):
    count = partial.shape[0]
    for bit in bits:
        half = partial.shape[0] // 2
        pairs = [(i, i ^ (1 << bit)) for i in range(count)]
        partial = partial[:half] + lax.ppermute(partial[half:], "stn", pairs)
    return partial[0]


def owned_entries(slots, template_channels):
    flat = template_channels.reshape(-1)
    count = flat.shape[0]
    match = (flat[None, :] == slots[:, None]).astype(jnp.int32)
    row = jnp.sum(match * jnp.arange(slots.shape[0], dtype=jnp.int32)[:, None], axis=0)
    here = jnp.sum(match, axis=0)
    number = jnp.arange(count, dtype=jnp.int32)
    before = jnp.sum(jnp.where(number[None, :] < number[:, None], here[None, :], 0), axis=1)
    where_to = jnp.where(here > 0, before, count)
    entries = jnp.sum(jnp.where(where_to[None, :] == number[:, None], number[None, :], 0), axis=1)
    return entries, row, jnp.sum(here).reshape(1)


def rank_among(slots, rows):
    target = slots // rows
    number = jnp.arange(rows, dtype=jnp.int32)
    same = (target[..., :, None] == target[..., None, :]) & (number[None, :] < number[:, None])
    return target, jnp.sum(same.astype(jnp.int32), axis=-1)


def shards(archive, slot_of_row, templates, template_channels, moveouts, *, sizes):
    stations = lax.axis_size("stn")
    my_index = lax.axis_index("stn")
    which = lax.axis_index("tpl").astype(jnp.int32)
    rows, samples = archive.shape
    half = rows // 2
    local_templates, channels, length = templates.shape
    tiles = stations // 2
    tail_tiles = (samples // LANES - 2 * tiles) // 2
    block_lines = half + 2 * tail_tiles + 8
    f32, bf16, i32 = jnp.float32, jnp.bfloat16, jnp.int32
    shape = jax.ShapeDtypeStruct

    target, rank = rank_among(slot_of_row, rows)
    info = jnp.concatenate([target, slot_of_row % rows + rows * rank]).astype(f32)
    info = jnp.broadcast_to(info[None, :], (8, LANES))
    packed = kernel_call(
        functools.partial(pack_kernel, rows=rows, tiles=tiles, tail_tiles=tail_tiles),
        (which.reshape(1), target * 2 + rank),
        (info, archive),
        shape((stations, block_lines, LANES), bf16),
        [pltpu.VMEM((stations * 2 * tail_tiles, LANES), f32)],
        4_000_000, 4_000_000,
    )
    packed, later_archive = lax.optimization_barrier((packed, archive))
    first = lax.all_to_all(packed, "stn", 0, 0, tiled=True)

    entries, entry_row, entry_count = owned_entries(slot_of_row, template_channels)
    waves = jnp.pad(templates.reshape(-1, length).astype(f32), ((0, 0), (0, SPAN - length)))
    padded = samples // LANES + 8
    bits = halving_bits(sizes)
    my_place = place_of(my_index.astype(i32), bits).reshape(1)
    partial = kernel_call(
        functools.partial(correlate_kernel, length=length, channels=channels, bits=bits),
        (entry_count, entries, entry_row, moveouts.reshape(-1), my_place),
        (later_archive, waves),
        shape((stations, local_templates, LANES), f32),
        [
            pltpu.VMEM((padded, rows, LANES), f32),
            pltpu.VMEM((LANES + 8, LANES), f32),
            pltpu.VMEM((LANES + 8, LANES), f32),
            pltpu.VMEM((LANES + 8, LANES), f32),
        ],
        1000, 1000,
    )
    stack = reduce_stack(partial, bits) * math.sqrt(length / channels)

    lines, tail_rows = kernel_call(
        functools.partial(permute_kernel, rows=rows, tail_tiles=tail_tiles),
        (my_index.astype(i32).reshape(1),),
        (first,),
        (shape((2 * stations, half, LANES), bf16), shape((rows, tail_tiles * LANES), bf16)),
        [
            pltpu.VMEM((2 * stations * half, LANES), f32),
            pltpu.VMEM((stations * rows, LANES), f32),
            pltpu.VMEM((stations * 2 * tail_tiles, LANES), f32),
            pltpu.VMEM((tail_tiles, rows + 8, LANES), f32),
            pltpu.VMEM((stations, LANES), f32),
            pltpu.VMEM((stations, LANES), i32),
            pltpu.VMEM((stations, LANES), i32),
            pltpu.SMEM((stations, LANES), i32),
            pltpu.SMEM((stations, LANES), i32),
            pltpu.SemaphoreType.DMA,
            pltpu.SemaphoreType.DMA,
        ],
        4_000_000, 8_000_000,
    )
    second = lax.all_to_all(lines, ("stn", "tpl"), 0, 0, tiled=True)
    tail_other = lax.ppermute(tail_rows, "tpl", [(0, 1), (1, 0)])
    tail_low = jnp.where(which == 0, tail_rows, tail_other)
    tail_high = jnp.where(which == 0, tail_other, tail_rows)
    grouped = kernel_call(
        functools.partial(assemble_kernel, tiles=tiles),
        (),
        (second, tail_low, tail_high),
        shape((rows, samples), bf16),
        [],
        4_000_000, 6_000_000,
    )
    return grouped, stack


def solution(mesh):
    sizes = (2, 8, 4, 2)
    in_specs = (P("stn", None), P("stn"), P("tpl", None, None), P("tpl", None), P("tpl", None))
    out_specs = (P("stn", None), P("tpl", "stn"))
    return jax.shard_map(
        functools.partial(shards, sizes=sizes), mesh=mesh, in_specs=in_specs, out_specs=out_specs, check_vma=False
    )
```

time: 1660 us -> 181 us (0.11)
  waiting for transfers between devices: 1090 us -> 81.8 us
  local copies, waits for them, and re-layouts: 495 us -> 8.56 us
  Pallas kernels: 0 us -> 35.9 us
    psum x1 -> x0, waiting for transfers between devices: 1090 us -> none  [shards(): summed = lax.psum(local_stack, 'stn')]
    gather x95 -> x0, local copies, waits for them, and re-layouts: 424 us -> none  [the longest x2 361 us: correlate(): ref_wave[:, clipped]]
    ppermute x0 -> x8, waiting for transfers between devices: none -> 47.4 us  [the longest x7 44.6 us: reduce_stack(): partial = partial[:half] + lax.ppermute(partial[half:], 'stn', pairs)]
    scatter x5 -> x0, local copies, waits for them, and re-layouts: 36.1 us -> none  [the longest x1 15.1 us: unpack_rows(): return jnp.zeros((row_count, received.shape[1]), received.dtype).at[safe_...]
    pallas_call x0 -> x4, Pallas kernels: none -> 35.9 us  [kernel_call(): pl.pallas_call(body, out_shape=outs, in_specs=[SMEM_SPEC] * len(scalars)...]
    all_to_all x2, waiting for transfers between devices: 0.01 us -> 34.3 us  [the longest x1 34.3 us: shards(): first = lax.all_to_all(packed, 'stn', 0, 0, tiled=True)]
    all_to_all x5 -> x0, local copies, waits for them, and re-layouts: 28.3 us -> none  [the longest x2 26.9 us: shards(): lax.all_to_all(buffer, 'stn', split_axis=0, concat_axis=0, tiled=True)]
    ppermute x0 -> x8, starting transfers between devices: none -> 23.7 us  [the longest x7 23.7 us: reduce_stack(): partial = partial[:half] + lax.ppermute(partial[half:], 'stn', pairs)]
  transfers between devices with their start and end apart: 3 -> 10, of which waited for: 1 -> 9; matrix products, arithmetic and copies ran while one was open for 23% -> 6% of each run, Pallas kernels for 0% -> 4%
where the time goes in v1:
time: 181 us
  waiting for transfers between devices  81.8 us (45%)
  starting transfers between devices  45.7 us (25%)
  Pallas kernels  35.9 us (20%)
  local copies, waits for them, and re-layouts  8.56 us (5%)
  other arithmetic  7.88 us (4%)
    ppermute x7, waiting for transfers between devices, reduce_stack(): partial = partial[:half] + lax.ppermute(partial[half:], 'stn', pairs)  44.6 us
    pallas_call x4, Pallas kernels, kernel_call(): pl.pallas_call(body, out_shape=outs, in_specs=[SMEM_SPEC] * len(scalars)...  35.9 us
    all_to_all x1, waiting for transfers between devices, shards(): first = lax.all_to_all(packed, 'stn', 0, 0, tiled=True)  34.3 us
    ppermute x7, starting transfers between devices, reduce_stack(): partial = partial[:half] + lax.ppermute(partial[half:], 'stn', pairs)  23.7 us
    all_to_all x1, starting transfers between devices, shards(): first = lax.all_to_all(packed, 'stn', 0, 0, tiled=True)  14 us
    all_to_all x1, starting transfers between devices, shards(): second = lax.all_to_all(lines, ('stn', 'tpl'), 0, 0, tiled=True)  7.98 us
    unnamed x17, local copies, waits for them, and re-layouts  4.22 us
  transfers between devices with their start and end apart: 10, of which 9 were waited for; matrix products, arithmetic and copies ran while one was open for 6% of the time, Pallas kernels for 4%

profile of v1, /device:TPU:16, one launch (start us, length us, event | category | flops | bytes accessed | tf_op | source)
XLA Modules:
  0.0 180.7 jit_solution(11365793999797611454)
XLA Ops:
  0.6 0.7 and_select_fusion.1
  1.5 1.3 fusion.4
  3.4 3.9 %shard_map.68 = bf16[128,48,128]{2,1,0:T(8,128)(2,1)} custom-call(s32[1]{0:T(128)} %bitcast.1.half_ref, s32[64]{0:T(128)} %get-tuple-element.16.base_ref, f32[8,128]{1,0:T(8,128)} %broadcast_in_dim.21.info_ref, bf16[64,17408]{1,0:T(8,128)(2,1)} %archive_ref.2), custom_call_target="tpu_custom_call" | custom-call | flops 4000000 | bytes 4000000 | tf_op jit(solution)/shard_map/pallas_call | solution.py:249
  7.3 14.0 %all-to-all-start = ((bf16[128,48,128]{2,1,0:T(8,128)(2,1)}), bf16[128,48,128]{2,1,0:T(8,128)(2,1)S(1)}, u32[]{:S(2)}, u32[]{:S(2)}) async-start(bf16[128,48,128]{2,1,0:T(8,128)(2,1)} %shard_map.68), calls=%async_computation | async-start | bytes 3145728 | tf_op jit(solution)/shard_map/all_to_all | solution.py:314
  21.5 1.7 copy.9
  23.2 1.4 convert_element_type.22
  24.6 0.7 reshape.53.shift_ref
  25.3 0.8 fusion
  26.3 1.1 select_reduce_fusion.entry_ref
  27.4 34.3 %all-to-all-done.got_ref = bf16[128,48,128]{2,1,0:T(8,128)(2,1)S(1)} async-done(((bf16[128,48,128]{2,1,0:T(8,128)(2,1)}), bf16[128,48,128]{2,1,0:T(8,128)(2,1)S(1)}, u32[]{:S(2)}, u32[]{:S(2)}) %all-to-all-start) | async-done | bytes 1572896 | tf_op jit(solution)/shard_map/all_to_all | solution.py:314
  61.8 1.2 copy-done.2
  62.9 19.9 %shard_map.69 = (bf16[256,32,128]{2,1,0:T(8,128)(2,1)}, bf16[64,512]{1,0:T(8,128)(2,1)}) custom-call(s32[1]{0:T(128)} %bitcast.owner_ref, bf16[128,48,128]{2,1,0:T(8,128)(2,1)} %copy-done.2), custom_call_target="tpu_custom_call" | custom-call | flops 4000000 | bytes 8000000 | tf_op jit(solution)/shard_map/pallas_call | solution.py:249
  82.9 8.0 %all-to-all-start.1 = ((bf16[256,32,128]{2,1,0:T(8,128)(2,1)}), bf16[256,32,128]{2,1,0:T(8,128)(2,1)S(1)}, u32[]{:S(2)}, u32[]{:S(2)}) async-start(bf16[256,32,128]{2,1,0:T(8,128)(2,1)} %get-tuple-element.7), calls=%async_computation.1 | async-start | bytes 4194304 | tf_op jit(solution)/shard_map/all_to_all | solution.py:356
  90.9 1.9 %pad_convert_fusion.wave_ref = f32[960,896]{1,0:T(8,128)} fusion(bf16[960,600]{1,0:T(8,128)(2,1)S(1)} %copy-done.3), kind=kLoop, calls=%fused_computation.4 | loop fusion | flops 860160 | bytes 4592640 | tf_op jit(solution)/shard_map/jit(_pad)/pad | solution.py:317
  92.8 7.4 %shard_map.71 = f32[128,32,128]{2,1,0:T(8,128)} custom-call(s32[1]{0:T(128)} %bitcast.2.count_ref, s32[960]{0:T(1024)} %select_reduce_fusion.entry_ref, s32[960]{0:T(1024)} %get-tuple-element.10.row_ref, s32[960]{0:T(1024)} %reshape.53.shift_ref, s32[1]{0:T(128)} %bitcast.3.place_ref, bf16[64,17408]{1,0:T(8,128)(2,1)} %archive_ref.2, ...), custom_call_target="tpu_custom_call" | custom-call | flops 1000 | bytes 1000 | tf_op jit(solution)/shard_map/pallas_call | solution.py:249
  100.2 1.4 slice.57
  101.7 6.8 %collective-permute-start.1 = (f32[64,32,128]{2,1,0:T(8,128)S(1)}, f32[64,32,128]{2,1,0:T(8,128)S(1)}, u32[]{:S(2)}, u32[]{:S(2)}) collective-permute-start(f32[64,32,128]{2,1,0:T(8,128)S(1)} %slice.57), channel_id=1, source_target_pairs={{0,2},{2,0},{4,6},{6,4},{8,10},{10,8},{12,14},{14,12},{16,18},{18,... | collective-permute-start | bytes 3145736 | tf_op jit(solution)/shard_map/ppermute | solution.py:265
  108.4 2.3 %collective-permute-done.1 = f32[64,32,128]{2,1,0:T(8,128)S(1)} collective-permute-done((f32[64,32,128]{2,1,0:T(8,128)S(1)}, f32[64,32,128]{2,1,0:T(8,128)S(1)}, u32[]{:S(2)}, u32[]{:S(2)}) %collective-permute-start.1) | collective-permute-done | bytes 1048608 | tf_op jit(solution)/shard_map/ppermute | solution.py:265
  111.6 22.4 %collective-permute-done.2 = f32[32,32,128]{2,1,0:T(8,128)S(1)} collective-permute-done((f32[32,32,128]{2,1,0:T(8,128)S(1)}, f32[32,32,128]{2,1,0:T(8,128)S(1)}, u32[]{:S(2)}, u32[]{:S(2)}) %collective-permute-start.2) | collective-permute-done | bytes 524320 | tf_op jit(solution)/shard_map/ppermute | solution.py:265
  134.1 2.5 %collective-permute-start.3 = (f32[16,32,128]{2,1,0:T(8,128)S(1)}, f32[16,32,128]{2,1,0:T(8,128)S(1)}, u32[]{:S(2)}, u32[]{:S(2)}) collective-permute-start(f32[16,32,128]{2,1,0:T(8,128)S(1)} %slice.61), channel_id=1, source_target_pairs={{0,4},{2,6},{4,0},{6,2},{8,12},{10,14},{12,8},{14,10},{16,20},{18,... | collective-permute-start | bytes 786440 | tf_op jit(solution)/shard_map/ppermute | solution.py:265
  136.5 6.5 %collective-permute-done.3 = f32[16,32,128]{2,1,0:T(8,128)S(1)} collective-permute-done((f32[16,32,128]{2,1,0:T(8,128)S(1)}, f32[16,32,128]{2,1,0:T(8,128)S(1)}, u32[]{:S(2)}, u32[]{:S(2)}) %collective-permute-start.3) | collective-permute-done | bytes 262176 | tf_op jit(solution)/shard_map/ppermute | solution.py:265
  143.0 3.8 %collective-permute-start.4 = (f32[8,32,128]{2,1,0:T(8,128)S(1)}, f32[8,32,128]{2,1,0:T(8,128)S(1)}, u32[]{:S(2)}, u32[]{:S(2)}) collective-permute-start(f32[8,32,128]{2,1,0:T(8,128)S(1)} %slice.63), channel_id=1, source_target_pairs={{0,8},{2,10},{4,12},{6,14},{8,0},{10,2},{12,4},{14,6},{16,24},{18,... | collective-permute-start | bytes 393224 | tf_op jit(solution)/shard_map/ppermute | solution.py:265
  146.8 3.5 %collective-permute-done.4 = f32[8,32,128]{2,1,0:T(8,128)S(1)} collective-permute-done((f32[8,32,128]{2,1,0:T(8,128)S(1)}, f32[8,32,128]{2,1,0:T(8,128)S(1)}, u32[]{:S(2)}, u32[]{:S(2)}) %collective-permute-start.4) | collective-permute-done | bytes 131104 | tf_op jit(solution)/shard_map/ppermute | solution.py:265
  150.4 8.4 %collective-permute-start.5 = (f32[4,32,128]{2,1,0:T(8,128)S(1)}, f32[4,32,128]{2,1,0:T(8,128)S(1)}, u32[]{:S(2)}, u32[]{:S(2)}) collective-permute-start(f32[4,32,128]{2,1,0:T(8,128)S(1)} %slice.65), channel_id=1, source_target_pairs={{0,64},{2,66},{4,68},{6,70},{8,72},{10,74},{12,76},{14,78},{16,80}... | collective-permute-start | bytes 196616 | tf_op jit(solution)/shard_map/ppermute | solution.py:265
  158.8 2.9 %collective-permute-done.5 = f32[4,32,128]{2,1,0:T(8,128)S(1)} collective-permute-done((f32[4,32,128]{2,1,0:T(8,128)S(1)}, f32[4,32,128]{2,1,0:T(8,128)S(1)}, u32[]{:S(2)}, u32[]{:S(2)}) %collective-permute-start.5) | collective-permute-done | bytes 65568 | tf_op jit(solution)/shard_map/ppermute | solution.py:265
  162.0 4.7 %collective-permute-done.6 = f32[2,32,128]{2,1,0:T(8,128)S(1)} collective-permute-done((f32[2,32,128]{2,1,0:T(8,128)S(1)}, f32[2,32,128]{2,1,0:T(8,128)S(1)}, u32[]{:S(2)}, u32[]{:S(2)}) %collective-permute-start.6) | collective-permute-done | bytes 32800 | tf_op jit(solution)/shard_map/ppermute | solution.py:265
  166.7 1.5 collective-permute-start.7
  168.2 2.3 %collective-permute-done.7 = f32[1,32,128]{2,1,0:T(8,128)S(1)} collective-permute-done((f32[1,32,128]{2,1,0:T(8,128)S(1)}, f32[1,32,128]{2,1,0:T(8,128)S(1)}, u32[]{:S(2)}, u32[]{:S(2)}) %collective-permute-start.7) | collective-permute-done | bytes 16416 | tf_op jit(solution)/shard_map/ppermute | solution.py:265
  171.1 2.8 %collective-permute-done = bf16[64,512]{1,0:T(8,128)(2,1)S(1)} collective-permute-done((bf16[64,512]{1,0:T(8,128)(2,1)S(1)}, bf16[64,512]{1,0:T(8,128)(2,1)S(1)}, u32[]{:S(2)}, u32[]{:S(2)}) %collective-permute-start) | collective-permute-done | bytes 65568 | tf_op jit(solution)/shard_map/ppermute | solution.py:357
  174.0 0.7 broadcast_select_fusion
  174.6 1.4 copy-done.1
  176.0 4.7 %shard_map.70 = bf16[64,17408]{1,0:T(8,128)(2,1)} custom-call(bf16[256,32,128]{2,1,0:T(8,128)(2,1)} %copy-done.1, bf16[64,512]{1,0:T(8,128)(2,1)} %get-tuple-element.14.tail_low_ref, bf16[64,512]{1,0:T(8,128)(2,1)} %get-tuple-element.13.tail_high_ref), custom_call_target="tpu_custom_call" | custom-call | flops 4000000 | bytes 6000000 | tf_op jit(solution)/shard_map/pallas_call | solution.py:249
  (37 shorter events, 3.0 us)
Async XLA Ops:
  7.3 14.0 %copy-start.5 = (s32[32,30]{1,0:T(8,128)S(1)}, s32[32,30]{1,0:T(8,128)}, u32[]{:S(2)}) copy-start(s32[32,30]{1,0:T(8,128)} %param.8) | copy-start | bytes 11524
  7.3 54.5 %all-to-all-start = ((bf16[128,48,128]{2,1,0:T(8,128)(2,1)}), bf16[128,48,128]{2,1,0:T(8,128)(2,1)S(1)}, u32[]{:S(2)}, u32[]{:S(2)}) async-start(bf16[128,48,128]{2,1,0:T(8,128)(2,1)} %shard_map.68), calls=%async_computation | async-start | bytes 3145728 | tf_op jit(solution)/shard_map/all_to_all | solution.py:314
  21.4 3.1 %copy-start.6 = (s32[32,30]{1,0:T(8,128)S(1)}, s32[32,30]{1,0:T(8,128)}, u32[]{:S(2)}) copy-start(s32[32,30]{1,0:T(8,128)} %param.9) | copy-start | bytes 11524
  21.5 3.8 %copy-start.7 = (s32[64]{0:T(128)S(1)}, s32[64]{0:T(128)}, u32[]{:S(2)}) copy-start(s32[64]{0:T(128)} %param.6) | copy-start | bytes 772
  61.8 1.2 copy-start.2
  82.8 8.0 %copy-start.3 = (bf16[960,600]{1,0:T(8,128)(2,1)S(1)}, bf16[960,600]{1,0:T(8,128)(2,1)}, u32[]{:S(2)}) copy-start(bf16[960,600]{1,0:T(8,128)(2,1)} %convert_element_type.22) | copy-start | bytes 3456004
  82.9 91.8 %all-to-all-start.1 = ((bf16[256,32,128]{2,1,0:T(8,128)(2,1)}), bf16[256,32,128]{2,1,0:T(8,128)(2,1)S(1)}, u32[]{:S(2)}, u32[]{:S(2)}) async-start(bf16[256,32,128]{2,1,0:T(8,128)(2,1)} %get-tuple-element.7), calls=%async_computation.1 | async-start | bytes 4194304 | tf_op jit(solution)/shard_map/all_to_all | solution.py:356
  100.2 10.5 %copy-start = (f32[128,32,128]{2,1,0:T(8,128)S(1)}, f32[128,32,128]{2,1,0:T(8,128)}, u32[]{:S(2)}) copy-start(f32[128,32,128]{2,1,0:T(8,128)} %shard_map.71) | copy-start | bytes 6291460
  101.7 9.1 %collective-permute-start.1 = (f32[64,32,128]{2,1,0:T(8,128)S(1)}, f32[64,32,128]{2,1,0:T(8,128)S(1)}, u32[]{:S(2)}, u32[]{:S(2)}) collective-permute-start(f32[64,32,128]{2,1,0:T(8,128)S(1)} %slice.57), channel_id=1, source_target_pairs={{0,2},{2,0},{4,6},{6,4},{8,10},{10,8},{12,14},{14,12},{16,18},{18,... | collective-permute-start | bytes 3145736 | tf_op jit(solution)/shard_map/ppermute | solution.py:265
  111.0 57.2 %copy-start.4 = (bf16[64,512]{1,0:T(8,128)(2,1)S(1)}, bf16[64,512]{1,0:T(8,128)(2,1)}, u32[]{:S(2)}) copy-start(bf16[64,512]{1,0:T(8,128)(2,1)} %get-tuple-element.8) | copy-start | bytes 196612
  111.0 23.0 %collective-permute-start.2 = (f32[32,32,128]{2,1,0:T(8,128)S(1)}, f32[32,32,128]{2,1,0:T(8,128)S(1)}, u32[]{:S(2)}, u32[]{:S(2)}) collective-permute-start(f32[32,32,128]{2,1,0:T(8,128)S(1)} %slice.59), channel_id=1, source_target_pairs={{0,128},{2,130},{4,132},{6,134},{8,136},{10,138},{12,140},{14,142}... | collective-permute-start | bytes 1572872 | tf_op jit(solution)/shard_map/ppermute | solution.py:265
  134.1 8.9 %collective-permute-start.3 = (f32[16,32,128]{2,1,0:T(8,128)S(1)}, f32[16,32,128]{2,1,0:T(8,128)S(1)}, u32[]{:S(2)}, u32[]{:S(2)}) collective-permute-start(f32[16,32,128]{2,1,0:T(8,128)S(1)} %slice.61), channel_id=1, source_target_pairs={{0,4},{2,6},{4,0},{6,2},{8,12},{10,14},{12,8},{14,10},{16,20},{18,... | collective-permute-start | bytes 786440 | tf_op jit(solution)/shard_map/ppermute | solution.py:265
  143.0 7.3 %collective-permute-start.4 = (f32[8,32,128]{2,1,0:T(8,128)S(1)}, f32[8,32,128]{2,1,0:T(8,128)S(1)}, u32[]{:S(2)}, u32[]{:S(2)}) collective-permute-start(f32[8,32,128]{2,1,0:T(8,128)S(1)} %slice.63), channel_id=1, source_target_pairs={{0,8},{2,10},{4,12},{6,14},{8,0},{10,2},{12,4},{14,6},{16,24},{18,... | collective-permute-start | bytes 393224 | tf_op jit(solution)/shard_map/ppermute | solution.py:265
  150.4 11.4 %collective-permute-start.5 = (f32[4,32,128]{2,1,0:T(8,128)S(1)}, f32[4,32,128]{2,1,0:T(8,128)S(1)}, u32[]{:S(2)}, u32[]{:S(2)}) collective-permute-start(f32[4,32,128]{2,1,0:T(8,128)S(1)} %slice.65), channel_id=1, source_target_pairs={{0,64},{2,66},{4,68},{6,70},{8,72},{10,74},{12,76},{14,78},{16,80}... | collective-permute-start | bytes 196616 | tf_op jit(solution)/shard_map/ppermute | solution.py:265
  161.8 4.9 %collective-permute-start.6 = (f32[2,32,128]{2,1,0:T(8,128)S(1)}, f32[2,32,128]{2,1,0:T(8,128)S(1)}, u32[]{:S(2)}, u32[]{:S(2)}) collective-permute-start(f32[2,32,128]{2,1,0:T(8,128)S(1)} %slice.67), channel_id=1, source_target_pairs={{0,32},{2,34},{4,36},{6,38},{8,40},{10,42},{12,44},{14,46},{16,48}... | collective-permute-start | bytes 98312 | tf_op jit(solution)/shard_map/ppermute | solution.py:265
  166.7 3.8 %collective-permute-start.7 = (f32[1,32,128]{2,1,0:T(8,128)S(1)}, f32[1,32,128]{2,1,0:T(8,128)S(1)}, u32[]{:S(2)}, u32[]{:S(2)}) collective-permute-start(f32[1,32,128]{2,1,0:T(8,128)S(1)} %slice.69), channel_id=1, source_target_pairs={{0,16},{2,18},{4,20},{6,22},{8,24},{10,26},{12,28},{14,30},{16,0},... | collective-permute-start | bytes 49160 | tf_op jit(solution)/shard_map/ppermute | solution.py:265
  168.2 5.8 %collective-permute-start = (bf16[64,512]{1,0:T(8,128)(2,1)S(1)}, bf16[64,512]{1,0:T(8,128)(2,1)S(1)}, u32[]{:S(2)}, u32[]{:S(2)}) collective-permute-start(bf16[64,512]{1,0:T(8,128)(2,1)S(1)} %copy-done.4), channel_id=1, source_target_pairs={{0,1},{1,0},{2,3},{3,2},{4,5},{5,4},{6,7},{7,6},{8,9},{9,8},{10,11... | collective-permute-start | bytes 196616 | tf_op jit(solution)/shard_map/ppermute | solution.py:357
  174.6 1.4 copy-start.1

commit v2 on v1

--- a/solution.py
+++ b/solution.py
@@ -12,7 +12,8 @@
 LANES = 128
 KW = 7
 SPAN = KW * LANES
-VMEM_LIMIT = 60 * 1024 * 1024
+MIB = 1024 * 1024
+PARTS = 4
 
 
 def roll_half(x):
@@ -23,7 +24,16 @@
     return lax.broadcasted_iota(jnp.int32, (rows, LANES), 1) < LANES // 2
 
 
-def pack_kernel(half_ref, base_ref, info_ref, archive_ref, out_ref, tail_ref, *, rows, tiles, tail_tiles):
+def send_part(source, target, part, size, sem):
+    at = pl.ds(part * size, size)
+    copy = pltpu.make_async_copy(source.at[at], target.at[at], sem)
+    copy.start()
+    return copy
+
+
+def pack_kernel(
+    half_ref, base_ref, info_ref, archive_ref, out_hbm, out_ref, tail_ref, sems, *, rows, tiles, tail_tiles
+):
     which = half_ref[0]
     half = rows // 2
     left = left_lanes(half)
@@ -50,19 +60,23 @@
             out_ref[owner] = jnp.concatenate([lines, tail, info], axis=0).astype(jnp.bfloat16)
         return carry
 
-    lax.fori_loop(0, owners // 2, one, 0, unroll=8)
+    copies = []
+    for part in range(PARTS):
+        lax.fori_loop(part * tiles // PARTS, (part + 1) * tiles // PARTS, one, 0, unroll=8)
+        copies.append(send_part(out_ref, out_hbm, part, owners // PARTS, sems.at[part]))
+    for copy in copies:
+        copy.wait()
 
 
 def permute_kernel(
-    owner_ref, got_ref, out_ref, tail_out_ref,
-    plain_ref, placed_ref, tail_ref, tail_rows_ref, info_ref, route_ref, keep_ref,
-    route_smem, keep_smem, route_sem, keep_sem, *, rows, tail_tiles,
+    owner_ref, got_ref, out_hbm, tail_out_ref,
+    out_ref, plain_ref, placed_ref, tail_ref, tail_rows_ref, info_ref, route_ref, route_smem, route_sem, sems,
+    *, rows, tail_tiles,
 ):
     stations = got_ref.shape[0]
     half = rows // 2
     left = left_lanes(half)
     tail_lines = 2 * tail_tiles
-    swapped = stations * half
 
     def note(station, carry):
         info_ref[pl.ds(station, 1), :] = got_ref[station][half + tail_lines : half + tail_lines + 8].astype(
@@ -73,52 +87,56 @@
     lax.fori_loop(0, stations, note, 0, unroll=8)
     info = info_ref[...].astype(jnp.int32)
     other = pltpu.roll(info_ref[...], rows, 1).astype(jnp.int32)
-    lane = lax.broadcasted_iota(jnp.int32, info.shape, 1)
-    station = lax.broadcasted_iota(jnp.int32, info.shape, 0)
-    on_left = lane < rows
+    on_left = lax.broadcasted_iota(jnp.int32, info.shape, 1) < rows
     target = jnp.where(on_left, info, other)
     packed = jnp.where(on_left, other, info)
     place, rank = packed % rows, packed // rows
-    row = lane % rows
-    crossed = (place // half) != (row // half)
-    source = station * half + row % half + jnp.where(crossed, swapped, 0)
-    route_ref[...] = jnp.where(on_left, target * rows + place, source)
     mine = target == owner_ref[0]
-    side = jnp.where(on_left, 0, 1)
     first = jnp.max(jnp.where(mine & (rank == 0), place, -1), axis=1, keepdims=True)
     second = jnp.max(jnp.where(mine & (rank == 1), place, -1), axis=1, keepdims=True)
-    kept = jnp.where(side == 0, first, second)
-    keep_ref[...] = jnp.where(kept < 0, rows, kept)
+    lane = lax.broadcasted_iota(jnp.int32, info.shape, 1)
+    kept = jnp.where(lane == rows, first, second)
+    kept = jnp.where(kept < 0, rows, kept)
+    route_ref[...] = jnp.where(on_left, target * rows + place, kept)
     route_copy = pltpu.make_async_copy(route_ref, route_smem, route_sem)
-    keep_copy = pltpu.make_async_copy(keep_ref, keep_smem, keep_sem)
     route_copy.start()
-    keep_copy.start()
 
     def expand(station, carry):
         block = got_ref[station].astype(jnp.float32)
         lines = block[:half]
-        at = pl.multiple_of(station * half, 8)
+        at = pl.multiple_of(station * rows, 8)
         plain_ref[pl.ds(at, half), :] = lines
-        plain_ref[pl.ds(swapped + at, half), :] = roll_half(lines)
+        plain_ref[pl.ds(at + half, half), :] = roll_half(lines)
         tail_ref[pl.ds(pl.multiple_of(station * tail_lines, 8), tail_lines), :] = block[half : half + tail_lines]
         return carry
 
     lax.fori_loop(0, stations, expand, 0, unroll=8)
     route_copy.wait()
-    keep_copy.wait()
 
     def move(station, carry):
+        lines = plain_ref[pl.ds(pl.multiple_of(station * rows, 8), rows), :]
         for row in range(rows):
-            placed_ref[pl.ds(route_smem[station, row], 1), :] = plain_ref[
-                pl.ds(route_smem[station, rows + row], 1), :
-            ]
+            placed_ref[pl.ds(route_smem[station, row], 1), :] = lines[row : row + 1, :]
         return carry
 
     lax.fori_loop(0, stations, move, 0)
 
+    def join(station, carry):
+        at = pl.multiple_of(station * rows, 8)
+        lines = jnp.where(left, placed_ref[pl.ds(at, half), :], roll_half(placed_ref[pl.ds(at + half, half), :]))
+        out_ref[station] = lines.astype(jnp.bfloat16)
+        return carry
+
+    copies = []
+    for part in range(PARTS):
+        lax.fori_loop(part * stations // PARTS, (part + 1) * stations // PARTS, join, 0, unroll=8)
+        for which in range(2):
+            copies.append(
+                send_part(out_ref, out_hbm.at[:, which], part, stations // PARTS, sems.at[which, part])
+            )
     def keep(station, carry):
         for rank in range(2):
-            row = keep_smem[station, rank * rows]
+            row = route_smem[station, rows + rank]
             for tile in range(tail_tiles):
                 line = station * tail_lines + rank * tail_tiles + tile
                 tail_rows_ref[tile, pl.ds(row, 1), :] = tail_ref[pl.ds(line, 1), :]
@@ -127,21 +145,25 @@
     lax.fori_loop(0, stations, keep, 0, unroll=8)
     for tile in range(tail_tiles):
         tail_out_ref[:, tile * LANES : (tile + 1) * LANES] = tail_rows_ref[tile, :rows, :].astype(jnp.bfloat16)
-
-    def join(station, carry):
-        at = pl.multiple_of(station * rows, 8)
-        lines = jnp.where(left, placed_ref[pl.ds(at, half), :], placed_ref[pl.ds(at + half, half), :])
-        lines = lines.astype(jnp.bfloat16)
-        out_ref[2 * station] = lines
-        out_ref[2 * station + 1] = lines
-        return carry
-
-    lax.fori_loop(0, stations, join, 0, unroll=8)
-
-
-def assemble_kernel(got_ref, tail_low_ref, tail_high_ref, out_ref, *, tiles):
+    for copy in copies:
+        copy.wait()
+
+
+def assemble_kernel(got_ref, tail_low_ref, tail_high_ref, out_hbm, out_ref, sems, *, tiles):
     half = got_ref.shape[1]
     left = left_lanes(half)
+    copies = []
+
+    def send(start, size):
+        at = (slice(None), pl.ds(start, size))
+        copies.append(pltpu.make_async_copy(out_ref.at[at], out_hbm.at[at], sems.at[len(copies)]))
+        copies[-1].start()
+
+    at = 2 * tiles * LANES
+    width = tail_low_ref.shape[1]
+    out_ref[:, at : at + width] = tail_low_ref[...]
+    out_ref[:, at + width : at + 2 * width] = tail_high_ref[...]
+    send(at, 2 * width)
     for which in range(2):
 
         def one(tile, carry, which=which):
@@ -153,11 +175,12 @@
             out_ref[:, pl.ds(at, LANES)] = jnp.concatenate([upper, lower], axis=0).astype(jnp.bfloat16)
             return carry
 
-        lax.fori_loop(0, tiles, one, 0, unroll=8)
-    at = 2 * tiles * LANES
-    width = tail_low_ref.shape[1]
-    out_ref[:, at : at + width] = tail_low_ref[...]
-    out_ref[:, at + width : at + 2 * width] = tail_high_ref[...]
+        part = tiles // 2
+        for start in range(0, tiles, part):
+            lax.fori_loop(start, start + part, one, 0, unroll=8)
+            send((which * tiles + start) * LANES, part * LANES)
+    for copy in copies:
+        copy.wait()
 
 
 def halving_bits(sizes):
@@ -243,27 +266,25 @@
 
 VMEM_SPEC = pl.BlockSpec(memory_space=pltpu.VMEM)
 SMEM_SPEC = pl.BlockSpec(memory_space=pltpu.SMEM)
-
-
-def kernel_call(body, scalars, arrays, outs, scratch, flops, moved):
+HBM_SPEC = pl.BlockSpec(memory_space=pltpu.HBM)
+
+
+def kernel_call(body, scalars, arrays, outs, scratch, flops, moved, vmem, out_specs=VMEM_SPEC):
     return pl.pallas_call(
         body,
         out_shape=outs,
         in_specs=[SMEM_SPEC] * len(scalars) + [VMEM_SPEC] * len(arrays),
-        out_specs=jax.tree.map(lambda _: VMEM_SPEC, outs),
+        out_specs=out_specs,
         scratch_shapes=scratch,
-        compiler_params=pltpu.CompilerParams(vmem_limit_bytes=VMEM_LIMIT),
+        compiler_params=pltpu.CompilerParams(vmem_limit_bytes=vmem * MIB),
         cost_estimate=pl.CostEstimate(flops=flops, bytes_accessed=moved, transcendentals=0),
     )(*scalars, *arrays)
 
 
-def reduce_stack(partial, bits):
-    count = partial.shape[0]
-    for bit in bits:
-        half = partial.shape[0] // 2
-        pairs = [(i, i ^ (1 << bit)) for i in range(count)]
-        partial = partial[:half] + lax.ppermute(partial[half:], "stn", pairs)
-    return partial[0]
+def halve(partial, bit, count):
+    half = partial.shape[0] // 2
+    pairs = [(i, i ^ (1 << bit)) for i in range(count)]
+    return partial[:half] + lax.ppermute(partial[half:], "stn", pairs)
 
 
 def owned_entries(slots, template_channels):
@@ -307,8 +328,12 @@
         (which.reshape(1), target * 2 + rank),
         (info, archive),
         shape((stations, block_lines, LANES), bf16),
-        [pltpu.VMEM((stations * 2 * tail_tiles, LANES), f32)],
-        4_000_000, 4_000_000,
+        [
+            pltpu.VMEM((stations, block_lines, LANES), bf16),
+            pltpu.VMEM((stations * 2 * tail_tiles, LANES), f32),
+            pltpu.SemaphoreType.DMA((PARTS,)),
+        ],
+        4_000_000, 4_000_000, 12, HBM_SPEC,
     )
     packed, later_archive = lax.optimization_barrier((packed, archive))
     first = lax.all_to_all(packed, "stn", 0, 0, tiled=True)
@@ -329,30 +354,34 @@
             pltpu.VMEM((LANES + 8, LANES), f32),
             pltpu.VMEM((LANES + 8, LANES), f32),
         ],
-        1000, 1000,
-    )
-    stack = reduce_stack(partial, bits) * math.sqrt(length / channels)
+        1000, 1000, 28,
+    )
+    partial = halve(partial, bits[0], stations)
+    first, _ = lax.optimization_barrier((first, partial))
+    for bit in bits[1:]:
+        partial = halve(partial, bit, stations)
+    stack = partial[0] * math.sqrt(length / channels)
 
     lines, tail_rows = kernel_call(
         functools.partial(permute_kernel, rows=rows, tail_tiles=tail_tiles),
         (my_index.astype(i32).reshape(1),),
         (first,),
-        (shape((2 * stations, half, LANES), bf16), shape((rows, tail_tiles * LANES), bf16)),
+        (shape((stations, 2, half, LANES), bf16), shape((rows, tail_tiles * LANES), bf16)),
         [
-            pltpu.VMEM((2 * stations * half, LANES), f32),
+            pltpu.VMEM((stations, half, LANES), bf16),
+            pltpu.VMEM((stations * rows, LANES), f32),
             pltpu.VMEM((stations * rows, LANES), f32),
             pltpu.VMEM((stations * 2 * tail_tiles, LANES), f32),
             pltpu.VMEM((tail_tiles, rows + 8, LANES), f32),
             pltpu.VMEM((stations, LANES), f32),
             pltpu.VMEM((stations, LANES), i32),
-            pltpu.VMEM((stations, LANES), i32),
-            pltpu.SMEM((stations, LANES), i32),
             pltpu.SMEM((stations, LANES), i32),
             pltpu.SemaphoreType.DMA,
-            pltpu.SemaphoreType.DMA,
+            pltpu.SemaphoreType.DMA((2, PARTS)),
         ],
-        4_000_000, 8_000_000,
-    )
+        4_000_000, 30_000_000, 52, (HBM_SPEC, VMEM_SPEC),
+    )
+    lines = lines.reshape(2 * stations, half, LANES)
     second = lax.all_to_all(lines, ("stn", "tpl"), 0, 0, tiled=True)
     tail_other = lax.ppermute(tail_rows, "tpl", [(0, 1), (1, 0)])
     tail_low = jnp.where(which == 0, tail_rows, tail_other)
@@ -362,8 +391,8 @@
         (),
         (second, tail_low, tail_high),
         shape((rows, samples), bf16),
-        [],
-        4_000_000, 6_000_000,
+        [pltpu.VMEM((rows, samples), bf16), pltpu.SemaphoreType.DMA((5,))],
+        4_000_000, 6_000_000, 12, HBM_SPEC,
     )
     return grouped, stack
 

time: 181 us -> 153 us (0.85)
  waiting for transfers between devices: 81.8 us -> 72.9 us
  starting transfers between devices: 45.7 us -> 38.3 us
  Pallas kernels: 35.9 us -> 29.5 us
  local copies, waits for them, and re-layouts: 8.56 us -> 5.12 us
  other arithmetic: 7.88 us -> 5.73 us
    all_to_all x1, waiting for transfers between devices: 34.3 us -> 17.7 us  [shards(): first = lax.all_to_all(packed, 'stn', 0, 0, tiled=True)]
    ppermute x7, waiting for transfers between devices: 44.6 us -> 52.2 us  [halve(): return partial[:half] + lax.ppermute(partial[half:], 'stn', pairs)]
    ppermute x7, starting transfers between devices: 23.7 us -> 16.2 us  [halve(): return partial[:half] + lax.ppermute(partial[half:], 'stn', pairs)]
    pallas_call x4, Pallas kernels: 35.9 us -> 29.5 us  [kernel_call(): pl.pallas_call(body, out_shape=outs, in_specs=[SMEM_SPEC] * len(scalars)...]
    unnamed x17 -> x11, local copies, waits for them, and re-layouts: 4.22 us -> 3.34 us
  transfers between devices with their start and end apart: 10 -> 10, of which waited for: 9 -> 9; matrix products, arithmetic and copies ran while one was open for 6% -> 5% of each run, Pallas kernels for 4% -> 9%
where the time goes in v2:
time: 153 us; the launch traced here: 152 us
  waiting for transfers between devices  72.9 us (48%)
  starting transfers between devices  38.3 us (25%)
  Pallas kernels  29.5 us (19%)
  other arithmetic  5.73 us (4%)
  local copies, waits for them, and re-layouts  5.12 us (3%)
    ppermute x7, waiting for transfers between devices, halve(): return partial[:half] + lax.ppermute(partial[half:], 'stn', pairs)  52.2 us
    pallas_call x4, Pallas kernels, kernel_call(): pl.pallas_call(body, out_shape=outs, in_specs=[SMEM_SPEC] * len(scalars)...  29.5 us
    all_to_all x1, waiting for transfers between devices, shards(): first = lax.all_to_all(packed, 'stn', 0, 0, tiled=True)  17.7 us
    ppermute x7, starting transfers between devices, halve(): return partial[:half] + lax.ppermute(partial[half:], 'stn', pairs)  16.2 us
    all_to_all x1, starting transfers between devices, shards(): first = lax.all_to_all(packed, 'stn', 0, 0, tiled=True)  13.9 us
    all_to_all x1, starting transfers between devices, shards(): second = lax.all_to_all(lines, ('stn', 'tpl'), 0, 0, tiled=True)  7.98 us
    unnamed x11, local copies, waits for them, and re-layouts  3.34 us
  transfers between devices with their start and end apart: 10, of which 9 were waited for; matrix products, arithmetic and copies ran while one was open for 5% of the time, Pallas kernels for 9%

profile of v2, /device:TPU:16, one launch (start us, length us, event | category | flops | bytes accessed | tf_op | source)
XLA Modules:
  0.0 152.5 jit_solution(3283871181620591790)
XLA Ops:
  0.6 0.7 and_select_fusion.1
  1.5 0.7 fusion.4
  2.2 1.6 %copy-done = bf16[64,17408]{1,0:T(8,128)(2,1)S(1)} copy-done((bf16[64,17408]{1,0:T(8,128)(2,1)S(1)}, bf16[64,17408]{1,0:T(8,128)(2,1)}, u32[]{:S(2)}) %copy-start) | copy-done | bytes 2228248
  3.9 2.4 %shard_map.68 = bf16[128,48,128]{2,1,0:T(8,128)(2,1)} custom-call(s32[1]{0:T(128)} %bitcast.1.half_ref, s32[64]{0:T(128)S(1)} %get-tuple-element.18.base_ref, f32[8,128]{1,0:T(8,128)S(1)} %broadcast_in_dim.21.info_ref, bf16[64,17408]{1,0:T(8,128)(2,1)S(1)} %copy-done), custom_call_target="tpu_custom_call" | custom-call | flops 4000000 | bytes 4000000 | tf_op jit(solution)/shard_map/pallas_call | solution.py:273
  6.3 13.9 %all-to-all-start = ((bf16[128,48,128]{2,1,0:T(8,128)(2,1)}), bf16[128,48,128]{2,1,0:T(8,128)(2,1)S(1)}, u32[]{:S(2)}, u32[]{:S(2)}) async-start(bf16[128,48,128]{2,1,0:T(8,128)(2,1)} %shard_map.68), calls=%async_computation | async-start | bytes 3145728 | tf_op jit(solution)/shard_map/all_to_all | solution.py:339
  20.5 1.7 %copy.9 = bf16[32,30,600]{2,1,0:T(8,128)(2,1)S(1)} copy(bf16[32,30,600]{2,0,1:T(8,128)(2,1)} %param.7) | data formatting | bytes 2304000 | tf_op args[2]
  22.1 1.4 convert_element_type.22
  23.6 0.8 fusion
  24.4 1.7 %pad_convert_fusion.wave_ref = f32[960,896]{1,0:T(8,128)S(1)} fusion(bf16[960,600]{1,0:T(8,128)(2,1)} %convert_element_type.22), kind=kLoop, calls=%fused_computation.4 | loop fusion | flops 860160 | bytes 4592640 | tf_op jit(solution)/shard_map/jit(_pad)/pad | solution.py:342
  26.3 0.5 select_reduce_fusion.entry_ref
  26.8 13.1 %shard_map.69 = f32[128,32,128]{2,1,0:T(8,128)S(1)} custom-call(s32[1]{0:T(128)} %bitcast.2.count_ref, s32[960]{0:T(1024)S(1)} %select_reduce_fusion.entry_ref, s32[960]{0:T(1024)S(1)} %get-tuple-element.12.row_ref, s32[960]{0:T(1024)S(1)} %reshape.56.shift_ref, s32[1]{0:T(128)} %bitcast.3.place_ref, bf16[64,17408]{1,0:T(8,128)(2,1)S(1)} %copy-done.1, ...), custom_call_target="tpu_custom_call" | custom-call | flops 1000 | bytes 1000 | tf_op jit(solution)/shard_map/pallas_call | solution.py:273
  40.1 2.6 %collective-permute-done = f32[64,32,128]{2,1,0:T(8,128)S(1)} collective-permute-done((f32[64,32,128]{2,1,0:T(8,128)S(1)}, f32[64,32,128]{2,1,0:T(8,128)S(1)}, u32[]{:S(2)}, u32[]{:S(2)}) %collective-permute-start) | collective-permute-done | bytes 1048608 | tf_op jit(solution)/shard_map/ppermute | solution.py:287
  42.7 0.2 slice_add_fusion
  42.9 17.7 %all-to-all-done.got_ref = bf16[128,48,128]{2,1,0:T(8,128)(2,1)S(1)} async-done(((bf16[128,48,128]{2,1,0:T(8,128)(2,1)}), bf16[128,48,128]{2,1,0:T(8,128)(2,1)S(1)}, u32[]{:S(2)}, u32[]{:S(2)}) %all-to-all-start) | async-done | bytes 1572896 | tf_op jit(solution)/shard_map/all_to_all | solution.py:339
  60.6 11.5 %shard_map.70 = (bf16[128,2,32,128]{3,2,1,0:T(8,128)(2,1)}, bf16[64,512]{1,0:T(8,128)(2,1)S(1)}) custom-call(s32[1]{0:T(128)} %bitcast.owner_ref, bf16[128,48,128]{2,1,0:T(8,128)(2,1)S(1)} %all-to-all-done.got_ref), custom_call_target="tpu_custom_call" | custom-call | flops 4000000 | bytes 30000000 | tf_op jit(solution)/shard_map/pallas_call | solution.py:273
  72.1 8.0 %all-to-all-start.1 = ((bf16[256,32,128]{2,1,0:T(8,128)(2,1)}), bf16[256,32,128]{2,1,0:T(8,128)(2,1)S(1)}, u32[]{:S(2)}, u32[]{:S(2)}) async-start(bf16[256,32,128]{2,1,0:T(8,128)(2,1)} %bitcast.7), calls=%async_computation.1 | async-start | bytes 4194304 | tf_op jit(solution)/shard_map/all_to_all | solution.py:385
  80.1 1.3 collective-permute-start.2
  81.4 23.1 %collective-permute-done.2 = f32[32,32,128]{2,1,0:T(8,128)S(1)} collective-permute-done((f32[32,32,128]{2,1,0:T(8,128)S(1)}, f32[32,32,128]{2,1,0:T(8,128)S(1)}, u32[]{:S(2)}, u32[]{:S(2)}) %collective-permute-start.2) | collective-permute-done | bytes 524320 | tf_op jit(solution)/shard_map/ppermute | solution.py:287
  104.7 2.2 %collective-permute-start.3 = (f32[16,32,128]{2,1,0:T(8,128)S(1)}, f32[16,32,128]{2,1,0:T(8,128)S(1)}, u32[]{:S(2)}, u32[]{:S(2)}) collective-permute-start(f32[16,32,128]{2,1,0:T(8,128)S(1)} %slice.61), channel_id=1, source_target_pairs={{0,4},{2,6},{4,0},{6,2},{8,12},{10,14},{12,8},{14,10},{16,20},{18,... | collective-permute-start | bytes 786440 | tf_op jit(solution)/shard_map/ppermute | solution.py:287
  106.9 11.1 %collective-permute-done.3 = f32[16,32,128]{2,1,0:T(8,128)S(1)} collective-permute-done((f32[16,32,128]{2,1,0:T(8,128)S(1)}, f32[16,32,128]{2,1,0:T(8,128)S(1)}, u32[]{:S(2)}, u32[]{:S(2)}) %collective-permute-start.3) | collective-permute-done | bytes 262176 | tf_op jit(solution)/shard_map/ppermute | solution.py:287
  118.0 2.0 %collective-permute-start.4 = (f32[8,32,128]{2,1,0:T(8,128)S(1)}, f32[8,32,128]{2,1,0:T(8,128)S(1)}, u32[]{:S(2)}, u32[]{:S(2)}) collective-permute-start(f32[8,32,128]{2,1,0:T(8,128)S(1)} %slice.63), channel_id=1, source_target_pairs={{0,8},{2,10},{4,12},{6,14},{8,0},{10,2},{12,4},{14,6},{16,24},{18,... | collective-permute-start | bytes 393224 | tf_op jit(solution)/shard_map/ppermute | solution.py:287
  120.0 7.2 %collective-permute-done.4 = f32[8,32,128]{2,1,0:T(8,128)S(1)} collective-permute-done((f32[8,32,128]{2,1,0:T(8,128)S(1)}, f32[8,32,128]{2,1,0:T(8,128)S(1)}, u32[]{:S(2)}, u32[]{:S(2)}) %collective-permute-start.4) | collective-permute-done | bytes 131104 | tf_op jit(solution)/shard_map/ppermute | solution.py:287
  127.3 7.5 %collective-permute-start.5 = (f32[4,32,128]{2,1,0:T(8,128)S(1)}, f32[4,32,128]{2,1,0:T(8,128)S(1)}, u32[]{:S(2)}, u32[]{:S(2)}) collective-permute-start(f32[4,32,128]{2,1,0:T(8,128)S(1)} %slice.65), channel_id=1, source_target_pairs={{0,64},{2,66},{4,68},{6,70},{8,72},{10,74},{12,76},{14,78},{16,80}... | collective-permute-start | bytes 196616 | tf_op jit(solution)/shard_map/ppermute | solution.py:287
  134.8 2.7 %collective-permute-done.5 = f32[4,32,128]{2,1,0:T(8,128)S(1)} collective-permute-done((f32[4,32,128]{2,1,0:T(8,128)S(1)}, f32[4,32,128]{2,1,0:T(8,128)S(1)}, u32[]{:S(2)}, u32[]{:S(2)}) %collective-permute-start.5) | collective-permute-done | bytes 65568 | tf_op jit(solution)/shard_map/ppermute | solution.py:287
  137.6 1.5 collective-permute-start.6
  139.0 3.5 %collective-permute-done.6 = f32[2,32,128]{2,1,0:T(8,128)S(1)} collective-permute-done((f32[2,32,128]{2,1,0:T(8,128)S(1)}, f32[2,32,128]{2,1,0:T(8,128)S(1)}, u32[]{:S(2)}, u32[]{:S(2)}) %collective-permute-start.6) | collective-permute-done | bytes 32800 | tf_op jit(solution)/shard_map/ppermute | solution.py:287
  142.5 1.6 %collective-permute-start.7 = (f32[1,32,128]{2,1,0:T(8,128)S(1)}, f32[1,32,128]{2,1,0:T(8,128)S(1)}, u32[]{:S(2)}, u32[]{:S(2)}) collective-permute-start(f32[1,32,128]{2,1,0:T(8,128)S(1)} %slice.69), channel_id=1, source_target_pairs={{0,16},{2,18},{4,20},{6,22},{8,24},{10,26},{12,28},{14,30},{16,0},... | collective-permute-start | bytes 49160 | tf_op jit(solution)/shard_map/ppermute | solution.py:287
  144.1 0.2 collective-permute-start.1
  144.4 1.9 %collective-permute-done.7 = f32[1,32,128]{2,1,0:T(8,128)S(1)} collective-permute-done((f32[1,32,128]{2,1,0:T(8,128)S(1)}, f32[1,32,128]{2,1,0:T(8,128)S(1)}, u32[]{:S(2)}, u32[]{:S(2)}) %collective-permute-start.7) | collective-permute-done | bytes 16416 | tf_op jit(solution)/shard_map/ppermute | solution.py:287
  146.3 0.6 fusion.3
  146.9 3.0 %collective-permute-done.1 = bf16[64,512]{1,0:T(8,128)(2,1)S(1)} collective-permute-done((bf16[64,512]{1,0:T(8,128)(2,1)S(1)}, bf16[64,512]{1,0:T(8,128)(2,1)S(1)}, u32[]{:S(2)}, u32[]{:S(2)}) %collective-permute-start.1) | collective-permute-done | bytes 65568 | tf_op jit(solution)/shard_map/ppermute | solution.py:386
  149.9 2.5 %shard_map.71 = bf16[64,17408]{1,0:T(8,128)(2,1)} custom-call(bf16[256,32,128]{2,1,0:T(8,128)(2,1)S(1)} %all-to-all-done.1.got_ref, bf16[64,512]{1,0:T(8,128)(2,1)S(1)} %get-tuple-element.16.tail_low_ref, bf16[64,512]{1,0:T(8,128)(2,1)S(1)} %get-tuple-element.15.tail_high_ref), custom_call_target="tpu_custom_call" | custom-call | flops 4000000 | bytes 6000000 | tf_op jit(solution)/shard_map/pallas_call | solution.py:273
  (31 shorter events, 1.1 us)
Async XLA Ops:
  2.2 1.6 %copy-start = (bf16[64,17408]{1,0:T(8,128)(2,1)S(1)}, bf16[64,17408]{1,0:T(8,128)(2,1)}, u32[]{:S(2)}) copy-start(bf16[64,17408]{1,0:T(8,128)(2,1)} %archive_ref.2) | copy-start | bytes 6684676
  6.3 13.9 %copy-start.2 = (s32[32,30]{1,0:T(8,128)S(1)}, s32[32,30]{1,0:T(8,128)}, u32[]{:S(2)}) copy-start(s32[32,30]{1,0:T(8,128)} %param.8) | copy-start | bytes 11524
  6.3 14.0 %copy-start.3 = (s32[32,30]{1,0:T(8,128)S(1)}, s32[32,30]{1,0:T(8,128)}, u32[]{:S(2)}) copy-start(s32[32,30]{1,0:T(8,128)} %param.9) | copy-start | bytes 11524
  6.3 54.3 %all-to-all-start = ((bf16[128,48,128]{2,1,0:T(8,128)(2,1)}), bf16[128,48,128]{2,1,0:T(8,128)(2,1)S(1)}, u32[]{:S(2)}, u32[]{:S(2)}) async-start(bf16[128,48,128]{2,1,0:T(8,128)(2,1)} %shard_map.68), calls=%async_computation | async-start | bytes 3145728 | tf_op jit(solution)/shard_map/all_to_all | solution.py:339
  20.4 3.1 %copy-start.4 = (s32[64]{0:T(128)S(1)}, s32[64]{0:T(128)}, u32[]{:S(2)}) copy-start(s32[64]{0:T(128)} %param.6) | copy-start | bytes 772
  24.4 2.4 %copy-start.1 = (bf16[64,17408]{1,0:T(8,128)(2,1)S(1)}, bf16[64,17408]{1,0:T(8,128)(2,1)}, u32[]{:S(2)}) copy-start(bf16[64,17408]{1,0:T(8,128)(2,1)} %archive_ref.2) | copy-start | bytes 6684676
  40.0 2.7 %collective-permute-start = (f32[64,32,128]{2,1,0:T(8,128)S(1)}, f32[64,32,128]{2,1,0:T(8,128)S(1)}, u32[]{:S(2)}, u32[]{:S(2)}) collective-permute-start(f32[64,32,128]{2,1,0:T(8,128)S(1)} %slice.57), channel_id=1, source_target_pairs={{0,2},{2,0},{4,6},{6,4},{8,10},{10,8},{12,14},{14,12},{16,18},{18,... | collective-permute-start | bytes 3145736 | tf_op jit(solution)/shard_map/ppermute | solution.py:287
  72.1 77.8 %all-to-all-start.1 = ((bf16[256,32,128]{2,1,0:T(8,128)(2,1)}), bf16[256,32,128]{2,1,0:T(8,128)(2,1)S(1)}, u32[]{:S(2)}, u32[]{:S(2)}) async-start(bf16[256,32,128]{2,1,0:T(8,128)(2,1)} %bitcast.7), calls=%async_computation.1 | async-start | bytes 4194304 | tf_op jit(solution)/shard_map/all_to_all | solution.py:385
  80.1 24.4 %collective-permute-start.2 = (f32[32,32,128]{2,1,0:T(8,128)S(1)}, f32[32,32,128]{2,1,0:T(8,128)S(1)}, u32[]{:S(2)}, u32[]{:S(2)}) collective-permute-start(f32[32,32,128]{2,1,0:T(8,128)S(1)} %slice.59), channel_id=1, source_target_pairs={{0,128},{2,130},{4,132},{6,134},{8,136},{10,138},{12,140},{14,142}... | collective-permute-start | bytes 1572872 | tf_op jit(solution)/shard_map/ppermute | solution.py:287
  104.7 13.2 %collective-permute-start.3 = (f32[16,32,128]{2,1,0:T(8,128)S(1)}, f32[16,32,128]{2,1,0:T(8,128)S(1)}, u32[]{:S(2)}, u32[]{:S(2)}) collective-permute-start(f32[16,32,128]{2,1,0:T(8,128)S(1)} %slice.61), channel_id=1, source_target_pairs={{0,4},{2,6},{4,0},{6,2},{8,12},{10,14},{12,8},{14,10},{16,20},{18,... | collective-permute-start | bytes 786440 | tf_op jit(solution)/shard_map/ppermute | solution.py:287
  118.0 9.3 %collective-permute-start.4 = (f32[8,32,128]{2,1,0:T(8,128)S(1)}, f32[8,32,128]{2,1,0:T(8,128)S(1)}, u32[]{:S(2)}, u32[]{:S(2)}) collective-permute-start(f32[8,32,128]{2,1,0:T(8,128)S(1)} %slice.63), channel_id=1, source_target_pairs={{0,8},{2,10},{4,12},{6,14},{8,0},{10,2},{12,4},{14,6},{16,24},{18,... | collective-permute-start | bytes 393224 | tf_op jit(solution)/shard_map/ppermute | solution.py:287
  127.3 10.2 %collective-permute-start.5 = (f32[4,32,128]{2,1,0:T(8,128)S(1)}, f32[4,32,128]{2,1,0:T(8,128)S(1)}, u32[]{:S(2)}, u32[]{:S(2)}) collective-permute-start(f32[4,32,128]{2,1,0:T(8,128)S(1)} %slice.65), channel_id=1, source_target_pairs={{0,64},{2,66},{4,68},{6,70},{8,72},{10,74},{12,76},{14,78},{16,80}... | collective-permute-start | bytes 196616 | tf_op jit(solution)/shard_map/ppermute | solution.py:287
  137.6 4.9 %collective-permute-start.6 = (f32[2,32,128]{2,1,0:T(8,128)S(1)}, f32[2,32,128]{2,1,0:T(8,128)S(1)}, u32[]{:S(2)}, u32[]{:S(2)}) collective-permute-start(f32[2,32,128]{2,1,0:T(8,128)S(1)} %slice.67), channel_id=1, source_target_pairs={{0,32},{2,34},{4,36},{6,38},{8,40},{10,42},{12,44},{14,46},{16,48}... | collective-permute-start | bytes 98312 | tf_op jit(solution)/shard_map/ppermute | solution.py:287
  142.5 3.8 %collective-permute-start.7 = (f32[1,32,128]{2,1,0:T(8,128)S(1)}, f32[1,32,128]{2,1,0:T(8,128)S(1)}, u32[]{:S(2)}, u32[]{:S(2)}) collective-permute-start(f32[1,32,128]{2,1,0:T(8,128)S(1)} %slice.69), channel_id=1, source_target_pairs={{0,16},{2,18},{4,20},{6,22},{8,24},{10,26},{12,28},{14,30},{16,0},... | collective-permute-start | bytes 49160 | tf_op jit(solution)/shard_map/ppermute | solution.py:287
  144.1 5.8 %collective-permute-start.1 = (bf16[64,512]{1,0:T(8,128)(2,1)S(1)}, bf16[64,512]{1,0:T(8,128)(2,1)S(1)}, u32[]{:S(2)}, u32[]{:S(2)}) collective-permute-start(bf16[64,512]{1,0:T(8,128)(2,1)S(1)} %get-tuple-element.11), channel_id=1, source_target_pairs={{0,1},{1,0},{2,3},{3,2},{4,5},{5,4},{6,7},{7,6},{8,9},{9,8},{10,11... | collective-permute-start | bytes 196616 | tf_op jit(solution)/shard_map/ppermute | solution.py:386

commit v3 on v2

--- a/solution.py
+++ b/solution.py
@@ -14,6 +14,8 @@
 SPAN = KW * LANES
 MIB = 1024 * 1024
 PARTS = 4
+GROUP = 16
+EARLY = 3
 
 
 def roll_half(x):
@@ -32,24 +34,38 @@
 
 
 def pack_kernel(
-    half_ref, base_ref, info_ref, archive_ref, out_hbm, out_ref, tail_ref, sems, *, rows, tiles, tail_tiles
+    half_ref, base_ref, info_ref, archive_hbm, out_hbm, archive_ref, out_ref, tail_ref, get_sems, sems,
+    *, rows, tiles, tail_tiles,
 ):
     which = half_ref[0]
     half = rows // 2
     left = left_lanes(half)
     owners = out_ref.shape[0]
     tail_lines = 2 * tail_tiles
+    width, tail_width = tiles * LANES, tail_tiles * LANES
+
+    def fetch(start, at, size, number):
+        start = pl.multiple_of(start, LANES)
+        copy = pltpu.make_async_copy(
+            archive_hbm.at[:, pl.ds(start, size)], archive_ref.at[:, pl.ds(at, size)], get_sems.at[number]
+        )
+        copy.start()
+        return copy
+
+    tail_fetch = fetch(2 * width + which * tail_width, width, tail_width, PARTS)
+    part_width = width // PARTS
+    fetches = [fetch(which * width + part * part_width, part * part_width, part_width, part) for part in range(PARTS)]
     tail_ref[...] = jnp.zeros_like(tail_ref)
-    tail_start = 2 * tiles * LANES
     info = info_ref[...]
+    tail_fetch.wait()
     for tile in range(tail_tiles):
-        at = pl.multiple_of(tail_start + (which * tail_tiles + tile) * LANES, LANES)
-        block = archive_ref[:, pl.ds(at, LANES)].astype(jnp.float32)
+        at = width + tile * LANES
+        block = archive_ref[:, at : at + LANES].astype(jnp.float32)
         for row in range(rows):
             tail_ref[pl.ds(base_ref[row] * tail_tiles + tile, 1), :] = block[row : row + 1, :]
 
     def one(tile, carry):
-        at = pl.multiple_of((which * tiles + tile) * LANES, LANES)
+        at = pl.multiple_of(tile * LANES, LANES)
         block = archive_ref[:, pl.ds(at, LANES)].astype(jnp.float32)
         upper, lower = block[:half], block[half:]
         even = jnp.where(left, upper, roll_half(lower))
@@ -62,6 +78,7 @@
 
     copies = []
     for part in range(PARTS):
+        fetches[part].wait()
         lax.fori_loop(part * tiles // PARTS, (part + 1) * tiles // PARTS, one, 0, unroll=8)
         copies.append(send_part(out_ref, out_hbm, part, owners // PARTS, sems.at[part]))
     for copy in copies:
@@ -70,7 +87,7 @@
 
 def permute_kernel(
     owner_ref, got_ref, out_hbm, tail_out_ref,
-    out_ref, plain_ref, placed_ref, tail_ref, tail_rows_ref, info_ref, route_ref, route_smem, route_sem, sems,
+    out_ref, placed_ref, tail_ref, tail_rows_ref, info_ref, route_ref, route_smem, route_sem, sems,
     *, rows, tail_tiles,
 ):
     stations = got_ref.shape[0]
@@ -101,25 +118,24 @@
     route_copy = pltpu.make_async_copy(route_ref, route_smem, route_sem)
     route_copy.start()
 
-    def expand(station, carry):
+    def tails(station, carry):
         block = got_ref[station].astype(jnp.float32)
-        lines = block[:half]
-        at = pl.multiple_of(station * rows, 8)
-        plain_ref[pl.ds(at, half), :] = lines
-        plain_ref[pl.ds(at + half, half), :] = roll_half(lines)
         tail_ref[pl.ds(pl.multiple_of(station * tail_lines, 8), tail_lines), :] = block[half : half + tail_lines]
         return carry
 
-    lax.fori_loop(0, stations, expand, 0, unroll=8)
+    lax.fori_loop(0, stations, tails, 0, unroll=8)
     route_copy.wait()
 
     def move(station, carry):
-        lines = plain_ref[pl.ds(pl.multiple_of(station * rows, 8), rows), :]
-        for row in range(rows):
-            placed_ref[pl.ds(route_smem[station, row], 1), :] = lines[row : row + 1, :]
-        return carry
-
-    lax.fori_loop(0, stations, move, 0)
+        upper = got_ref[station].astype(jnp.float32)[:half]
+        lower = roll_half(upper)
+        for row in range(half):
+            placed_ref[pl.ds(route_smem[station, row], 1), :] = upper[row : row + 1, :]
+        for row in range(half):
+            placed_ref[pl.ds(route_smem[station, half + row], 1), :] = lower[row : row + 1, :]
+        return carry
+
+    lax.fori_loop(0, stations, move, 0, unroll=2)
 
     def join(station, carry):
         at = pl.multiple_of(station * rows, 8)
@@ -203,7 +219,7 @@
 
 def correlate_kernel(
     count_ref, entry_ref, row_ref, shift_ref, place_ref, archive_ref, wave_ref, out_ref,
-    series_ref, line_ref, high_ref, low_ref, *, length, channels, bits,
+    series_ref, line_ref, high_ref, low_ref, group_ref, *, length, bits,
 ):
     rows = archive_ref.shape[0]
     tiles = archive_ref.shape[1] // LANES
@@ -241,7 +257,11 @@
                 [ref[k : k + blocks, :].astype(jnp.bfloat16) for k in range(KW)], axis=1
             )
 
-        wave = wave_ref[pl.ds(entry, 1), :]
+        group = pl.multiple_of(entry // GROUP * GROUP, GROUP)
+        group_ref[...] = wave_ref[pl.ds(group, GROUP), :].astype(jnp.float32)
+        wave = jnp.concatenate(
+            [group_ref[pl.ds(entry % GROUP, 1), :], jnp.zeros((1, SPAN - length), jnp.float32)], axis=1
+        )
         power = jnp.sum(wave * wave, axis=1, keepdims=True)
         base = pltpu.roll(jnp.broadcast_to(wave, (8, SPAN)), fine, 1)
         banded = pltpu.roll(
@@ -255,7 +275,7 @@
         ) + lax.dot_general(windows(low_ref), mask, contract, preferred_element_type=jnp.float32)
         scale = (energy / length + EPSILON) * (power / length + EPSILON)
         normalized = product / length / jnp.sqrt(scale)
-        template = entry // channels
+        template = entry % out_ref.shape[1]
         for block in range(blocks):
             at = (place_of(block, bits) ^ my_place, pl.ds(template, 1), slice(None))
             out_ref[at] = out_ref[at] + normalized[block : block + 1, :]
@@ -269,11 +289,13 @@
 HBM_SPEC = pl.BlockSpec(memory_space=pltpu.HBM)
 
 
-def kernel_call(body, scalars, arrays, outs, scratch, flops, moved, vmem, out_specs=VMEM_SPEC):
+def kernel_call(
+    body, scalars, arrays, outs, scratch, flops, moved, vmem, out_specs=VMEM_SPEC, in_specs=None
+):
     return pl.pallas_call(
         body,
         out_shape=outs,
-        in_specs=[SMEM_SPEC] * len(scalars) + [VMEM_SPEC] * len(arrays),
+        in_specs=[SMEM_SPEC] * len(scalars) + (in_specs or [VMEM_SPEC] * len(arrays)),
         out_specs=out_specs,
         scratch_shapes=scratch,
         compiler_params=pltpu.CompilerParams(vmem_limit_bytes=vmem * MIB),
@@ -329,23 +351,25 @@
         (info, archive),
         shape((stations, block_lines, LANES), bf16),
         [
+            pltpu.VMEM((rows, (tiles + tail_tiles) * LANES), bf16),
             pltpu.VMEM((stations, block_lines, LANES), bf16),
             pltpu.VMEM((stations * 2 * tail_tiles, LANES), f32),
+            pltpu.SemaphoreType.DMA((PARTS + 1,)),
             pltpu.SemaphoreType.DMA((PARTS,)),
         ],
-        4_000_000, 4_000_000, 12, HBM_SPEC,
+        4_000_000, 4_000_000, 56, HBM_SPEC, [VMEM_SPEC, HBM_SPEC],
     )
     packed, later_archive = lax.optimization_barrier((packed, archive))
     first = lax.all_to_all(packed, "stn", 0, 0, tiled=True)
 
-    entries, entry_row, entry_count = owned_entries(slot_of_row, template_channels)
-    waves = jnp.pad(templates.reshape(-1, length).astype(f32), ((0, 0), (0, SPAN - length)))
+    entries, entry_row, entry_count = owned_entries(slot_of_row, template_channels.T)
+    waves = templates.transpose(1, 0, 2).reshape(-1, length)
     padded = samples // LANES + 8
     bits = halving_bits(sizes)
     my_place = place_of(my_index.astype(i32), bits).reshape(1)
     partial = kernel_call(
-        functools.partial(correlate_kernel, length=length, channels=channels, bits=bits),
-        (entry_count, entries, entry_row, moveouts.reshape(-1), my_place),
+        functools.partial(correlate_kernel, length=length, bits=bits),
+        (entry_count, entries, entry_row, moveouts.T.reshape(-1), my_place),
         (later_archive, waves),
         shape((stations, local_templates, LANES), f32),
         [
@@ -353,12 +377,14 @@
             pltpu.VMEM((LANES + 8, LANES), f32),
             pltpu.VMEM((LANES + 8, LANES), f32),
             pltpu.VMEM((LANES + 8, LANES), f32),
+            pltpu.VMEM((GROUP, length), f32),
         ],
         1000, 1000, 28,
     )
-    partial = halve(partial, bits[0], stations)
+    for bit in bits[:EARLY]:
+        partial = halve(partial, bit, stations)
     first, _ = lax.optimization_barrier((first, partial))
-    for bit in bits[1:]:
+    for bit in bits[EARLY:]:
         partial = halve(partial, bit, stations)
     stack = partial[0] * math.sqrt(length / channels)
 
@@ -369,7 +395,6 @@
         (shape((stations, 2, half, LANES), bf16), shape((rows, tail_tiles * LANES), bf16)),
         [
             pltpu.VMEM((stations, half, LANES), bf16),
-            pltpu.VMEM((stations * rows, LANES), f32),
             pltpu.VMEM((stations * rows, LANES), f32),
             pltpu.VMEM((stations * 2 * tail_tiles, LANES), f32),
             pltpu.VMEM((tail_tiles, rows + 8, LANES), f32),

time: 153 us -> 164 us (1.072)
  waiting for transfers between devices: 72.9 us -> 81.6 us
  starting transfers between devices: 38.3 us -> 44 us
  local copies, waits for them, and re-layouts: 5.12 us -> 1.09 us
    ppermute x7, waiting for transfers between devices: 52.2 us -> 79.2 us  [halve(): return partial[:half] + lax.ppermute(partial[half:], 'stn', pairs)]
    all_to_all x1, waiting for transfers between devices: 17.7 us -> 0.01 us  [shards(): first = lax.all_to_all(packed, 'stn', 0, 0, tiled=True)]
    unnamed x11 -> x10, local copies, waits for them, and re-layouts: 3.34 us -> 0.03 us
    ppermute x7, starting transfers between devices: 16.2 us -> 18.7 us  [halve(): return partial[:half] + lax.ppermute(partial[half:], 'stn', pairs)]
    all_to_all x1, starting transfers between devices: 7.98 us -> 10.3 us  [shards(): second = lax.all_to_all(lines, ('stn', 'tpl'), 0, 0, tiled=True)]
    pad x1 -> x0, other arithmetic: 1.66 us -> none  [shards(): jnp.pad(templates.reshape(-1, length).astype(f32), ((0, 0), (0, SPAN - le...]
  transfers between devices with their start and end apart: 10 -> 10, of which waited for: 9 -> 8; matrix products, arithmetic and copies ran while one was open for 5% -> 2% of each run, Pallas kernels for 9% -> 6%
where the time goes in v3:
time: 164 us; the launch traced here: 163 us
  waiting for transfers between devices  81.6 us (50%)
  starting transfers between devices  44 us (27%)
  Pallas kernels  30.8 us (19%)
  other arithmetic  4.67 us (3%)
    ppermute x7, waiting for transfers between devices, halve(): return partial[:half] + lax.ppermute(partial[half:], 'stn', pairs)  79.2 us
    pallas_call x4, Pallas kernels, kernel_call(): pl.pallas_call(body, out_shape=outs, in_specs=[SMEM_SPEC] * len(scalars)...  30.8 us
    ppermute x7, starting transfers between devices, halve(): return partial[:half] + lax.ppermute(partial[half:], 'stn', pairs)  18.7 us
    all_to_all x1, starting transfers between devices, shards(): first = lax.all_to_all(packed, 'stn', 0, 0, tiled=True)  14.5 us
    all_to_all x1, starting transfers between devices, shards(): second = lax.all_to_all(lines, ('stn', 'tpl'), 0, 0, tiled=True)  10.3 us
  transfers between devices with their start and end apart: 10, of which 8 were waited for; matrix products, arithmetic and copies ran while one was open for 2% of the time, Pallas kernels for 6%

profile of v3, /device:TPU:16, one launch (start us, length us, event | category | flops | bytes accessed | tf_op | source)
XLA Modules:
  0.0 162.9 jit_solution(13721755528432360544)
XLA Ops:
  0.6 0.7 and_select_fusion.1
  1.3 0.2 convert_reduce_fusion.2
  1.5 1.2 fusion.4
  2.8 0.6 broadcast_in_dim.21.info_ref
  3.4 3.5 %shard_map.68 = bf16[128,48,128]{2,1,0:T(8,128)(2,1)} custom-call(s32[1]{0:T(128)} %bitcast.1.half_ref, s32[64]{0:T(128)} %get-tuple-element.18.base_ref, f32[8,128]{1,0:T(8,128)} %broadcast_in_dim.21.info_ref, bf16[64,17408]{1,0:T(8,128)(2,1)} %archive_ref), custom_call_target="tpu_custom_call" | custom-call | flops 4000000 | bytes 4000000 | tf_op jit(solution)/shard_map/pallas_call | solution.py:295
  6.9 14.5 %all-to-all-start = ((bf16[128,48,128]{2,1,0:T(8,128)(2,1)}), bf16[128,48,128]{2,1,0:T(8,128)(2,1)}, u32[]{:S(2)}, u32[]{:S(2)}) async-start(bf16[128,48,128]{2,1,0:T(8,128)(2,1)} %shard_map.68), calls=%async_computation | async-start | bytes 3145728 | tf_op jit(solution)/shard_map/all_to_all | solution.py:363
  21.6 0.8 fusion
  22.5 0.2 select_reduce_fusion.1
  22.9 0.5 select_reduce_fusion.entry_ref
  23.4 10.1 %shard_map.69 = f32[128,32,128]{2,1,0:T(8,128)S(1)} custom-call(s32[1]{0:T(128)} %bitcast.3.count_ref, s32[960]{0:T(1024)S(1)} %select_reduce_fusion.entry_ref, s32[960]{0:T(1024)S(1)} %get-tuple-element.12.row_ref, s32[960]{0:T(1024)S(1)} %reshape.56.shift_ref, s32[1]{0:T(128)} %bitcast.5.place_ref, bf16[64,17408]{1,0:T(8,128)(2,1)S(1)} %copy-done, ...), custom_call_target="tpu_custom_call" | custom-call | flops 1000 | bytes 1000 | tf_op jit(solution)/shard_map/pallas_call | solution.py:295
  33.6 4.6 %collective-permute-start = (f32[64,32,128]{2,1,0:T(8,128)S(1)}, f32[64,32,128]{2,1,0:T(8,128)S(1)}, u32[]{:S(2)}, u32[]{:S(2)}) collective-permute-start(f32[64,32,128]{2,1,0:T(8,128)S(1)} %slice.57), channel_id=1, source_target_pairs={{0,2},{2,0},{4,6},{6,4},{8,10},{10,8},{12,14},{14,12},{16,18},{18,... | collective-permute-start | bytes 3145736 | tf_op jit(solution)/shard_map/ppermute | solution.py:309
  38.2 2.3 %collective-permute-done = f32[64,32,128]{2,1,0:T(8,128)S(1)} collective-permute-done((f32[64,32,128]{2,1,0:T(8,128)S(1)}, f32[64,32,128]{2,1,0:T(8,128)S(1)}, u32[]{:S(2)}, u32[]{:S(2)}) %collective-permute-start) | collective-permute-done | bytes 1048608 | tf_op jit(solution)/shard_map/ppermute | solution.py:309
  40.5 0.2 slice_add_fusion
  40.7 0.1 collective-permute-start.1
  40.8 21.3 %collective-permute-done.1 = f32[32,32,128]{2,1,0:T(8,128)S(1)} collective-permute-done((f32[32,32,128]{2,1,0:T(8,128)S(1)}, f32[32,32,128]{2,1,0:T(8,128)S(1)}, u32[]{:S(2)}, u32[]{:S(2)}) %collective-permute-start.1) | collective-permute-done | bytes 524320 | tf_op jit(solution)/shard_map/ppermute | solution.py:309
  62.1 0.1 slice_add_fusion.1
  62.2 0.1 collective-permute-start.2
  62.3 8.0 %collective-permute-done.2 = f32[16,32,128]{2,1,0:T(8,128)S(1)} collective-permute-done((f32[16,32,128]{2,1,0:T(8,128)S(1)}, f32[16,32,128]{2,1,0:T(8,128)S(1)}, u32[]{:S(2)}, u32[]{:S(2)}) %collective-permute-start.2) | collective-permute-done | bytes 262176 | tf_op jit(solution)/shard_map/ppermute | solution.py:309
  70.4 14.6 %shard_map.70 = (bf16[128,2,32,128]{3,2,1,0:T(8,128)(2,1)}, bf16[64,512]{1,0:T(8,128)(2,1)S(1)}) custom-call(s32[1]{0:T(128)} %bitcast.owner_ref, bf16[128,48,128]{2,1,0:T(8,128)(2,1)} %all-to-all-done.got_ref), custom_call_target="tpu_custom_call" | custom-call | flops 4000000 | bytes 30000000 | tf_op jit(solution)/shard_map/pallas_call | solution.py:295
  84.9 10.3 %all-to-all-start.1 = ((bf16[256,32,128]{2,1,0:T(8,128)(2,1)}), bf16[256,32,128]{2,1,0:T(8,128)(2,1)S(1)}, u32[]{:S(2)}, u32[]{:S(2)}) async-start(bf16[256,32,128]{2,1,0:T(8,128)(2,1)} %bitcast.13), calls=%async_computation.1 | async-start | bytes 4194304 | tf_op jit(solution)/shard_map/all_to_all | solution.py:410
  95.3 3.1 %collective-permute-start.4 = (f32[8,32,128]{2,1,0:T(8,128)S(1)}, f32[8,32,128]{2,1,0:T(8,128)S(1)}, u32[]{:S(2)}, u32[]{:S(2)}) collective-permute-start(f32[8,32,128]{2,1,0:T(8,128)S(1)} %slice.63), channel_id=1, source_target_pairs={{0,8},{2,10},{4,12},{6,14},{8,0},{10,2},{12,4},{14,6},{16,24},{18,... | collective-permute-start | bytes 393224 | tf_op jit(solution)/shard_map/ppermute | solution.py:309
  98.3 7.8 %collective-permute-done.4 = f32[8,32,128]{2,1,0:T(8,128)S(1)} collective-permute-done((f32[8,32,128]{2,1,0:T(8,128)S(1)}, f32[8,32,128]{2,1,0:T(8,128)S(1)}, u32[]{:S(2)}, u32[]{:S(2)}) %collective-permute-start.4) | collective-permute-done | bytes 131104 | tf_op jit(solution)/shard_map/ppermute | solution.py:309
  106.1 9.2 %collective-permute-start.5 = (f32[4,32,128]{2,1,0:T(8,128)S(1)}, f32[4,32,128]{2,1,0:T(8,128)S(1)}, u32[]{:S(2)}, u32[]{:S(2)}) collective-permute-start(f32[4,32,128]{2,1,0:T(8,128)S(1)} %slice.65), channel_id=1, source_target_pairs={{0,64},{2,66},{4,68},{6,70},{8,72},{10,74},{12,76},{14,78},{16,80}... | collective-permute-start | bytes 196616 | tf_op jit(solution)/shard_map/ppermute | solution.py:309
  115.3 33.3 %collective-permute-done.5 = f32[4,32,128]{2,1,0:T(8,128)S(1)} collective-permute-done((f32[4,32,128]{2,1,0:T(8,128)S(1)}, f32[4,32,128]{2,1,0:T(8,128)S(1)}, u32[]{:S(2)}, u32[]{:S(2)}) %collective-permute-start.5) | collective-permute-done | bytes 65568 | tf_op jit(solution)/shard_map/ppermute | solution.py:309
  148.7 0.7 collective-permute-start.6
  149.3 4.2 %collective-permute-done.6 = f32[2,32,128]{2,1,0:T(8,128)S(1)} collective-permute-done((f32[2,32,128]{2,1,0:T(8,128)S(1)}, f32[2,32,128]{2,1,0:T(8,128)S(1)}, u32[]{:S(2)}, u32[]{:S(2)}) %collective-permute-start.6) | collective-permute-done | bytes 32800 | tf_op jit(solution)/shard_map/ppermute | solution.py:309
  153.6 1.0 collective-permute-start.7
  154.6 0.4 collective-permute-start.3
  155.0 2.4 %collective-permute-done.7 = f32[1,32,128]{2,1,0:T(8,128)S(1)} collective-permute-done((f32[1,32,128]{2,1,0:T(8,128)S(1)}, f32[1,32,128]{2,1,0:T(8,128)S(1)}, u32[]{:S(2)}, u32[]{:S(2)}) %collective-permute-start.7) | collective-permute-done | bytes 16416 | tf_op jit(solution)/shard_map/ppermute | solution.py:309
  157.4 0.6 fusion.3
  158.0 2.4 %collective-permute-done.3 = bf16[64,512]{1,0:T(8,128)(2,1)S(1)} collective-permute-done((bf16[64,512]{1,0:T(8,128)(2,1)S(1)}, bf16[64,512]{1,0:T(8,128)(2,1)S(1)}, u32[]{:S(2)}, u32[]{:S(2)}) %collective-permute-start.3) | collective-permute-done | bytes 65568 | tf_op jit(solution)/shard_map/ppermute | solution.py:411
  160.4 2.5 %shard_map.71 = bf16[64,17408]{1,0:T(8,128)(2,1)} custom-call(bf16[256,32,128]{2,1,0:T(8,128)(2,1)S(1)} %all-to-all-done.1.got_ref, bf16[64,512]{1,0:T(8,128)(2,1)S(1)} %get-tuple-element.16.tail_low_ref, bf16[64,512]{1,0:T(8,128)(2,1)S(1)} %get-tuple-element.15.tail_high_ref), custom_call_target="tpu_custom_call" | custom-call | flops 4000000 | bytes 6000000 | tf_op jit(solution)/shard_map/pallas_call | solution.py:295
  (30 shorter events, 0.7 us)
Async XLA Ops:
  3.4 20.0 %copy-start.1 = (bf16[32,30,600]{2,0,1:T(8,128)(2,1)S(1)}, bf16[32,30,600]{2,0,1:T(8,128)(2,1)}, u32[]{:S(2)}) copy-start(bf16[32,30,600]{2,0,1:T(8,128)(2,1)} %param.7) | copy-start | bytes 3456004
  6.9 14.5 %copy-start.2 = (s32[32,30]{1,0:T(8,128)S(1)}, s32[32,30]{1,0:T(8,128)}, u32[]{:S(2)}) copy-start(s32[32,30]{1,0:T(8,128)} %param.8) | copy-start | bytes 11524
  6.9 14.7 %copy-start.4 = (s32[64]{0:T(128)S(1)}, s32[64]{0:T(128)}, u32[]{:S(2)}) copy-start(s32[64]{0:T(128)} %param.6) | copy-start | bytes 772
  6.9 15.8 %copy-start.3 = (s32[32,30]{1,0:T(8,128)S(1)}, s32[32,30]{1,0:T(8,128)}, u32[]{:S(2)}) copy-start(s32[32,30]{1,0:T(8,128)} %param.9) | copy-start | bytes 11524
  6.9 16.4 %copy-start = (bf16[64,17408]{1,0:T(8,128)(2,1)S(1)}, bf16[64,17408]{1,0:T(8,128)(2,1)}, u32[]{:S(2)}) copy-start(bf16[64,17408]{1,0:T(8,128)(2,1)} %archive_ref) | copy-start | bytes 6684676
  6.9 63.4 %all-to-all-start = ((bf16[128,48,128]{2,1,0:T(8,128)(2,1)}), bf16[128,48,128]{2,1,0:T(8,128)(2,1)}, u32[]{:S(2)}, u32[]{:S(2)}) async-start(bf16[128,48,128]{2,1,0:T(8,128)(2,1)} %shard_map.68), calls=%async_computation | async-start | bytes 3145728 | tf_op jit(solution)/shard_map/all_to_all | solution.py:363
  33.6 6.9 %collective-permute-start = (f32[64,32,128]{2,1,0:T(8,128)S(1)}, f32[64,32,128]{2,1,0:T(8,128)S(1)}, u32[]{:S(2)}, u32[]{:S(2)}) collective-permute-start(f32[64,32,128]{2,1,0:T(8,128)S(1)} %slice.57), channel_id=1, source_target_pairs={{0,2},{2,0},{4,6},{6,4},{8,10},{10,8},{12,14},{14,12},{16,18},{18,... | collective-permute-start | bytes 3145736 | tf_op jit(solution)/shard_map/ppermute | solution.py:309
  40.7 21.4 %collective-permute-start.1 = (f32[32,32,128]{2,1,0:T(8,128)S(1)}, f32[32,32,128]{2,1,0:T(8,128)S(1)}, u32[]{:S(2)}, u32[]{:S(2)}) collective-permute-start(f32[32,32,128]{2,1,0:T(8,128)S(1)} %slice.59), channel_id=1, source_target_pairs={{0,128},{2,130},{4,132},{6,134},{8,136},{10,138},{12,140},{14,142}... | collective-permute-start | bytes 1572872 | tf_op jit(solution)/shard_map/ppermute | solution.py:309
  62.2 8.1 %collective-permute-start.2 = (f32[16,32,128]{2,1,0:T(8,128)S(1)}, f32[16,32,128]{2,1,0:T(8,128)S(1)}, u32[]{:S(2)}, u32[]{:S(2)}) collective-permute-start(f32[16,32,128]{2,1,0:T(8,128)S(1)} %slice.61), channel_id=1, source_target_pairs={{0,4},{2,6},{4,0},{6,2},{8,12},{10,14},{12,8},{14,10},{16,20},{18,... | collective-permute-start | bytes 786440 | tf_op jit(solution)/shard_map/ppermute | solution.py:309
  84.9 75.5 %all-to-all-start.1 = ((bf16[256,32,128]{2,1,0:T(8,128)(2,1)}), bf16[256,32,128]{2,1,0:T(8,128)(2,1)S(1)}, u32[]{:S(2)}, u32[]{:S(2)}) async-start(bf16[256,32,128]{2,1,0:T(8,128)(2,1)} %bitcast.13), calls=%async_computation.1 | async-start | bytes 4194304 | tf_op jit(solution)/shard_map/all_to_all | solution.py:410
  95.3 10.8 %collective-permute-start.4 = (f32[8,32,128]{2,1,0:T(8,128)S(1)}, f32[8,32,128]{2,1,0:T(8,128)S(1)}, u32[]{:S(2)}, u32[]{:S(2)}) collective-permute-start(f32[8,32,128]{2,1,0:T(8,128)S(1)} %slice.63), channel_id=1, source_target_pairs={{0,8},{2,10},{4,12},{6,14},{8,0},{10,2},{12,4},{14,6},{16,24},{18,... | collective-permute-start | bytes 393224 | tf_op jit(solution)/shard_map/ppermute | solution.py:309
  106.1 42.5 %collective-permute-start.5 = (f32[4,32,128]{2,1,0:T(8,128)S(1)}, f32[4,32,128]{2,1,0:T(8,128)S(1)}, u32[]{:S(2)}, u32[]{:S(2)}) collective-permute-start(f32[4,32,128]{2,1,0:T(8,128)S(1)} %slice.65), channel_id=1, source_target_pairs={{0,64},{2,66},{4,68},{6,70},{8,72},{10,74},{12,76},{14,78},{16,80}... | collective-permute-start | bytes 196616 | tf_op jit(solution)/shard_map/ppermute | solution.py:309
  148.7 4.9 %collective-permute-start.6 = (f32[2,32,128]{2,1,0:T(8,128)S(1)}, f32[2,32,128]{2,1,0:T(8,128)S(1)}, u32[]{:S(2)}, u32[]{:S(2)}) collective-permute-start(f32[2,32,128]{2,1,0:T(8,128)S(1)} %slice.67), channel_id=1, source_target_pairs={{0,32},{2,34},{4,36},{6,38},{8,40},{10,42},{12,44},{14,46},{16,48}... | collective-permute-start | bytes 98312 | tf_op jit(solution)/shard_map/ppermute | solution.py:309
  153.6 3.8 %collective-permute-start.7 = (f32[1,32,128]{2,1,0:T(8,128)S(1)}, f32[1,32,128]{2,1,0:T(8,128)S(1)}, u32[]{:S(2)}, u32[]{:S(2)}) collective-permute-start(f32[1,32,128]{2,1,0:T(8,128)S(1)} %slice.69), channel_id=1, source_target_pairs={{0,16},{2,18},{4,20},{6,22},{8,24},{10,26},{12,28},{14,30},{16,0},... | collective-permute-start | bytes 49160 | tf_op jit(solution)/shard_map/ppermute | solution.py:309
  154.6 5.8 %collective-permute-start.3 = (bf16[64,512]{1,0:T(8,128)(2,1)S(1)}, bf16[64,512]{1,0:T(8,128)(2,1)S(1)}, u32[]{:S(2)}, u32[]{:S(2)}) collective-permute-start(bf16[64,512]{1,0:T(8,128)(2,1)S(1)} %get-tuple-element.11), channel_id=1, source_target_pairs={{0,1},{1,0},{2,3},{3,2},{4,5},{5,4},{6,7},{7,6},{8,9},{9,8},{10,11... | collective-permute-start | bytes 196616 | tf_op jit(solution)/shard_map/ppermute | solution.py:411

commit v4 on v3

--- a/solution.py
+++ b/solution.py
@@ -15,7 +15,6 @@
 MIB = 1024 * 1024
 PARTS = 4
 GROUP = 16
-EARLY = 3
 
 
 def roll_half(x):
@@ -34,7 +33,7 @@
 
 
 def pack_kernel(
-    half_ref, base_ref, info_ref, archive_hbm, out_hbm, archive_ref, out_ref, tail_ref, get_sems, sems,
+    half_ref, slot_ref, archive_hbm, out_hbm, archive_ref, out_ref, tail_ref, base_vmem, base_ref, get_sems, sems, base_sem,
     *, rows, tiles, tail_tiles,
 ):
     which = half_ref[0]
@@ -55,14 +54,26 @@
     tail_fetch = fetch(2 * width + which * tail_width, width, tail_width, PARTS)
     part_width = width // PARTS
     fetches = [fetch(which * width + part * part_width, part * part_width, part_width, part) for part in range(PARTS)]
+    slots = slot_ref[...]
+    target, place = slots // rows, slots % rows
+    before = lax.broadcasted_iota(jnp.int32, (rows, rows), 0)
+    after = lax.broadcasted_iota(jnp.int32, (rows, rows), 1)
+    across = jnp.broadcast_to(target, (rows, rows))
+    down = jnp.sum(jnp.where(before == after, across, 0), axis=1, keepdims=True)
+    rank = jnp.sum(jnp.where((across == down) & (before < after), 1, 0), axis=0, keepdims=True)
+    base_vmem[0:1, 0:rows] = target * 2 + rank
+    base_copy = pltpu.make_async_copy(base_vmem, base_ref, base_sem)
+    base_copy.start()
+    info = jnp.concatenate([target, place + rows * rank], axis=1).astype(jnp.float32)
+    info = jnp.broadcast_to(info, (8, LANES))
     tail_ref[...] = jnp.zeros_like(tail_ref)
-    info = info_ref[...]
     tail_fetch.wait()
+    base_copy.wait()
     for tile in range(tail_tiles):
         at = width + tile * LANES
         block = archive_ref[:, at : at + LANES].astype(jnp.float32)
         for row in range(rows):
-            tail_ref[pl.ds(base_ref[row] * tail_tiles + tile, 1), :] = block[row : row + 1, :]
+            tail_ref[pl.ds(base_ref[0, row] * tail_tiles + tile, 1), :] = block[row : row + 1, :]
 
     def one(tile, carry):
         at = pl.multiple_of(tile * LANES, LANES)
@@ -87,7 +98,7 @@
 
 def permute_kernel(
     owner_ref, got_ref, out_hbm, tail_out_ref,
-    out_ref, placed_ref, tail_ref, tail_rows_ref, info_ref, route_ref, route_smem, route_sem, sems,
+    out_ref, plain_ref, placed_ref, tail_ref, tail_rows_ref, info_ref, route_ref, route_smem, route_sem, sems,
     *, rows, tail_tiles,
 ):
     stations = got_ref.shape[0]
@@ -118,24 +129,25 @@
     route_copy = pltpu.make_async_copy(route_ref, route_smem, route_sem)
     route_copy.start()
 
-    def tails(station, carry):
+    def expand(station, carry):
         block = got_ref[station].astype(jnp.float32)
+        lines = block[:half]
+        at = pl.multiple_of(station * rows, 8)
+        plain_ref[pl.ds(at, half), :] = lines
+        plain_ref[pl.ds(at + half, half), :] = roll_half(lines)
         tail_ref[pl.ds(pl.multiple_of(station * tail_lines, 8), tail_lines), :] = block[half : half + tail_lines]
         return carry
 
-    lax.fori_loop(0, stations, tails, 0, unroll=8)
+    lax.fori_loop(0, stations, expand, 0, unroll=8)
     route_copy.wait()
 
     def move(station, carry):
-        upper = got_ref[station].astype(jnp.float32)[:half]
-        lower = roll_half(upper)
-        for row in range(half):
-            placed_ref[pl.ds(route_smem[station, row], 1), :] = upper[row : row + 1, :]
-        for row in range(half):
-            placed_ref[pl.ds(route_smem[station, half + row], 1), :] = lower[row : row + 1, :]
-        return carry
-
-    lax.fori_loop(0, stations, move, 0, unroll=2)
+        lines = plain_ref[pl.ds(pl.multiple_of(station * rows, 8), rows), :]
+        for row in range(rows):
+            placed_ref[pl.ds(route_smem[station, row], 1), :] = lines[row : row + 1, :]
+        return carry
+
+    lax.fori_loop(0, stations, move, 0)
 
     def join(station, carry):
         at = pl.multiple_of(station * rows, 8)
@@ -309,6 +321,14 @@
     return partial[:half] + lax.ppermute(partial[half:], "stn", pairs)
 
 
+def exchange(partial, bits, count):
+    total = partial[0]
+    for block in range(1, partial.shape[0]):
+        mask = sum(1 << bit for at, bit in enumerate(bits) if block >> (len(bits) - 1 - at) & 1)
+        total = total + lax.ppermute(partial[block], "stn", [(i, i ^ mask) for i in range(count)])
+    return total
+
+
 def owned_entries(slots, template_channels):
     flat = template_channels.reshape(-1)
     count = flat.shape[0]
@@ -320,13 +340,6 @@
     where_to = jnp.where(here > 0, before, count)
     entries = jnp.sum(jnp.where(where_to[None, :] == number[:, None], number[None, :], 0), axis=1)
     return entries, row, jnp.sum(here).reshape(1)
-
-
-def rank_among(slots, rows):
-    target = slots // rows
-    number = jnp.arange(rows, dtype=jnp.int32)
-    same = (target[..., :, None] == target[..., None, :]) & (number[None, :] < number[:, None])
-    return target, jnp.sum(same.astype(jnp.int32), axis=-1)
 
 
 def shards(archive, slot_of_row, templates, template_channels, moveouts, *, sizes):
@@ -342,20 +355,20 @@
     f32, bf16, i32 = jnp.float32, jnp.bfloat16, jnp.int32
     shape = jax.ShapeDtypeStruct
 
-    target, rank = rank_among(slot_of_row, rows)
-    info = jnp.concatenate([target, slot_of_row % rows + rows * rank]).astype(f32)
-    info = jnp.broadcast_to(info[None, :], (8, LANES))
     packed = kernel_call(
         functools.partial(pack_kernel, rows=rows, tiles=tiles, tail_tiles=tail_tiles),
-        (which.reshape(1), target * 2 + rank),
-        (info, archive),
+        (which.reshape(1),),
+        (slot_of_row.reshape(1, rows), archive),
         shape((stations, block_lines, LANES), bf16),
         [
             pltpu.VMEM((rows, (tiles + tail_tiles) * LANES), bf16),
             pltpu.VMEM((stations, block_lines, LANES), bf16),
             pltpu.VMEM((stations * 2 * tail_tiles, LANES), f32),
+            pltpu.VMEM((8, LANES), i32),
+            pltpu.SMEM((8, LANES), i32),
             pltpu.SemaphoreType.DMA((PARTS + 1,)),
             pltpu.SemaphoreType.DMA((PARTS,)),
+            pltpu.SemaphoreType.DMA,
         ],
         4_000_000, 4_000_000, 56, HBM_SPEC, [VMEM_SPEC, HBM_SPEC],
     )
@@ -381,12 +394,9 @@
         ],
         1000, 1000, 28,
     )
-    for bit in bits[:EARLY]:
-        partial = halve(partial, bit, stations)
-    first, _ = lax.optimization_barrier((first, partial))
-    for bit in bits[EARLY:]:
-        partial = halve(partial, bit, stations)
-    stack = partial[0] * math.sqrt(length / channels)
+    partial = halve(partial, bits[0], stations)
+    first, partial = lax.optimization_barrier((first, partial))
+    partial = halve(partial, bits[1], stations)
 
     lines, tail_rows = kernel_call(
         functools.partial(permute_kernel, rows=rows, tail_tiles=tail_tiles),
@@ -395,6 +405,7 @@
         (shape((stations, 2, half, LANES), bf16), shape((rows, tail_tiles * LANES), bf16)),
         [
             pltpu.VMEM((stations, half, LANES), bf16),
+            pltpu.VMEM((stations * rows, LANES), f32),
             pltpu.VMEM((stations * rows, LANES), f32),
             pltpu.VMEM((stations * 2 * tail_tiles, LANES), f32),
             pltpu.VMEM((tail_tiles, rows + 8, LANES), f32),
@@ -406,8 +417,12 @@
         ],
         4_000_000, 30_000_000, 52, (HBM_SPEC, VMEM_SPEC),
     )
+    lines, _ = lax.optimization_barrier((lines, partial))
     lines = lines.reshape(2 * stations, half, LANES)
     second = lax.all_to_all(lines, ("stn", "tpl"), 0, 0, tiled=True)
+    for bit in bits[2:-3]:
+        partial = halve(partial, bit, stations)
+    stack = exchange(partial, bits[-3:], stations) * math.sqrt(length / channels)
     tail_other = lax.ppermute(tail_rows, "tpl", [(0, 1), (1, 0)])
     tail_low = jnp.where(which == 0, tail_rows, tail_other)
     tail_high = jnp.where(which == 0, tail_other, tail_rows)

time: 164 us -> 140 us (0.85)
  waiting for transfers between devices: 81.6 us -> 53.7 us
  starting transfers between devices: 44 us -> 50.6 us
  other arithmetic: 4.67 us -> 2.48 us
    ppermute x7 -> x4, waiting for transfers between devices: 79.2 us -> 21.2 us  [halve(): return partial[:half] + lax.ppermute(partial[half:], 'stn', pairs)]
    all_to_all x1, waiting for transfers between devices: 0.01 us -> 23.1 us  [shards(): first = lax.all_to_all(packed, 'stn', 0, 0, tiled=True)]
    ppermute x0 -> x7, starting transfers between devices: none -> 21.6 us  [exchange(): lax.ppermute(partial[block], 'stn', [(i, i ^ mask) for i in range(count)])]
    ppermute x7 -> x4, starting transfers between devices: 18.7 us -> 7.02 us  [halve(): return partial[:half] + lax.ppermute(partial[half:], 'stn', pairs)]
    ppermute x0 -> x7, waiting for transfers between devices: none -> 9.35 us  [exchange(): lax.ppermute(partial[block], 'stn', [(i, i ^ mask) for i in range(count)])]
    all_to_all x1, starting transfers between devices: 10.3 us -> 7.04 us  [shards(): second = lax.all_to_all(lines, ('stn', 'tpl'), 0, 0, tiled=True)]
    ppermute x1, waiting for transfers between devices: 2.37 us -> 0.01 us  [shards(): tail_other = lax.ppermute(tail_rows, 'tpl', [(0, 1), (1, 0)])]
  transfers between devices with their start and end apart: 10 -> 14, of which waited for: 8 -> 6; matrix products, arithmetic and copies ran while one was open for 2% -> 2% of each run, Pallas kernels for 6% -> 18%
where the time goes in v4:
time: 140 us; the launch traced here: 139 us
  waiting for transfers between devices  53.7 us (38%)
  starting transfers between devices  50.6 us (36%)
  Pallas kernels  31 us (22%)
  other arithmetic  2.48 us (2%)
    pallas_call x4, Pallas kernels, kernel_call(): pl.pallas_call(body, out_shape=outs, in_specs=[SMEM_SPEC] * len(scalars)...  31 us
    all_to_all x1, waiting for transfers between devices, shards(): first = lax.all_to_all(packed, 'stn', 0, 0, tiled=True)  23.1 us
    ppermute x7, starting transfers between devices, exchange(): lax.ppermute(partial[block], 'stn', [(i, i ^ mask) for i in range(count)])  21.6 us
    ppermute x4, waiting for transfers between devices, halve(): return partial[:half] + lax.ppermute(partial[half:], 'stn', pairs)  21.2 us
    all_to_all x1, starting transfers between devices, shards(): first = lax.all_to_all(packed, 'stn', 0, 0, tiled=True)  14.5 us
    ppermute x7, waiting for transfers between devices, exchange(): lax.ppermute(partial[block], 'stn', [(i, i ^ mask) for i in range(count)])  9.35 us
    all_to_all x1, starting transfers between devices, shards(): second = lax.all_to_all(lines, ('stn', 'tpl'), 0, 0, tiled=True)  7.04 us
    ppermute x4, starting transfers between devices, halve(): return partial[:half] + lax.ppermute(partial[half:], 'stn', pairs)  7.02 us
  transfers between devices with their start and end apart: 14, of which 6 were waited for; matrix products, arithmetic and copies ran while one was open for 2% of the time, Pallas kernels for 18%

profile of v4, /device:TPU:16, one launch (start us, length us, event | category | flops | bytes accessed | tf_op | source)
XLA Modules:
  0.0 139.1 jit_solution(14679940998068026455)
XLA Ops:
  0.6 3.5 %shard_map.68 = bf16[128,48,128]{2,1,0:T(8,128)(2,1)} custom-call(s32[1]{0:T(128)} %bitcast.1.half_ref, s32[1,64]{1,0:T(1,128)} %bitcast.47, bf16[64,17408]{1,0:T(8,128)(2,1)} %archive_ref), custom_call_target="tpu_custom_call" | custom-call | flops 4000000 | bytes 4000000 | tf_op jit(solution)/shard_map/pallas_call | solution.py:307
  4.2 14.5 %all-to-all-start = ((bf16[128,48,128]{2,1,0:T(8,128)(2,1)}), bf16[128,48,128]{2,1,0:T(8,128)(2,1)}, u32[]{:S(2)}, u32[]{:S(2)}) async-start(bf16[128,48,128]{2,1,0:T(8,128)(2,1)} %shard_map.68), calls=%async_computation | async-start | bytes 3145728 | tf_op jit(solution)/shard_map/all_to_all | solution.py:376
  18.7 0.1 copy.9
  18.8 0.1 eq.14
  18.9 0.1 copy.10
  19.1 0.8 fusion
  19.9 0.2 select_reduce_fusion.1
  20.1 0.5 select_reduce_fusion.entry_ref
  20.6 12.1 %shard_map.69 = f32[128,32,128]{2,1,0:T(8,128)S(1)} custom-call(s32[1]{0:T(128)} %bitcast.4.count_ref, s32[960]{0:T(1024)S(1)} %select_reduce_fusion.entry_ref, s32[960]{0:T(1024)S(1)} %get-tuple-element.16.row_ref, s32[960]{0:T(1024)S(1)} %reshape.41.shift_ref, s32[1]{0:T(128)} %bitcast.6.place_ref, bf16[64,17408]{1,0:T(8,128)(2,1)S(1)} %copy-done, ...), custom_call_target="tpu_custom_call" | custom-call | flops 1000 | bytes 1000 | tf_op jit(solution)/shard_map/pallas_call | solution.py:307
  32.7 0.1 collective-permute-start
  32.8 2.6 %collective-permute-done = f32[64,32,128]{2,1,0:T(8,128)S(1)} collective-permute-done((f32[64,32,128]{2,1,0:T(8,128)S(1)}, f32[64,32,128]{2,1,0:T(8,128)S(1)}, u32[]{:S(2)}, u32[]{:S(2)}) %collective-permute-start) | collective-permute-done | bytes 1048608 | tf_op jit(solution)/shard_map/ppermute | solution.py:321
  35.5 0.2 slice_add_fusion
  35.7 23.1 %all-to-all-done.got_ref = bf16[128,48,128]{2,1,0:T(8,128)(2,1)} async-done(((bf16[128,48,128]{2,1,0:T(8,128)(2,1)}), bf16[128,48,128]{2,1,0:T(8,128)(2,1)}, u32[]{:S(2)}, u32[]{:S(2)}) %all-to-all-start) | async-done | bytes 1572896 | tf_op jit(solution)/shard_map/all_to_all | solution.py:376
  58.8 2.1 %collective-permute-start.1 = (f32[32,32,128]{2,1,0:T(8,128)S(1)}, f32[32,32,128]{2,1,0:T(8,128)S(1)}, u32[]{:S(2)}, u32[]{:S(2)}) collective-permute-start(f32[32,32,128]{2,1,0:T(8,128)S(1)} %slice.51), channel_id=1, source_target_pairs={{0,128},{2,130},{4,132},{6,134},{8,136},{10,138},{12,140},{14,142}... | collective-permute-start | bytes 1572872 | tf_op jit(solution)/shard_map/ppermute | solution.py:321
  60.9 12.9 %shard_map.70 = (bf16[128,2,32,128]{3,2,1,0:T(8,128)(2,1)}, bf16[64,512]{1,0:T(8,128)(2,1)S(1)}) custom-call(s32[1]{0:T(128)} %bitcast.owner_ref, bf16[128,48,128]{2,1,0:T(8,128)(2,1)} %all-to-all-done.got_ref), custom_call_target="tpu_custom_call" | custom-call | flops 4000000 | bytes 30000000 | tf_op jit(solution)/shard_map/pallas_call | solution.py:307
  73.8 0.1 slice_add_fusion.1
  73.9 7.0 %all-to-all-start.1 = ((bf16[256,32,128]{2,1,0:T(8,128)(2,1)}), bf16[256,32,128]{2,1,0:T(8,128)(2,1)S(1)}, u32[]{:S(2)}, u32[]{:S(2)}) async-start(bf16[256,32,128]{2,1,0:T(8,128)(2,1)} %bitcast.44), calls=%async_computation.1 | async-start | bytes 4194304 | tf_op jit(solution)/shard_map/all_to_all | solution.py:422
  80.9 1.6 %collective-permute-start.3 = (f32[16,32,128]{2,1,0:T(8,128)S(1)}, f32[16,32,128]{2,1,0:T(8,128)S(1)}, u32[]{:S(2)}, u32[]{:S(2)}) collective-permute-start(f32[16,32,128]{2,1,0:T(8,128)S(1)} %slice.67), channel_id=1, source_target_pairs={{0,4},{2,6},{4,0},{6,2},{8,12},{10,14},{12,8},{14,10},{16,20},{18,... | collective-permute-start | bytes 786440 | tf_op jit(solution)/shard_map/ppermute | solution.py:321
  82.5 12.4 %collective-permute-done.3 = f32[16,32,128]{2,1,0:T(8,128)S(1)} collective-permute-done((f32[16,32,128]{2,1,0:T(8,128)S(1)}, f32[16,32,128]{2,1,0:T(8,128)S(1)}, u32[]{:S(2)}, u32[]{:S(2)}) %collective-permute-start.3) | collective-permute-done | bytes 262176 | tf_op jit(solution)/shard_map/ppermute | solution.py:321
  94.9 3.3 %collective-permute-start.4 = (f32[8,32,128]{2,1,0:T(8,128)S(1)}, f32[8,32,128]{2,1,0:T(8,128)S(1)}, u32[]{:S(2)}, u32[]{:S(2)}) collective-permute-start(f32[8,32,128]{2,1,0:T(8,128)S(1)} %slice.69), channel_id=1, source_target_pairs={{0,8},{2,10},{4,12},{6,14},{8,0},{10,2},{12,4},{14,6},{16,24},{18,... | collective-permute-start | bytes 393224 | tf_op jit(solution)/shard_map/ppermute | solution.py:321
  98.3 0.4 collective-permute-start.2
  98.7 6.2 %collective-permute-done.4 = f32[8,32,128]{2,1,0:T(8,128)S(1)} collective-permute-done((f32[8,32,128]{2,1,0:T(8,128)S(1)}, f32[8,32,128]{2,1,0:T(8,128)S(1)}, u32[]{:S(2)}, u32[]{:S(2)}) %collective-permute-start.4) | collective-permute-done | bytes 131104 | tf_op jit(solution)/shard_map/ppermute | solution.py:321
  104.9 4.1 %collective-permute-start.5 = (f32[32,128]{1,0:T(8,128)S(1)}, f32[32,128]{1,0:T(8,128)S(1)}, u32[]{:S(2)}, u32[]{:S(2)}) collective-permute-start(f32[32,128]{1,0:T(8,128)S(1)} %get-tuple-element.19), channel_id=1, source_target_pairs={{0,16},{2,18},{4,20},{6,22},{8,24},{10,26},{12,28},{14,30},{16,0},... | collective-permute-start | bytes 49160 | tf_op jit(solution)/shard_map/ppermute | solution.py:328
  109.0 3.9 %collective-permute-start.11 = (f32[32,128]{1,0:T(8,128)S(1)}, f32[32,128]{1,0:T(8,128)S(1)}, u32[]{:S(2)}, u32[]{:S(2)}) collective-permute-start(f32[32,128]{1,0:T(8,128)S(1)} %get-tuple-element.20), channel_id=1, source_target_pairs={{0,112},{2,114},{4,116},{6,118},{8,120},{10,122},{12,124},{14,126}... | collective-permute-start | bytes 49160 | tf_op jit(solution)/shard_map/ppermute | solution.py:328
  112.8 5.1 %collective-permute-start.9 = (f32[32,128]{1,0:T(8,128)S(1)}, f32[32,128]{1,0:T(8,128)S(1)}, u32[]{:S(2)}, u32[]{:S(2)}) collective-permute-start(f32[32,128]{1,0:T(8,128)S(1)} %get-tuple-element.22), channel_id=1, source_target_pairs={{0,80},{2,82},{4,84},{6,86},{8,88},{10,90},{12,92},{14,94},{16,64}... | collective-permute-start | bytes 49160 | tf_op jit(solution)/shard_map/ppermute | solution.py:328
  117.9 2.3 %collective-permute-start.8 = (f32[32,128]{1,0:T(8,128)S(1)}, f32[32,128]{1,0:T(8,128)S(1)}, u32[]{:S(2)}, u32[]{:S(2)}) collective-permute-start(f32[32,128]{1,0:T(8,128)S(1)} %get-tuple-element.23), channel_id=1, source_target_pairs={{0,64},{2,66},{4,68},{6,70},{8,72},{10,74},{12,76},{14,78},{16,80}... | collective-permute-start | bytes 49160 | tf_op jit(solution)/shard_map/ppermute | solution.py:328
  120.2 7.7 %collective-permute-done.5 = f32[32,128]{1,0:T(8,128)S(1)} collective-permute-done((f32[32,128]{1,0:T(8,128)S(1)}, f32[32,128]{1,0:T(8,128)S(1)}, u32[]{:S(2)}, u32[]{:S(2)}) %collective-permute-start.5) | collective-permute-done | bytes 16416 | tf_op jit(solution)/shard_map/ppermute | solution.py:328
  127.9 2.6 %collective-permute-start.7 = (f32[32,128]{1,0:T(8,128)S(1)}, f32[32,128]{1,0:T(8,128)S(1)}, u32[]{:S(2)}, u32[]{:S(2)}) collective-permute-start(f32[32,128]{1,0:T(8,128)S(1)} %get-tuple-element.24), channel_id=1, source_target_pairs={{0,48},{2,50},{4,52},{6,54},{8,56},{10,58},{12,60},{14,62},{16,32}... | collective-permute-start | bytes 49160 | tf_op jit(solution)/shard_map/ppermute | solution.py:328
  130.5 3.7 %collective-permute-start.6 = (f32[32,128]{1,0:T(8,128)S(1)}, f32[32,128]{1,0:T(8,128)S(1)}, u32[]{:S(2)}, u32[]{:S(2)}) collective-permute-start(f32[32,128]{1,0:T(8,128)S(1)} %get-tuple-element.25), channel_id=1, source_target_pairs={{0,32},{2,34},{4,36},{6,38},{8,40},{10,42},{12,44},{14,46},{16,48}... | collective-permute-start | bytes 49160 | tf_op jit(solution)/shard_map/ppermute | solution.py:328
  134.2 1.7 %collective-permute-done.6 = f32[32,128]{1,0:T(8,128)S(1)} collective-permute-done((f32[32,128]{1,0:T(8,128)S(1)}, f32[32,128]{1,0:T(8,128)S(1)}, u32[]{:S(2)}, u32[]{:S(2)}) %collective-permute-start.6) | collective-permute-done | bytes 16416 | tf_op jit(solution)/shard_map/ppermute | solution.py:328
  135.9 0.6 fusion.8
  136.5 2.5 %shard_map.71 = bf16[64,17408]{1,0:T(8,128)(2,1)} custom-call(bf16[256,32,128]{2,1,0:T(8,128)(2,1)S(1)} %all-to-all-done.1.got_ref, bf16[64,512]{1,0:T(8,128)(2,1)S(1)} %get-tuple-element.27.tail_low_ref, bf16[64,512]{1,0:T(8,128)(2,1)S(1)} %get-tuple-element.26.tail_high_ref), custom_call_target="tpu_custom_call" | custom-call | flops 4000000 | bytes 6000000 | tf_op jit(solution)/shard_map/pallas_call | solution.py:307
  (29 shorter events, 0.4 us)
Async XLA Ops:
  0.6 19.9 %copy-start.1 = (bf16[32,30,600]{2,0,1:T(8,128)(2,1)S(1)}, bf16[32,30,600]{2,0,1:T(8,128)(2,1)}, u32[]{:S(2)}) copy-start(bf16[32,30,600]{2,0,1:T(8,128)(2,1)} %param.7) | copy-start | bytes 3456004
  4.2 14.6 %copy-start.2 = (s32[32,30]{1,0:T(8,128)S(1)}, s32[32,30]{1,0:T(8,128)}, u32[]{:S(2)}) copy-start(s32[32,30]{1,0:T(8,128)} %param.8) | copy-start | bytes 11524
  4.2 14.7 %copy-start.3 = (s32[32,30]{1,0:T(8,128)S(1)}, s32[32,30]{1,0:T(8,128)}, u32[]{:S(2)}) copy-start(s32[32,30]{1,0:T(8,128)} %param.9) | copy-start | bytes 11524
  4.2 14.9 %copy-start.4 = (s32[64]{0:T(128)S(1)}, s32[64]{0:T(128)}, u32[]{:S(2)}) copy-start(s32[64]{0:T(128)} %param.6) | copy-start | bytes 772
  4.2 16.4 %copy-start = (bf16[64,17408]{1,0:T(8,128)(2,1)S(1)}, bf16[64,17408]{1,0:T(8,128)(2,1)}, u32[]{:S(2)}) copy-start(bf16[64,17408]{1,0:T(8,128)(2,1)} %archive_ref) | copy-start | bytes 6684676
  4.2 54.6 %all-to-all-start = ((bf16[128,48,128]{2,1,0:T(8,128)(2,1)}), bf16[128,48,128]{2,1,0:T(8,128)(2,1)}, u32[]{:S(2)}, u32[]{:S(2)}) async-start(bf16[128,48,128]{2,1,0:T(8,128)(2,1)} %shard_map.68), calls=%async_computation | async-start | bytes 3145728 | tf_op jit(solution)/shard_map/all_to_all | solution.py:376
  32.7 2.7 %collective-permute-start = (f32[64,32,128]{2,1,0:T(8,128)S(1)}, f32[64,32,128]{2,1,0:T(8,128)S(1)}, u32[]{:S(2)}, u32[]{:S(2)}) collective-permute-start(f32[64,32,128]{2,1,0:T(8,128)S(1)} %slice.65), channel_id=1, source_target_pairs={{0,2},{2,0},{4,6},{6,4},{8,10},{10,8},{12,14},{14,12},{16,18},{18,... | collective-permute-start | bytes 3145736 | tf_op jit(solution)/shard_map/ppermute | solution.py:321
  58.8 14.9 %collective-permute-start.1 = (f32[32,32,128]{2,1,0:T(8,128)S(1)}, f32[32,32,128]{2,1,0:T(8,128)S(1)}, u32[]{:S(2)}, u32[]{:S(2)}) collective-permute-start(f32[32,32,128]{2,1,0:T(8,128)S(1)} %slice.51), channel_id=1, source_target_pairs={{0,128},{2,130},{4,132},{6,134},{8,136},{10,138},{12,140},{14,142}... | collective-permute-start | bytes 1572872 | tf_op jit(solution)/shard_map/ppermute | solution.py:321
  73.9 62.7 %all-to-all-start.1 = ((bf16[256,32,128]{2,1,0:T(8,128)(2,1)}), bf16[256,32,128]{2,1,0:T(8,128)(2,1)S(1)}, u32[]{:S(2)}, u32[]{:S(2)}) async-start(bf16[256,32,128]{2,1,0:T(8,128)(2,1)} %bitcast.44), calls=%async_computation.1 | async-start | bytes 4194304 | tf_op jit(solution)/shard_map/all_to_all | solution.py:422
  80.9 13.9 %collective-permute-start.3 = (f32[16,32,128]{2,1,0:T(8,128)S(1)}, f32[16,32,128]{2,1,0:T(8,128)S(1)}, u32[]{:S(2)}, u32[]{:S(2)}) collective-permute-start(f32[16,32,128]{2,1,0:T(8,128)S(1)} %slice.67), channel_id=1, source_target_pairs={{0,4},{2,6},{4,0},{6,2},{8,12},{10,14},{12,8},{14,10},{16,20},{18,... | collective-permute-start | bytes 786440 | tf_op jit(solution)/shard_map/ppermute | solution.py:321
  94.9 9.9 %collective-permute-start.4 = (f32[8,32,128]{2,1,0:T(8,128)S(1)}, f32[8,32,128]{2,1,0:T(8,128)S(1)}, u32[]{:S(2)}, u32[]{:S(2)}) collective-permute-start(f32[8,32,128]{2,1,0:T(8,128)S(1)} %slice.69), channel_id=1, source_target_pairs={{0,8},{2,10},{4,12},{6,14},{8,0},{10,2},{12,4},{14,6},{16,24},{18,... | collective-permute-start | bytes 393224 | tf_op jit(solution)/shard_map/ppermute | solution.py:321
  98.3 19.7 %collective-permute-start.2 = (bf16[64,512]{1,0:T(8,128)(2,1)S(1)}, bf16[64,512]{1,0:T(8,128)(2,1)S(1)}, u32[]{:S(2)}, u32[]{:S(2)}) collective-permute-start(bf16[64,512]{1,0:T(8,128)(2,1)S(1)} %get-tuple-element.15), channel_id=1, source_target_pairs={{0,1},{1,0},{2,3},{3,2},{4,5},{5,4},{6,7},{7,6},{8,9},{9,8},{10,11... | collective-permute-start | bytes 196616 | tf_op jit(solution)/shard_map/ppermute | solution.py:426
  104.9 23.0 %collective-permute-start.5 = (f32[32,128]{1,0:T(8,128)S(1)}, f32[32,128]{1,0:T(8,128)S(1)}, u32[]{:S(2)}, u32[]{:S(2)}) collective-permute-start(f32[32,128]{1,0:T(8,128)S(1)} %get-tuple-element.19), channel_id=1, source_target_pairs={{0,16},{2,18},{4,20},{6,22},{8,24},{10,26},{12,28},{14,30},{16,0},... | collective-permute-start | bytes 49160 | tf_op jit(solution)/shard_map/ppermute | solution.py:328
  109.0 21.5 %collective-permute-start.11 = (f32[32,128]{1,0:T(8,128)S(1)}, f32[32,128]{1,0:T(8,128)S(1)}, u32[]{:S(2)}, u32[]{:S(2)}) collective-permute-start(f32[32,128]{1,0:T(8,128)S(1)} %get-tuple-element.20), channel_id=1, source_target_pairs={{0,112},{2,114},{4,116},{6,118},{8,120},{10,122},{12,124},{14,126}... | collective-permute-start | bytes 49160 | tf_op jit(solution)/shard_map/ppermute | solution.py:328
  112.8 21.4 %collective-permute-start.10 = (f32[32,128]{1,0:T(8,128)S(1)}, f32[32,128]{1,0:T(8,128)S(1)}, u32[]{:S(2)}, u32[]{:S(2)}) collective-permute-start(f32[32,128]{1,0:T(8,128)S(1)} %get-tuple-element.21), channel_id=1, source_target_pairs={{0,96},{2,98},{4,100},{6,102},{8,104},{10,106},{12,108},{14,110},{... | collective-permute-start | bytes 49160 | tf_op jit(solution)/shard_map/ppermute | solution.py:328
  112.8 21.4 %collective-permute-start.9 = (f32[32,128]{1,0:T(8,128)S(1)}, f32[32,128]{1,0:T(8,128)S(1)}, u32[]{:S(2)}, u32[]{:S(2)}) collective-permute-start(f32[32,128]{1,0:T(8,128)S(1)} %get-tuple-element.22), channel_id=1, source_target_pairs={{0,80},{2,82},{4,84},{6,86},{8,88},{10,90},{12,92},{14,94},{16,64}... | collective-permute-start | bytes 49160 | tf_op jit(solution)/shard_map/ppermute | solution.py:328
  117.9 16.3 %collective-permute-start.8 = (f32[32,128]{1,0:T(8,128)S(1)}, f32[32,128]{1,0:T(8,128)S(1)}, u32[]{:S(2)}, u32[]{:S(2)}) collective-permute-start(f32[32,128]{1,0:T(8,128)S(1)} %get-tuple-element.23), channel_id=1, source_target_pairs={{0,64},{2,66},{4,68},{6,70},{8,72},{10,74},{12,76},{14,78},{16,80}... | collective-permute-start | bytes 49160 | tf_op jit(solution)/shard_map/ppermute | solution.py:328
  127.9 6.4 %collective-permute-start.7 = (f32[32,128]{1,0:T(8,128)S(1)}, f32[32,128]{1,0:T(8,128)S(1)}, u32[]{:S(2)}, u32[]{:S(2)}) collective-permute-start(f32[32,128]{1,0:T(8,128)S(1)} %get-tuple-element.24), channel_id=1, source_target_pairs={{0,48},{2,50},{4,52},{6,54},{8,56},{10,58},{12,60},{14,62},{16,32}... | collective-permute-start | bytes 49160 | tf_op jit(solution)/shard_map/ppermute | solution.py:328
  130.5 5.4 %collective-permute-start.6 = (f32[32,128]{1,0:T(8,128)S(1)}, f32[32,128]{1,0:T(8,128)S(1)}, u32[]{:S(2)}, u32[]{:S(2)}) collective-permute-start(f32[32,128]{1,0:T(8,128)S(1)} %get-tuple-element.25), channel_id=1, source_target_pairs={{0,32},{2,34},{4,36},{6,38},{8,40},{10,42},{12,44},{14,46},{16,48}... | collective-permute-start | bytes 49160 | tf_op jit(solution)/shard_map/ppermute | solution.py:328

commit v5 on v4

--- a/solution.py
+++ b/solution.py
@@ -15,6 +15,7 @@
 MIB = 1024 * 1024
 PARTS = 4
 GROUP = 16
+EARLY = 2
 
 
 def roll_half(x):
@@ -98,7 +99,7 @@
 
 def permute_kernel(
     owner_ref, got_ref, out_hbm, tail_out_ref,
-    out_ref, plain_ref, placed_ref, tail_ref, tail_rows_ref, info_ref, route_ref, route_smem, route_sem, sems,
+    out_ref, plain_ref, placed_ref, tail_ref, tail_rows_ref, info_ref, route_ref, route_smem, route_sems, sems,
     *, rows, tail_tiles,
 ):
     stations = got_ref.shape[0]
@@ -126,8 +127,8 @@
     kept = jnp.where(lane == rows, first, second)
     kept = jnp.where(kept < 0, rows, kept)
     route_ref[...] = jnp.where(on_left, target * rows + place, kept)
-    route_copy = pltpu.make_async_copy(route_ref, route_smem, route_sem)
-    route_copy.start()
+    share = stations // PARTS
+    route_copies = [send_part(route_ref, route_smem, part, share, route_sems.at[part]) for part in range(PARTS)]
 
     def expand(station, carry):
         block = got_ref[station].astype(jnp.float32)
@@ -139,7 +140,6 @@
         return carry
 
     lax.fori_loop(0, stations, expand, 0, unroll=8)
-    route_copy.wait()
 
     def move(station, carry):
         lines = plain_ref[pl.ds(pl.multiple_of(station * rows, 8), rows), :]
@@ -147,7 +147,9 @@
             placed_ref[pl.ds(route_smem[station, row], 1), :] = lines[row : row + 1, :]
         return carry
 
-    lax.fori_loop(0, stations, move, 0)
+    for part in range(PARTS):
+        route_copies[part].wait()
+        lax.fori_loop(part * share, (part + 1) * share, move, 0, unroll=4)
 
     def join(station, carry):
         at = pl.multiple_of(station * rows, 8)
@@ -157,7 +159,7 @@
 
     copies = []
     for part in range(PARTS):
-        lax.fori_loop(part * stations // PARTS, (part + 1) * stations // PARTS, join, 0, unroll=8)
+        lax.fori_loop(part * stations // PARTS, (part + 1) * stations // PARTS, join, 0, unroll=16)
         for which in range(2):
             copies.append(
                 send_part(out_ref, out_hbm.at[:, which], part, stations // PARTS, sems.at[which, part])
@@ -322,10 +324,12 @@
 
 
 def exchange(partial, bits, count):
+    parts = 1 << len(bits)
+    partial = partial.reshape((parts, partial.shape[0] // parts) + partial.shape[1:])
     total = partial[0]
-    for block in range(1, partial.shape[0]):
-        mask = sum(1 << bit for at, bit in enumerate(bits) if block >> (len(bits) - 1 - at) & 1)
-        total = total + lax.ppermute(partial[block], "stn", [(i, i ^ mask) for i in range(count)])
+    for part in range(1, parts):
+        mask = sum(1 << bit for at, bit in enumerate(bits) if part >> (len(bits) - 1 - at) & 1)
+        total = total + lax.ppermute(partial[part], "stn", [(i, i ^ mask) for i in range(count)])
     return total
 
 
@@ -394,9 +398,9 @@
         ],
         1000, 1000, 28,
     )
-    partial = halve(partial, bits[0], stations)
-    first, partial = lax.optimization_barrier((first, partial))
-    partial = halve(partial, bits[1], stations)
+    for bit in bits[:EARLY]:
+        partial = halve(partial, bit, stations)
+    first, _ = lax.optimization_barrier((first, partial))
 
     lines, tail_rows = kernel_call(
         functools.partial(permute_kernel, rows=rows, tail_tiles=tail_tiles),
@@ -412,17 +416,16 @@
             pltpu.VMEM((stations, LANES), f32),
             pltpu.VMEM((stations, LANES), i32),
             pltpu.SMEM((stations, LANES), i32),
-            pltpu.SemaphoreType.DMA,
+            pltpu.SemaphoreType.DMA((PARTS,)),
             pltpu.SemaphoreType.DMA((2, PARTS)),
         ],
         4_000_000, 30_000_000, 52, (HBM_SPEC, VMEM_SPEC),
     )
-    lines, _ = lax.optimization_barrier((lines, partial))
     lines = lines.reshape(2 * stations, half, LANES)
     second = lax.all_to_all(lines, ("stn", "tpl"), 0, 0, tiled=True)
-    for bit in bits[2:-3]:
-        partial = halve(partial, bit, stations)
-    stack = exchange(partial, bits[-3:], stations) * math.sqrt(length / channels)
+    for part in bits[EARLY:-3], bits[-3:]:
+        partial = exchange(partial, part, stations)
+    stack = partial[0] * math.sqrt(length / channels)
     tail_other = lax.ppermute(tail_rows, "tpl", [(0, 1), (1, 0)])
     tail_low = jnp.where(which == 0, tail_rows, tail_other)
     tail_high = jnp.where(which == 0, tail_other, tail_rows)

time: 140 us -> 144 us (1.029); the launches traced: 139 us -> 145 us
  starting transfers between devices: 50.6 us -> 57.1 us
  Pallas kernels: 31 us -> 26.8 us
  waiting for transfers between devices: 53.7 us -> 57.1 us
    all_to_all x1, waiting for transfers between devices: 23.1 us -> 1.95 us  [shards(): first = lax.all_to_all(packed, 'stn', 0, 0, tiled=True)]
    ppermute x7 -> x10, waiting for transfers between devices: 9.35 us -> 28.6 us  [exchange(): lax.ppermute(partial[part], 'stn', [(i, i ^ mask) for i in range(count)])]
    all_to_all x1, starting transfers between devices: 7.04 us -> 12.9 us  [shards(): second = lax.all_to_all(lines, ('stn', 'tpl'), 0, 0, tiled=True)]
    ppermute x7 -> x10, starting transfers between devices: 21.6 us -> 25.8 us  [exchange(): lax.ppermute(partial[part], 'stn', [(i, i ^ mask) for i in range(count)])]
    pallas_call x4, Pallas kernels: 31 us -> 26.8 us  [kernel_call(): pl.pallas_call(body, out_shape=outs, in_specs=[SMEM_SPEC] * len(scalars)...]
    ppermute x4 -> x2, starting transfers between devices: 7.02 us -> 3.54 us  [halve(): return partial[:half] + lax.ppermute(partial[half:], 'stn', pairs)]
    ppermute x1, waiting for transfers between devices: 0.01 us -> 3.44 us  [shards(): tail_other = lax.ppermute(tail_rows, 'tpl', [(0, 1), (1, 0)])]
    ppermute x4 -> x2, waiting for transfers between devices: 21.2 us -> 23.1 us  [halve(): return partial[:half] + lax.ppermute(partial[half:], 'stn', pairs)]
  transfers between devices with their start and end apart: 14 -> 15, of which waited for: 6 -> 8; matrix products, arithmetic and copies ran while one was open for 2% -> 2% of each run, Pallas kernels for 18% -> 6%
where the time goes in v5:
time: 144 us; the launch traced here: 145 us
  starting transfers between devices  57.1 us (40%)
  waiting for transfers between devices  57.1 us (40%)
  Pallas kernels  26.8 us (19%)
  other arithmetic  2.51 us (2%)
    ppermute x10, waiting for transfers between devices, exchange(): lax.ppermute(partial[part], 'stn', [(i, i ^ mask) for i in range(count)])  28.6 us
    pallas_call x4, Pallas kernels, kernel_call(): pl.pallas_call(body, out_shape=outs, in_specs=[SMEM_SPEC] * len(scalars)...  26.8 us
    ppermute x10, starting transfers between devices, exchange(): lax.ppermute(partial[part], 'stn', [(i, i ^ mask) for i in range(count)])  25.8 us
    ppermute x2, waiting for transfers between devices, halve(): return partial[:half] + lax.ppermute(partial[half:], 'stn', pairs)  23.1 us
    all_to_all x1, starting transfers between devices, shards(): first = lax.all_to_all(packed, 'stn', 0, 0, tiled=True)  14.5 us
    all_to_all x1, starting transfers between devices, shards(): second = lax.all_to_all(lines, ('stn', 'tpl'), 0, 0, tiled=True)  12.9 us
    ppermute x2, starting transfers between devices, halve(): return partial[:half] + lax.ppermute(partial[half:], 'stn', pairs)  3.54 us
    ppermute x1, waiting for transfers between devices, shards(): tail_other = lax.ppermute(tail_rows, 'tpl', [(0, 1), (1, 0)])  3.44 us
  transfers between devices with their start and end apart: 15, of which 8 were waited for; matrix products, arithmetic and copies ran while one was open for 2% of the time, Pallas kernels for 6%

profile of v5, /device:TPU:16, one launch (start us, length us, event | category | flops | bytes accessed | tf_op | source)
XLA Modules:
  0.0 145.0 jit_solution(10615567821450896449)
XLA Ops:
  0.6 3.5 %shard_map.68 = bf16[128,48,128]{2,1,0:T(8,128)(2,1)} custom-call(s32[1]{0:T(128)} %bitcast.1.half_ref, s32[1,64]{1,0:T(1,128)} %bitcast.17, bf16[64,17408]{1,0:T(8,128)(2,1)} %archive_ref), custom_call_target="tpu_custom_call" | custom-call | flops 4000000 | bytes 4000000 | tf_op jit(solution)/shard_map/pallas_call | solution.py:309
  4.2 14.5 %all-to-all-start = ((bf16[128,48,128]{2,1,0:T(8,128)(2,1)}), bf16[128,48,128]{2,1,0:T(8,128)(2,1)}, u32[]{:S(2)}, u32[]{:S(2)}) async-start(bf16[128,48,128]{2,1,0:T(8,128)(2,1)} %shard_map.68), calls=%async_computation | async-start | bytes 3145728 | tf_op jit(solution)/shard_map/all_to_all | solution.py:380
  18.7 0.1 copy.9
  19.1 0.9 fusion
  19.9 0.2 select_reduce_fusion.1
  20.1 0.5 select_reduce_fusion.entry_ref
  20.6 9.2 %shard_map.69 = f32[128,32,128]{2,1,0:T(8,128)S(1)} custom-call(s32[1]{0:T(128)} %bitcast.4.count_ref, s32[960]{0:T(1024)S(1)} %select_reduce_fusion.entry_ref, s32[960]{0:T(1024)S(1)} %get-tuple-element.12.row_ref, s32[960]{0:T(1024)S(1)} %reshape.69.shift_ref, s32[1]{0:T(128)} %bitcast.6.place_ref, bf16[64,17408]{1,0:T(8,128)(2,1)S(1)} %copy-done, ...), custom_call_target="tpu_custom_call" | custom-call | flops 1000 | bytes 1000 | tf_op jit(solution)/shard_map/pallas_call | solution.py:309
  29.9 0.1 collective-permute-start
  30.0 2.6 %collective-permute-done = f32[64,32,128]{2,1,0:T(8,128)S(1)} collective-permute-done((f32[64,32,128]{2,1,0:T(8,128)S(1)}, f32[64,32,128]{2,1,0:T(8,128)S(1)}, u32[]{:S(2)}, u32[]{:S(2)}) %collective-permute-start) | collective-permute-done | bytes 1048608 | tf_op jit(solution)/shard_map/ppermute | solution.py:323
  32.6 0.2 slice_add_fusion
  32.9 3.4 %collective-permute-start.1 = (f32[32,32,128]{2,1,0:T(8,128)S(1)}, f32[32,32,128]{2,1,0:T(8,128)S(1)}, u32[]{:S(2)}, u32[]{:S(2)}) collective-permute-start(f32[32,32,128]{2,1,0:T(8,128)S(1)} %slice.79), channel_id=1, source_target_pairs={{0,128},{2,130},{4,132},{6,134},{8,136},{10,138},{12,140},{14,142}... | collective-permute-start | bytes 1572872 | tf_op jit(solution)/shard_map/ppermute | solution.py:323
  36.3 20.4 %collective-permute-done.1 = f32[32,32,128]{2,1,0:T(8,128)S(1)} collective-permute-done((f32[32,32,128]{2,1,0:T(8,128)S(1)}, f32[32,32,128]{2,1,0:T(8,128)S(1)}, u32[]{:S(2)}, u32[]{:S(2)}) %collective-permute-start.1) | collective-permute-done | bytes 524320 | tf_op jit(solution)/shard_map/ppermute | solution.py:323
  56.7 0.1 slice_add_fusion.1
  56.8 2.0 %all-to-all-done.got_ref = bf16[128,48,128]{2,1,0:T(8,128)(2,1)} async-done(((bf16[128,48,128]{2,1,0:T(8,128)(2,1)}), bf16[128,48,128]{2,1,0:T(8,128)(2,1)}, u32[]{:S(2)}, u32[]{:S(2)}) %all-to-all-start) | async-done | bytes 1572896 | tf_op jit(solution)/shard_map/all_to_all | solution.py:380
  58.8 11.6 %shard_map.70 = (bf16[128,2,32,128]{3,2,1,0:T(8,128)(2,1)}, bf16[64,512]{1,0:T(8,128)(2,1)S(1)}) custom-call(s32[1]{0:T(128)} %bitcast.owner_ref, bf16[128,48,128]{2,1,0:T(8,128)(2,1)} %all-to-all-done.got_ref), custom_call_target="tpu_custom_call" | custom-call | flops 4000000 | bytes 30000000 | tf_op jit(solution)/shard_map/pallas_call | solution.py:309
  70.4 12.9 %all-to-all-start.1 = ((bf16[256,32,128]{2,1,0:T(8,128)(2,1)}), bf16[256,32,128]{2,1,0:T(8,128)(2,1)S(1)}, u32[]{:S(2)}, u32[]{:S(2)}) async-start(bf16[256,32,128]{2,1,0:T(8,128)(2,1)} %bitcast.14), calls=%async_computation.1 | async-start | bytes 4194304 | tf_op jit(solution)/shard_map/all_to_all | solution.py:425
  83.3 3.1 %collective-permute-start.3 = (f32[8,32,128]{2,1,0:T(8,128)S(1)}, f32[8,32,128]{2,1,0:T(8,128)S(1)}, u32[]{:S(2)}, u32[]{:S(2)}) collective-permute-start(f32[8,32,128]{2,1,0:T(8,128)S(1)} %get-tuple-element.15), channel_id=1, source_target_pairs={{0,8},{2,10},{4,12},{6,14},{8,0},{10,2},{12,4},{14,6},{16,24},{18,... | collective-permute-start | bytes 393224 | tf_op jit(solution)/shard_map/ppermute | solution.py:332
  86.4 1.2 collective-permute-start.5
  87.5 6.9 %collective-permute-done.3 = f32[8,32,128]{2,1,0:T(8,128)S(1)} collective-permute-done((f32[8,32,128]{2,1,0:T(8,128)S(1)}, f32[8,32,128]{2,1,0:T(8,128)S(1)}, u32[]{:S(2)}, u32[]{:S(2)}) %collective-permute-start.3) | collective-permute-done | bytes 131104 | tf_op jit(solution)/shard_map/ppermute | solution.py:332
  94.5 5.2 %collective-permute-done.5 = f32[8,32,128]{2,1,0:T(8,128)S(1)} collective-permute-done((f32[8,32,128]{2,1,0:T(8,128)S(1)}, f32[8,32,128]{2,1,0:T(8,128)S(1)}, u32[]{:S(2)}, u32[]{:S(2)}) %collective-permute-start.5) | collective-permute-done | bytes 131104 | tf_op jit(solution)/shard_map/ppermute | solution.py:332
  99.7 3.1 %collective-permute-start.6 = (f32[1,32,128]{2,1,0:T(8,128)S(1)}, f32[1,32,128]{2,1,0:T(8,128)S(1)}, u32[]{:S(2)}, u32[]{:S(2)}) collective-permute-start(f32[1,32,128]{2,1,0:T(8,128)S(1)} %get-tuple-element.18), channel_id=1, source_target_pairs={{0,16},{2,18},{4,20},{6,22},{8,24},{10,26},{12,28},{14,30},{16,0},... | collective-permute-start | bytes 49160 | tf_op jit(solution)/shard_map/ppermute | solution.py:332
  102.8 4.0 %collective-permute-start.12 = (f32[1,32,128]{2,1,0:T(8,128)S(1)}, f32[1,32,128]{2,1,0:T(8,128)S(1)}, u32[]{:S(2)}, u32[]{:S(2)}) collective-permute-start(f32[1,32,128]{2,1,0:T(8,128)S(1)} %get-tuple-element.19), channel_id=1, source_target_pairs={{0,112},{2,114},{4,116},{6,118},{8,120},{10,122},{12,124},{14,126}... | collective-permute-start | bytes 49160 | tf_op jit(solution)/shard_map/ppermute | solution.py:332
  106.8 6.0 %collective-permute-start.10 = (f32[1,32,128]{2,1,0:T(8,128)S(1)}, f32[1,32,128]{2,1,0:T(8,128)S(1)}, u32[]{:S(2)}, u32[]{:S(2)}) collective-permute-start(f32[1,32,128]{2,1,0:T(8,128)S(1)} %get-tuple-element.21), channel_id=1, source_target_pairs={{0,80},{2,82},{4,84},{6,86},{8,88},{10,90},{12,92},{14,94},{16,64}... | collective-permute-start | bytes 49160 | tf_op jit(solution)/shard_map/ppermute | solution.py:332
  112.7 2.3 %collective-permute-start.9 = (f32[1,32,128]{2,1,0:T(8,128)S(1)}, f32[1,32,128]{2,1,0:T(8,128)S(1)}, u32[]{:S(2)}, u32[]{:S(2)}) collective-permute-start(f32[1,32,128]{2,1,0:T(8,128)S(1)} %get-tuple-element.22), channel_id=1, source_target_pairs={{0,64},{2,66},{4,68},{6,70},{8,72},{10,74},{12,76},{14,78},{16,80}... | collective-permute-start | bytes 49160 | tf_op jit(solution)/shard_map/ppermute | solution.py:332
  115.0 15.3 %collective-permute-done.6 = f32[1,32,128]{2,1,0:T(8,128)S(1)} collective-permute-done((f32[1,32,128]{2,1,0:T(8,128)S(1)}, f32[1,32,128]{2,1,0:T(8,128)S(1)}, u32[]{:S(2)}, u32[]{:S(2)}) %collective-permute-start.6) | collective-permute-done | bytes 16416 | tf_op jit(solution)/shard_map/ppermute | solution.py:332
  130.2 2.6 %collective-permute-start.8 = (f32[1,32,128]{2,1,0:T(8,128)S(1)}, f32[1,32,128]{2,1,0:T(8,128)S(1)}, u32[]{:S(2)}, u32[]{:S(2)}) collective-permute-start(f32[1,32,128]{2,1,0:T(8,128)S(1)} %get-tuple-element.23), channel_id=1, source_target_pairs={{0,48},{2,50},{4,52},{6,54},{8,56},{10,58},{12,60},{14,62},{16,32}... | collective-permute-start | bytes 49160 | tf_op jit(solution)/shard_map/ppermute | solution.py:332
  132.9 3.7 %collective-permute-start.7 = (f32[1,32,128]{2,1,0:T(8,128)S(1)}, f32[1,32,128]{2,1,0:T(8,128)S(1)}, u32[]{:S(2)}, u32[]{:S(2)}) collective-permute-start(f32[1,32,128]{2,1,0:T(8,128)S(1)} %get-tuple-element.24), channel_id=1, source_target_pairs={{0,32},{2,34},{4,36},{6,38},{8,40},{10,42},{12,44},{14,46},{16,48}... | collective-permute-start | bytes 49160 | tf_op jit(solution)/shard_map/ppermute | solution.py:332
  136.6 0.4 collective-permute-start.2
  137.0 1.3 collective-permute-done.7
  138.3 0.6 fusion.10
  138.9 3.4 %collective-permute-done.2 = bf16[64,512]{1,0:T(8,128)(2,1)S(1)} collective-permute-done((bf16[64,512]{1,0:T(8,128)(2,1)S(1)}, bf16[64,512]{1,0:T(8,128)(2,1)S(1)}, u32[]{:S(2)}, u32[]{:S(2)}) %collective-permute-start.2) | collective-permute-done | bytes 65568 | tf_op jit(solution)/shard_map/ppermute | solution.py:429
  142.4 2.5 %shard_map.71 = bf16[64,17408]{1,0:T(8,128)(2,1)} custom-call(bf16[256,32,128]{2,1,0:T(8,128)(2,1)S(1)} %all-to-all-done.1.got_ref, bf16[64,512]{1,0:T(8,128)(2,1)S(1)} %get-tuple-element.26.tail_low_ref, bf16[64,512]{1,0:T(8,128)(2,1)S(1)} %get-tuple-element.25.tail_high_ref), custom_call_target="tpu_custom_call" | custom-call | flops 4000000 | bytes 6000000 | tf_op jit(solution)/shard_map/pallas_call | solution.py:309
  (29 shorter events, 0.5 us)
Async XLA Ops:
  0.6 20.0 %copy-start.1 = (bf16[32,30,600]{2,0,1:T(8,128)(2,1)S(1)}, bf16[32,30,600]{2,0,1:T(8,128)(2,1)}, u32[]{:S(2)}) copy-start(bf16[32,30,600]{2,0,1:T(8,128)(2,1)} %param.7) | copy-start | bytes 3456004
  4.2 14.6 %copy-start.2 = (s32[32,30]{1,0:T(8,128)S(1)}, s32[32,30]{1,0:T(8,128)}, u32[]{:S(2)}) copy-start(s32[32,30]{1,0:T(8,128)} %param.8) | copy-start | bytes 11524
  4.2 14.7 %copy-start.3 = (s32[32,30]{1,0:T(8,128)S(1)}, s32[32,30]{1,0:T(8,128)}, u32[]{:S(2)}) copy-start(s32[32,30]{1,0:T(8,128)} %param.9) | copy-start | bytes 11524
  4.2 14.9 %copy-start.4 = (s32[64]{0:T(128)S(1)}, s32[64]{0:T(128)}, u32[]{:S(2)}) copy-start(s32[64]{0:T(128)} %param.6) | copy-start | bytes 772
  4.2 16.4 %copy-start = (bf16[64,17408]{1,0:T(8,128)(2,1)S(1)}, bf16[64,17408]{1,0:T(8,128)(2,1)}, u32[]{:S(2)}) copy-start(bf16[64,17408]{1,0:T(8,128)(2,1)} %archive_ref) | copy-start | bytes 6684676
  4.2 54.6 %all-to-all-start = ((bf16[128,48,128]{2,1,0:T(8,128)(2,1)}), bf16[128,48,128]{2,1,0:T(8,128)(2,1)}, u32[]{:S(2)}, u32[]{:S(2)}) async-start(bf16[128,48,128]{2,1,0:T(8,128)(2,1)} %shard_map.68), calls=%async_computation | async-start | bytes 3145728 | tf_op jit(solution)/shard_map/all_to_all | solution.py:380
  29.9 2.7 %collective-permute-start = (f32[64,32,128]{2,1,0:T(8,128)S(1)}, f32[64,32,128]{2,1,0:T(8,128)S(1)}, u32[]{:S(2)}, u32[]{:S(2)}) collective-permute-start(f32[64,32,128]{2,1,0:T(8,128)S(1)} %slice.77), channel_id=1, source_target_pairs={{0,2},{2,0},{4,6},{6,4},{8,10},{10,8},{12,14},{14,12},{16,18},{18,... | collective-permute-start | bytes 3145736 | tf_op jit(solution)/shard_map/ppermute | solution.py:323
  32.9 23.9 %collective-permute-start.1 = (f32[32,32,128]{2,1,0:T(8,128)S(1)}, f32[32,32,128]{2,1,0:T(8,128)S(1)}, u32[]{:S(2)}, u32[]{:S(2)}) collective-permute-start(f32[32,32,128]{2,1,0:T(8,128)S(1)} %slice.79), channel_id=1, source_target_pairs={{0,128},{2,130},{4,132},{6,134},{8,136},{10,138},{12,140},{14,142}... | collective-permute-start | bytes 1572872 | tf_op jit(solution)/shard_map/ppermute | solution.py:323
  70.4 72.0 %all-to-all-start.1 = ((bf16[256,32,128]{2,1,0:T(8,128)(2,1)}), bf16[256,32,128]{2,1,0:T(8,128)(2,1)S(1)}, u32[]{:S(2)}, u32[]{:S(2)}) async-start(bf16[256,32,128]{2,1,0:T(8,128)(2,1)} %bitcast.14), calls=%async_computation.1 | async-start | bytes 4194304 | tf_op jit(solution)/shard_map/all_to_all | solution.py:425
  83.3 11.2 %collective-permute-start.3 = (f32[8,32,128]{2,1,0:T(8,128)S(1)}, f32[8,32,128]{2,1,0:T(8,128)S(1)}, u32[]{:S(2)}, u32[]{:S(2)}) collective-permute-start(f32[8,32,128]{2,1,0:T(8,128)S(1)} %get-tuple-element.15), channel_id=1, source_target_pairs={{0,8},{2,10},{4,12},{6,14},{8,0},{10,2},{12,4},{14,6},{16,24},{18,... | collective-permute-start | bytes 393224 | tf_op jit(solution)/shard_map/ppermute | solution.py:332
  86.4 13.3 %collective-permute-start.5 = (f32[8,32,128]{2,1,0:T(8,128)S(1)}, f32[8,32,128]{2,1,0:T(8,128)S(1)}, u32[]{:S(2)}, u32[]{:S(2)}) collective-permute-start(f32[8,32,128]{2,1,0:T(8,128)S(1)} %get-tuple-element.16), channel_id=1, source_target_pairs={{0,12},{2,14},{4,8},{6,10},{8,4},{10,6},{12,0},{14,2},{16,28},{18,... | collective-permute-start | bytes 393224 | tf_op jit(solution)/shard_map/ppermute | solution.py:332
  87.5 12.1 %collective-permute-start.4 = (f32[8,32,128]{2,1,0:T(8,128)S(1)}, f32[8,32,128]{2,1,0:T(8,128)S(1)}, u32[]{:S(2)}, u32[]{:S(2)}) collective-permute-start(f32[8,32,128]{2,1,0:T(8,128)S(1)} %get-tuple-element.17), channel_id=1, source_target_pairs={{0,4},{2,6},{4,0},{6,2},{8,12},{10,14},{12,8},{14,10},{16,20},{18,... | collective-permute-start | bytes 393224 | tf_op jit(solution)/shard_map/ppermute | solution.py:332
  99.7 30.5 %collective-permute-start.6 = (f32[1,32,128]{2,1,0:T(8,128)S(1)}, f32[1,32,128]{2,1,0:T(8,128)S(1)}, u32[]{:S(2)}, u32[]{:S(2)}) collective-permute-start(f32[1,32,128]{2,1,0:T(8,128)S(1)} %get-tuple-element.18), channel_id=1, source_target_pairs={{0,16},{2,18},{4,20},{6,22},{8,24},{10,26},{12,28},{14,30},{16,0},... | collective-permute-start | bytes 49160 | tf_op jit(solution)/shard_map/ppermute | solution.py:332
  102.8 30.1 %collective-permute-start.12 = (f32[1,32,128]{2,1,0:T(8,128)S(1)}, f32[1,32,128]{2,1,0:T(8,128)S(1)}, u32[]{:S(2)}, u32[]{:S(2)}) collective-permute-start(f32[1,32,128]{2,1,0:T(8,128)S(1)} %get-tuple-element.19), channel_id=1, source_target_pairs={{0,112},{2,114},{4,116},{6,118},{8,120},{10,122},{12,124},{14,126}... | collective-permute-start | bytes 49160 | tf_op jit(solution)/shard_map/ppermute | solution.py:332
  106.8 29.8 %collective-permute-start.11 = (f32[1,32,128]{2,1,0:T(8,128)S(1)}, f32[1,32,128]{2,1,0:T(8,128)S(1)}, u32[]{:S(2)}, u32[]{:S(2)}) collective-permute-start(f32[1,32,128]{2,1,0:T(8,128)S(1)} %get-tuple-element.20), channel_id=1, source_target_pairs={{0,96},{2,98},{4,100},{6,102},{8,104},{10,106},{12,108},{14,110},{... | collective-permute-start | bytes 49160 | tf_op jit(solution)/shard_map/ppermute | solution.py:332
  106.8 30.2 %collective-permute-start.10 = (f32[1,32,128]{2,1,0:T(8,128)S(1)}, f32[1,32,128]{2,1,0:T(8,128)S(1)}, u32[]{:S(2)}, u32[]{:S(2)}) collective-permute-start(f32[1,32,128]{2,1,0:T(8,128)S(1)} %get-tuple-element.21), channel_id=1, source_target_pairs={{0,80},{2,82},{4,84},{6,86},{8,88},{10,90},{12,92},{14,94},{16,64}... | collective-permute-start | bytes 49160 | tf_op jit(solution)/shard_map/ppermute | solution.py:332
  112.7 24.3 %collective-permute-start.9 = (f32[1,32,128]{2,1,0:T(8,128)S(1)}, f32[1,32,128]{2,1,0:T(8,128)S(1)}, u32[]{:S(2)}, u32[]{:S(2)}) collective-permute-start(f32[1,32,128]{2,1,0:T(8,128)S(1)} %get-tuple-element.22), channel_id=1, source_target_pairs={{0,64},{2,66},{4,68},{6,70},{8,72},{10,74},{12,76},{14,78},{16,80}... | collective-permute-start | bytes 49160 | tf_op jit(solution)/shard_map/ppermute | solution.py:332
  130.2 6.7 %collective-permute-start.8 = (f32[1,32,128]{2,1,0:T(8,128)S(1)}, f32[1,32,128]{2,1,0:T(8,128)S(1)}, u32[]{:S(2)}, u32[]{:S(2)}) collective-permute-start(f32[1,32,128]{2,1,0:T(8,128)S(1)} %get-tuple-element.23), channel_id=1, source_target_pairs={{0,48},{2,50},{4,52},{6,54},{8,56},{10,58},{12,60},{14,62},{16,32}... | collective-permute-start | bytes 49160 | tf_op jit(solution)/shard_map/ppermute | solution.py:332
  132.9 5.4 %collective-permute-start.7 = (f32[1,32,128]{2,1,0:T(8,128)S(1)}, f32[1,32,128]{2,1,0:T(8,128)S(1)}, u32[]{:S(2)}, u32[]{:S(2)}) collective-permute-start(f32[1,32,128]{2,1,0:T(8,128)S(1)} %get-tuple-element.24), channel_id=1, source_target_pairs={{0,32},{2,34},{4,36},{6,38},{8,40},{10,42},{12,44},{14,46},{16,48}... | collective-permute-start | bytes 49160 | tf_op jit(solution)/shard_map/ppermute | solution.py:332
  136.6 5.8 %collective-permute-start.2 = (bf16[64,512]{1,0:T(8,128)(2,1)S(1)}, bf16[64,512]{1,0:T(8,128)(2,1)S(1)}, u32[]{:S(2)}, u32[]{:S(2)}) collective-permute-start(bf16[64,512]{1,0:T(8,128)(2,1)S(1)} %get-tuple-element.11), channel_id=1, source_target_pairs={{0,1},{1,0},{2,3},{3,2},{4,5},{5,4},{6,7},{7,6},{8,9},{9,8},{10,11... | collective-permute-start | bytes 196616 | tf_op jit(solution)/shard_map/ppermute | solution.py:429

commit v6 on v5

--- a/solution.py
+++ b/solution.py
@@ -219,8 +219,9 @@
     return (
         list(range(cores))
         + list(range(y_from, y_from + ys))
+        + [z_from]
         + list(range(x_from, z_from))
-        + list(reversed(range(z_from, y_from)))
+        + list(reversed(range(z_from + 1, y_from)))
     )
 
 
@@ -400,7 +401,8 @@
     )
     for bit in bits[:EARLY]:
         partial = halve(partial, bit, stations)
-    first, _ = lax.optimization_barrier((first, partial))
+    first, partial = lax.optimization_barrier((first, partial))
+    partial = halve(partial, bits[EARLY], stations)
 
     lines, tail_rows = kernel_call(
         functools.partial(permute_kernel, rows=rows, tail_tiles=tail_tiles),
@@ -421,12 +423,14 @@
         ],
         4_000_000, 30_000_000, 52, (HBM_SPEC, VMEM_SPEC),
     )
+    lines, _ = lax.optimization_barrier((lines, partial))
     lines = lines.reshape(2 * stations, half, LANES)
     second = lax.all_to_all(lines, ("stn", "tpl"), 0, 0, tiled=True)
-    for part in bits[EARLY:-3], bits[-3:]:
-        partial = exchange(partial, part, stations)
+    tail_other = lax.ppermute(tail_rows, "tpl", [(0, 1), (1, 0)])
+    partial = exchange(partial, bits[EARLY + 1 : -2], stations)
+    partial, tail_other = lax.optimization_barrier((partial, tail_other))
+    partial = exchange(partial, bits[-2:], stations)
     stack = partial[0] * math.sqrt(length / channels)
-    tail_other = lax.ppermute(tail_rows, "tpl", [(0, 1), (1, 0)])
     tail_low = jnp.where(which == 0, tail_rows, tail_other)
     tail_high = jnp.where(which == 0, tail_other, tail_rows)
     grouped = kernel_call(

time: 144 us -> 140 us (0.972); the launches traced: 145 us -> 138 us
  starting transfers between devices: 57.1 us -> 48.1 us
  waiting for transfers between devices: 57.1 us -> 61.4 us
  Pallas kernels: 26.8 us -> 24.7 us
    ppermute x10 -> x6, starting transfers between devices: 25.8 us -> 14.9 us  [exchange(): lax.ppermute(partial[part], 'stn', [(i, i ^ mask) for i in range(count)])]
    ppermute x10 -> x6, waiting for transfers between devices: 28.6 us -> 34.9 us  [exchange(): lax.ppermute(partial[part], 'stn', [(i, i ^ mask) for i in range(count)])]
    ppermute x1, waiting for transfers between devices: 3.44 us -> 0.6 us  [shards(): tail_other = lax.ppermute(tail_rows, 'tpl', [(0, 1), (1, 0)])]
    ppermute x2 -> x3, starting transfers between devices: 3.54 us -> 5.81 us  [halve(): return partial[:half] + lax.ppermute(partial[half:], 'stn', pairs)]
    pallas_call x4, Pallas kernels: 26.8 us -> 24.7 us  [kernel_call(): pl.pallas_call(body, out_shape=outs, in_specs=[SMEM_SPEC] * len(scalars)...]
    all_to_all x1, waiting for transfers between devices: 1.95 us -> 3.69 us  [shards(): first = lax.all_to_all(packed, 'stn', 0, 0, tiled=True)]
    all_to_all x1, starting transfers between devices: 12.9 us -> 11.4 us  [shards(): second = lax.all_to_all(lines, ('stn', 'tpl'), 0, 0, tiled=True)]
    ppermute x2 -> x3, waiting for transfers between devices: 23.1 us -> 22.2 us  [halve(): return partial[:half] + lax.ppermute(partial[half:], 'stn', pairs)]
  transfers between devices with their start and end apart: 15 -> 12, of which waited for: 8 -> 9; matrix products, arithmetic and copies ran while one was open for 2% -> 2% of each run, Pallas kernels for 6% -> 14%
where the time goes in v6:
time: 140 us; the launch traced here: 138 us
  waiting for transfers between devices  61.4 us (44%)
  starting transfers between devices  48.1 us (34%)
  Pallas kernels  24.7 us (18%)
  other arithmetic  2.42 us (2%)
    ppermute x6, waiting for transfers between devices, exchange(): lax.ppermute(partial[part], 'stn', [(i, i ^ mask) for i in range(count)])  34.9 us
    pallas_call x4, Pallas kernels, kernel_call(): pl.pallas_call(body, out_shape=outs, in_specs=[SMEM_SPEC] * len(scalars)...  24.7 us
    ppermute x3, waiting for transfers between devices, halve(): return partial[:half] + lax.ppermute(partial[half:], 'stn', pairs)  22.2 us
    ppermute x6, starting transfers between devices, exchange(): lax.ppermute(partial[part], 'stn', [(i, i ^ mask) for i in range(count)])  14.9 us
    all_to_all x1, starting transfers between devices, shards(): first = lax.all_to_all(packed, 'stn', 0, 0, tiled=True)  14.5 us
    all_to_all x1, starting transfers between devices, shards(): second = lax.all_to_all(lines, ('stn', 'tpl'), 0, 0, tiled=True)  11.4 us
    ppermute x3, starting transfers between devices, halve(): return partial[:half] + lax.ppermute(partial[half:], 'stn', pairs)  5.81 us
    all_to_all x1, waiting for transfers between devices, shards(): first = lax.all_to_all(packed, 'stn', 0, 0, tiled=True)  3.69 us
  transfers between devices with their start and end apart: 12, of which 9 were waited for; matrix products, arithmetic and copies ran while one was open for 2% of the time, Pallas kernels for 14%

profile of v6, /device:TPU:16, one launch (start us, length us, event | category | flops | bytes accessed | tf_op | source)
XLA Modules:
  0.0 137.9 jit_solution(7354053455387386781)
XLA Ops:
  0.6 3.5 %shard_map.68 = bf16[128,48,128]{2,1,0:T(8,128)(2,1)} custom-call(s32[1]{0:T(128)} %bitcast.1.half_ref, s32[1,64]{1,0:T(1,128)} %bitcast.17, bf16[64,17408]{1,0:T(8,128)(2,1)} %archive_ref), custom_call_target="tpu_custom_call" | custom-call | flops 4000000 | bytes 4000000 | tf_op jit(solution)/shard_map/pallas_call | solution.py:310
  4.2 14.5 %all-to-all-start = ((bf16[128,48,128]{2,1,0:T(8,128)(2,1)}), bf16[128,48,128]{2,1,0:T(8,128)(2,1)}, u32[]{:S(2)}, u32[]{:S(2)}) async-start(bf16[128,48,128]{2,1,0:T(8,128)(2,1)} %shard_map.68), calls=%async_computation | async-start | bytes 3145728 | tf_op jit(solution)/shard_map/all_to_all | solution.py:381
  18.7 0.1 copy.9
  18.9 0.1 copy.10
  19.1 0.7 fusion
  19.8 0.2 select_reduce_fusion.1
  20.0 0.5 select_reduce_fusion.entry_ref
  20.5 7.1 %shard_map.69 = f32[128,32,128]{2,1,0:T(8,128)S(1)} custom-call(s32[1]{0:T(128)} %bitcast.4.count_ref, s32[960]{0:T(1024)S(1)} %select_reduce_fusion.entry_ref, s32[960]{0:T(1024)S(1)} %get-tuple-element.20.row_ref, s32[960]{0:T(1024)S(1)} %reshape.61.shift_ref, s32[1]{0:T(128)} %bitcast.6.place_ref, bf16[64,17408]{1,0:T(8,128)(2,1)S(1)} %copy-done, ...), custom_call_target="tpu_custom_call" | custom-call | flops 1000 | bytes 1000 | tf_op jit(solution)/shard_map/pallas_call | solution.py:310
  27.7 1.6 %collective-permute-start = (f32[64,32,128]{2,1,0:T(8,128)S(1)}, f32[64,32,128]{2,1,0:T(8,128)S(1)}, u32[]{:S(2)}, u32[]{:S(2)}) collective-permute-start(f32[64,32,128]{2,1,0:T(8,128)S(1)} %slice.65), channel_id=1, source_target_pairs={{0,2},{2,0},{4,6},{6,4},{8,10},{10,8},{12,14},{14,12},{16,18},{18,... | collective-permute-start | bytes 3145736 | tf_op jit(solution)/shard_map/ppermute | solution.py:324
  29.3 2.3 %collective-permute-done = f32[64,32,128]{2,1,0:T(8,128)S(1)} collective-permute-done((f32[64,32,128]{2,1,0:T(8,128)S(1)}, f32[64,32,128]{2,1,0:T(8,128)S(1)}, u32[]{:S(2)}, u32[]{:S(2)}) %collective-permute-start) | collective-permute-done | bytes 1048608 | tf_op jit(solution)/shard_map/ppermute | solution.py:324
  31.6 0.2 slice_add_fusion
  31.8 3.3 %collective-permute-start.1 = (f32[32,32,128]{2,1,0:T(8,128)S(1)}, f32[32,32,128]{2,1,0:T(8,128)S(1)}, u32[]{:S(2)}, u32[]{:S(2)}) collective-permute-start(f32[32,32,128]{2,1,0:T(8,128)S(1)} %slice.67), channel_id=1, source_target_pairs={{0,128},{2,130},{4,132},{6,134},{8,136},{10,138},{12,140},{14,142}... | collective-permute-start | bytes 1572872 | tf_op jit(solution)/shard_map/ppermute | solution.py:324
  35.1 19.9 %collective-permute-done.1 = f32[32,32,128]{2,1,0:T(8,128)S(1)} collective-permute-done((f32[32,32,128]{2,1,0:T(8,128)S(1)}, f32[32,32,128]{2,1,0:T(8,128)S(1)}, u32[]{:S(2)}, u32[]{:S(2)}) %collective-permute-start.1) | collective-permute-done | bytes 524320 | tf_op jit(solution)/shard_map/ppermute | solution.py:324
  55.0 0.1 slice_add_fusion.1
  55.1 3.7 %all-to-all-done.got_ref = bf16[128,48,128]{2,1,0:T(8,128)(2,1)} async-done(((bf16[128,48,128]{2,1,0:T(8,128)(2,1)}), bf16[128,48,128]{2,1,0:T(8,128)(2,1)}, u32[]{:S(2)}, u32[]{:S(2)}) %all-to-all-start) | async-done | bytes 1572896 | tf_op jit(solution)/shard_map/all_to_all | solution.py:381
  58.8 0.9 collective-permute-start.2
  59.7 11.6 %shard_map.70 = (bf16[128,2,32,128]{3,2,1,0:T(8,128)(2,1)}, bf16[64,512]{1,0:T(8,128)(2,1)S(1)}) custom-call(s32[1]{0:T(128)} %bitcast.owner_ref, bf16[128,48,128]{2,1,0:T(8,128)(2,1)} %all-to-all-done.got_ref), custom_call_target="tpu_custom_call" | custom-call | flops 4000000 | bytes 30000000 | tf_op jit(solution)/shard_map/pallas_call | solution.py:310
  71.4 11.4 %all-to-all-start.1 = ((bf16[256,32,128]{2,1,0:T(8,128)(2,1)}), bf16[256,32,128]{2,1,0:T(8,128)(2,1)S(1)}, u32[]{:S(2)}, u32[]{:S(2)}) async-start(bf16[256,32,128]{2,1,0:T(8,128)(2,1)} %bitcast.14), calls=%async_computation.1 | async-start | bytes 4194304 | tf_op jit(solution)/shard_map/all_to_all | solution.py:428
  82.8 3.1 %collective-permute-start.3 = (f32[4,32,128]{2,1,0:T(8,128)S(1)}, f32[4,32,128]{2,1,0:T(8,128)S(1)}, u32[]{:S(2)}, u32[]{:S(2)}) collective-permute-start(f32[4,32,128]{2,1,0:T(8,128)S(1)} %get-tuple-element.23), channel_id=1, source_target_pairs={{0,8},{2,10},{4,12},{6,14},{8,0},{10,2},{12,4},{14,6},{16,24},{18,... | collective-permute-start | bytes 196616 | tf_op jit(solution)/shard_map/ppermute | solution.py:333
  85.9 1.2 collective-permute-start.5
  87.0 1.5 %collective-permute-start.6 = (bf16[64,512]{1,0:T(8,128)(2,1)S(1)}, bf16[64,512]{1,0:T(8,128)(2,1)S(1)}, u32[]{:S(2)}, u32[]{:S(2)}) collective-permute-start(bf16[64,512]{1,0:T(8,128)(2,1)S(1)} %get-tuple-element.17), channel_id=1, source_target_pairs={{0,1},{1,0},{2,3},{3,2},{4,5},{5,4},{6,7},{7,6},{8,9},{9,8},{10,11... | collective-permute-start | bytes 196616 | tf_op jit(solution)/shard_map/ppermute | solution.py:429
  88.5 2.3 %collective-permute-done.3 = f32[4,32,128]{2,1,0:T(8,128)S(1)} collective-permute-done((f32[4,32,128]{2,1,0:T(8,128)S(1)}, f32[4,32,128]{2,1,0:T(8,128)S(1)}, u32[]{:S(2)}, u32[]{:S(2)}) %collective-permute-start.3) | collective-permute-done | bytes 65568 | tf_op jit(solution)/shard_map/ppermute | solution.py:333
  90.8 2.7 %collective-permute-done.5 = f32[4,32,128]{2,1,0:T(8,128)S(1)} collective-permute-done((f32[4,32,128]{2,1,0:T(8,128)S(1)}, f32[4,32,128]{2,1,0:T(8,128)S(1)}, u32[]{:S(2)}, u32[]{:S(2)}) %collective-permute-start.5) | collective-permute-done | bytes 65568 | tf_op jit(solution)/shard_map/ppermute | solution.py:333
  93.5 0.6 collective-permute-done.6
  94.1 2.7 %collective-permute-start.7 = (f32[1,32,128]{2,1,0:T(8,128)S(1)}, f32[1,32,128]{2,1,0:T(8,128)S(1)}, u32[]{:S(2)}, u32[]{:S(2)}) collective-permute-start(f32[1,32,128]{2,1,0:T(8,128)S(1)} %get-tuple-element.28), channel_id=1, source_target_pairs={{0,32},{2,34},{4,36},{6,38},{8,40},{10,42},{12,44},{14,46},{16,48}... | collective-permute-start | bytes 49160 | tf_op jit(solution)/shard_map/ppermute | solution.py:333
  96.8 6.7 %collective-permute-start.9 = (f32[1,32,128]{2,1,0:T(8,128)S(1)}, f32[1,32,128]{2,1,0:T(8,128)S(1)}, u32[]{:S(2)}, u32[]{:S(2)}) collective-permute-start(f32[1,32,128]{2,1,0:T(8,128)S(1)} %get-tuple-element.29), channel_id=1, source_target_pairs={{0,96},{2,98},{4,100},{6,102},{8,104},{10,106},{12,108},{14,110},{... | collective-permute-start | bytes 49160 | tf_op jit(solution)/shard_map/ppermute | solution.py:333
  103.6 1.3 collective-permute-start.8
  104.8 24.1 %collective-permute-done.7 = f32[1,32,128]{2,1,0:T(8,128)S(1)} collective-permute-done((f32[1,32,128]{2,1,0:T(8,128)S(1)}, f32[1,32,128]{2,1,0:T(8,128)S(1)}, u32[]{:S(2)}, u32[]{:S(2)}) %collective-permute-start.7) | collective-permute-done | bytes 16416 | tf_op jit(solution)/shard_map/ppermute | solution.py:333
  128.9 4.0 %collective-permute-done.9 = f32[1,32,128]{2,1,0:T(8,128)S(1)} collective-permute-done((f32[1,32,128]{2,1,0:T(8,128)S(1)}, f32[1,32,128]{2,1,0:T(8,128)S(1)}, u32[]{:S(2)}, u32[]{:S(2)}) %collective-permute-start.9) | collective-permute-done | bytes 16416 | tf_op jit(solution)/shard_map/ppermute | solution.py:333
  133.0 1.8 %collective-permute-done.8 = f32[1,32,128]{2,1,0:T(8,128)S(1)} collective-permute-done((f32[1,32,128]{2,1,0:T(8,128)S(1)}, f32[1,32,128]{2,1,0:T(8,128)S(1)}, u32[]{:S(2)}, u32[]{:S(2)}) %collective-permute-start.8) | collective-permute-done | bytes 16416 | tf_op jit(solution)/shard_map/ppermute | solution.py:333
  134.8 0.6 multiply_bitcast_fusion
  135.4 2.5 %shard_map.71 = bf16[64,17408]{1,0:T(8,128)(2,1)} custom-call(bf16[256,32,128]{2,1,0:T(8,128)(2,1)S(1)} %all-to-all-done.1.got_ref, bf16[64,512]{1,0:T(8,128)(2,1)S(1)} %get-tuple-element.27.tail_low_ref, bf16[64,512]{1,0:T(8,128)(2,1)S(1)} %get-tuple-element.26.tail_high_ref), custom_call_target="tpu_custom_call" | custom-call | flops 4000000 | bytes 6000000 | tf_op jit(solution)/shard_map/pallas_call | solution.py:310
  (25 shorter events, 0.4 us)
Async XLA Ops:
  0.6 19.9 %copy-start.1 = (bf16[32,30,600]{2,0,1:T(8,128)(2,1)S(1)}, bf16[32,30,600]{2,0,1:T(8,128)(2,1)}, u32[]{:S(2)}) copy-start(bf16[32,30,600]{2,0,1:T(8,128)(2,1)} %param.7) | copy-start | bytes 3456004
  4.2 14.6 %copy-start.2 = (s32[32,30]{1,0:T(8,128)S(1)}, s32[32,30]{1,0:T(8,128)}, u32[]{:S(2)}) copy-start(s32[32,30]{1,0:T(8,128)} %param.8) | copy-start | bytes 11524
  4.2 14.7 %copy-start.3 = (s32[32,30]{1,0:T(8,128)S(1)}, s32[32,30]{1,0:T(8,128)}, u32[]{:S(2)}) copy-start(s32[32,30]{1,0:T(8,128)} %param.9) | copy-start | bytes 11524
  4.2 14.9 %copy-start.4 = (s32[64]{0:T(128)S(1)}, s32[64]{0:T(128)}, u32[]{:S(2)}) copy-start(s32[64]{0:T(128)} %param.6) | copy-start | bytes 772
  4.2 16.3 %copy-start = (bf16[64,17408]{1,0:T(8,128)(2,1)S(1)}, bf16[64,17408]{1,0:T(8,128)(2,1)}, u32[]{:S(2)}) copy-start(bf16[64,17408]{1,0:T(8,128)(2,1)} %archive_ref) | copy-start | bytes 6684676
  4.2 54.6 %all-to-all-start = ((bf16[128,48,128]{2,1,0:T(8,128)(2,1)}), bf16[128,48,128]{2,1,0:T(8,128)(2,1)}, u32[]{:S(2)}, u32[]{:S(2)}) async-start(bf16[128,48,128]{2,1,0:T(8,128)(2,1)} %shard_map.68), calls=%async_computation | async-start | bytes 3145728 | tf_op jit(solution)/shard_map/all_to_all | solution.py:381
  27.7 3.9 %collective-permute-start = (f32[64,32,128]{2,1,0:T(8,128)S(1)}, f32[64,32,128]{2,1,0:T(8,128)S(1)}, u32[]{:S(2)}, u32[]{:S(2)}) collective-permute-start(f32[64,32,128]{2,1,0:T(8,128)S(1)} %slice.65), channel_id=1, source_target_pairs={{0,2},{2,0},{4,6},{6,4},{8,10},{10,8},{12,14},{14,12},{16,18},{18,... | collective-permute-start | bytes 3145736 | tf_op jit(solution)/shard_map/ppermute | solution.py:324
  31.8 23.2 %collective-permute-start.1 = (f32[32,32,128]{2,1,0:T(8,128)S(1)}, f32[32,32,128]{2,1,0:T(8,128)S(1)}, u32[]{:S(2)}, u32[]{:S(2)}) collective-permute-start(f32[32,32,128]{2,1,0:T(8,128)S(1)} %slice.67), channel_id=1, source_target_pairs={{0,128},{2,130},{4,132},{6,134},{8,136},{10,138},{12,140},{14,142}... | collective-permute-start | bytes 1572872 | tf_op jit(solution)/shard_map/ppermute | solution.py:324
  58.8 12.5 %collective-permute-start.2 = (f32[16,32,128]{2,1,0:T(8,128)S(1)}, f32[16,32,128]{2,1,0:T(8,128)S(1)}, u32[]{:S(2)}, u32[]{:S(2)}) collective-permute-start(f32[16,32,128]{2,1,0:T(8,128)S(1)} %slice.55), channel_id=1, source_target_pairs={{0,16},{2,18},{4,20},{6,22},{8,24},{10,26},{12,28},{14,30},{16,0},... | collective-permute-start | bytes 786440 | tf_op jit(solution)/shard_map/ppermute | solution.py:324
  71.4 64.0 %all-to-all-start.1 = ((bf16[256,32,128]{2,1,0:T(8,128)(2,1)}), bf16[256,32,128]{2,1,0:T(8,128)(2,1)S(1)}, u32[]{:S(2)}, u32[]{:S(2)}) async-start(bf16[256,32,128]{2,1,0:T(8,128)(2,1)} %bitcast.14), calls=%async_computation.1 | async-start | bytes 4194304 | tf_op jit(solution)/shard_map/all_to_all | solution.py:428
  82.8 8.0 %collective-permute-start.3 = (f32[4,32,128]{2,1,0:T(8,128)S(1)}, f32[4,32,128]{2,1,0:T(8,128)S(1)}, u32[]{:S(2)}, u32[]{:S(2)}) collective-permute-start(f32[4,32,128]{2,1,0:T(8,128)S(1)} %get-tuple-element.23), channel_id=1, source_target_pairs={{0,8},{2,10},{4,12},{6,14},{8,0},{10,2},{12,4},{14,6},{16,24},{18,... | collective-permute-start | bytes 196616 | tf_op jit(solution)/shard_map/ppermute | solution.py:333
  85.9 7.6 %collective-permute-start.5 = (f32[4,32,128]{2,1,0:T(8,128)S(1)}, f32[4,32,128]{2,1,0:T(8,128)S(1)}, u32[]{:S(2)}, u32[]{:S(2)}) collective-permute-start(f32[4,32,128]{2,1,0:T(8,128)S(1)} %get-tuple-element.24), channel_id=1, source_target_pairs={{0,12},{2,14},{4,8},{6,10},{8,4},{10,6},{12,0},{14,2},{16,28},{18,... | collective-permute-start | bytes 196616 | tf_op jit(solution)/shard_map/ppermute | solution.py:333
  87.0 6.5 %collective-permute-start.4 = (f32[4,32,128]{2,1,0:T(8,128)S(1)}, f32[4,32,128]{2,1,0:T(8,128)S(1)}, u32[]{:S(2)}, u32[]{:S(2)}) collective-permute-start(f32[4,32,128]{2,1,0:T(8,128)S(1)} %get-tuple-element.25), channel_id=1, source_target_pairs={{0,4},{2,6},{4,0},{6,2},{8,12},{10,14},{12,8},{14,10},{16,20},{18,... | collective-permute-start | bytes 196616 | tf_op jit(solution)/shard_map/ppermute | solution.py:333
  87.0 7.1 %collective-permute-start.6 = (bf16[64,512]{1,0:T(8,128)(2,1)S(1)}, bf16[64,512]{1,0:T(8,128)(2,1)S(1)}, u32[]{:S(2)}, u32[]{:S(2)}) collective-permute-start(bf16[64,512]{1,0:T(8,128)(2,1)S(1)} %get-tuple-element.17), channel_id=1, source_target_pairs={{0,1},{1,0},{2,3},{3,2},{4,5},{5,4},{6,7},{7,6},{8,9},{9,8},{10,11... | collective-permute-start | bytes 196616 | tf_op jit(solution)/shard_map/ppermute | solution.py:429
  94.1 34.8 %collective-permute-start.7 = (f32[1,32,128]{2,1,0:T(8,128)S(1)}, f32[1,32,128]{2,1,0:T(8,128)S(1)}, u32[]{:S(2)}, u32[]{:S(2)}) collective-permute-start(f32[1,32,128]{2,1,0:T(8,128)S(1)} %get-tuple-element.28), channel_id=1, source_target_pairs={{0,32},{2,34},{4,36},{6,38},{8,40},{10,42},{12,44},{14,46},{16,48}... | collective-permute-start | bytes 49160 | tf_op jit(solution)/shard_map/ppermute | solution.py:333
  96.8 36.1 %collective-permute-start.9 = (f32[1,32,128]{2,1,0:T(8,128)S(1)}, f32[1,32,128]{2,1,0:T(8,128)S(1)}, u32[]{:S(2)}, u32[]{:S(2)}) collective-permute-start(f32[1,32,128]{2,1,0:T(8,128)S(1)} %get-tuple-element.29), channel_id=1, source_target_pairs={{0,96},{2,98},{4,100},{6,102},{8,104},{10,106},{12,108},{14,110},{... | collective-permute-start | bytes 49160 | tf_op jit(solution)/shard_map/ppermute | solution.py:333
  103.6 31.2 %collective-permute-start.8 = (f32[1,32,128]{2,1,0:T(8,128)S(1)}, f32[1,32,128]{2,1,0:T(8,128)S(1)}, u32[]{:S(2)}, u32[]{:S(2)}) collective-permute-start(f32[1,32,128]{2,1,0:T(8,128)S(1)} %get-tuple-element.30), channel_id=1, source_target_pairs={{0,64},{2,66},{4,68},{6,70},{8,72},{10,74},{12,76},{14,78},{16,80}... | collective-permute-start | bytes 49160 | tf_op jit(solution)/shard_map/ppermute | solution.py:333

commit v7 on v6

--- a/solution.py
+++ b/solution.py
@@ -16,6 +16,7 @@
 PARTS = 4
 GROUP = 16
 EARLY = 2
+BESIDE = 4
 
 
 def roll_half(x):
@@ -219,9 +220,9 @@
     return (
         list(range(cores))
         + list(range(y_from, y_from + ys))
-        + [z_from]
+        + list(range(z_from, y_from - 1))
         + list(range(x_from, z_from))
-        + list(reversed(range(z_from + 1, y_from)))
+        + [y_from - 1]
     )
 
 
@@ -402,7 +403,7 @@
     for bit in bits[:EARLY]:
         partial = halve(partial, bit, stations)
     first, partial = lax.optimization_barrier((first, partial))
-    partial = halve(partial, bits[EARLY], stations)
+    partial = exchange(partial, bits[EARLY:BESIDE], stations)
 
     lines, tail_rows = kernel_call(
         functools.partial(permute_kernel, rows=rows, tail_tiles=tail_tiles),
@@ -427,9 +428,9 @@
     lines = lines.reshape(2 * stations, half, LANES)
     second = lax.all_to_all(lines, ("stn", "tpl"), 0, 0, tiled=True)
     tail_other = lax.ppermute(tail_rows, "tpl", [(0, 1), (1, 0)])
-    partial = exchange(partial, bits[EARLY + 1 : -2], stations)
+    partial = exchange(partial, bits[BESIDE:-1], stations)
     partial, tail_other = lax.optimization_barrier((partial, tail_other))
-    partial = exchange(partial, bits[-2:], stations)
+    partial = halve(partial, bits[-1], stations)
     stack = partial[0] * math.sqrt(length / channels)
     tail_low = jnp.where(which == 0, tail_rows, tail_other)
     tail_high = jnp.where(which == 0, tail_other, tail_rows)

time: 140 us -> 145 us (1.036)
  starting transfers between devices: 48.1 us -> 51.8 us
  waiting for transfers between devices: 61.4 us -> 63.3 us
    ppermute x3, waiting for transfers between devices: 22.2 us -> 55.6 us  [halve(): return partial[:half] + lax.ppermute(partial[half:], 'stn', pairs)]
    ppermute x6, waiting for transfers between devices: 34.9 us -> 2.76 us  [exchange(): lax.ppermute(partial[part], 'stn', [(i, i ^ mask) for i in range(count)])]
    ppermute x3, starting transfers between devices: 5.81 us -> 14 us  [halve(): return partial[:half] + lax.ppermute(partial[half:], 'stn', pairs)]
    ppermute x6, starting transfers between devices: 14.9 us -> 7.8 us  [exchange(): lax.ppermute(partial[part], 'stn', [(i, i ^ mask) for i in range(count)])]
    all_to_all x1, starting transfers between devices: 11.4 us -> 14.1 us  [shards(): second = lax.all_to_all(lines, ('stn', 'tpl'), 0, 0, tiled=True)]
    ppermute x1, waiting for transfers between devices: 0.6 us -> 2.84 us  [shards(): tail_other = lax.ppermute(tail_rows, 'tpl', [(0, 1), (1, 0)])]
    all_to_all x1, waiting for transfers between devices: 3.69 us -> 2.13 us  [shards(): first = lax.all_to_all(packed, 'stn', 0, 0, tiled=True)]
  transfers between devices with their start and end apart: 12 -> 12, of which waited for: 9 -> 7; matrix products, arithmetic and copies ran while one was open for 2% -> 2% of each run, Pallas kernels for 14% -> 12%
where the time goes in v7:
time: 145 us; the launch traced here: 143 us
  waiting for transfers between devices  63.3 us (44%)
  starting transfers between devices  51.8 us (36%)
  Pallas kernels  23.7 us (16%)
  other arithmetic  2.4 us (2%)
    ppermute x3, waiting for transfers between devices, halve(): return partial[:half] + lax.ppermute(partial[half:], 'stn', pairs)  55.6 us
    pallas_call x4, Pallas kernels, kernel_call(): pl.pallas_call(body, out_shape=outs, in_specs=[SMEM_SPEC] * len(scalars)...  23.7 us
    all_to_all x1, starting transfers between devices, shards(): first = lax.all_to_all(packed, 'stn', 0, 0, tiled=True)  14.5 us
    all_to_all x1, starting transfers between devices, shards(): second = lax.all_to_all(lines, ('stn', 'tpl'), 0, 0, tiled=True)  14.1 us
    ppermute x3, starting transfers between devices, halve(): return partial[:half] + lax.ppermute(partial[half:], 'stn', pairs)  14 us
    ppermute x6, starting transfers between devices, exchange(): lax.ppermute(partial[part], 'stn', [(i, i ^ mask) for i in range(count)])  7.8 us
  transfers between devices with their start and end apart: 12, of which 7 were waited for; matrix products, arithmetic and copies ran while one was open for 2% of the time, Pallas kernels for 12%

profile of v7, /device:TPU:16, one launch (start us, length us, event | category | flops | bytes accessed | tf_op | source)
XLA Modules:
  0.0 142.6 jit_solution(12969515962677433552)
XLA Ops:
  0.6 3.5 %shard_map.68 = bf16[128,48,128]{2,1,0:T(8,128)(2,1)} custom-call(s32[1]{0:T(128)} %bitcast.1.half_ref, s32[1,64]{1,0:T(1,128)} %bitcast.17, bf16[64,17408]{1,0:T(8,128)(2,1)} %archive_ref), custom_call_target="tpu_custom_call" | custom-call | flops 4000000 | bytes 4000000 | tf_op jit(solution)/shard_map/pallas_call | solution.py:311
  4.2 14.5 %all-to-all-start = ((bf16[128,48,128]{2,1,0:T(8,128)(2,1)}), bf16[128,48,128]{2,1,0:T(8,128)(2,1)}, u32[]{:S(2)}, u32[]{:S(2)}) async-start(bf16[128,48,128]{2,1,0:T(8,128)(2,1)} %shard_map.68), calls=%async_computation | async-start | bytes 3145728 | tf_op jit(solution)/shard_map/all_to_all | solution.py:382
  18.7 0.1 copy.9
  18.8 0.1 eq.14
  18.9 0.1 copy.10
  19.0 0.1 reshape.61.shift_ref
  19.1 0.7 fusion
  19.8 0.2 select_reduce_fusion.1
  20.0 0.5 select_reduce_fusion.entry_ref
  20.5 6.1 %shard_map.69 = f32[128,32,128]{2,1,0:T(8,128)S(1)} custom-call(s32[1]{0:T(128)} %bitcast.4.count_ref, s32[960]{0:T(1024)S(1)} %select_reduce_fusion.entry_ref, s32[960]{0:T(1024)S(1)} %get-tuple-element.20.row_ref, s32[960]{0:T(1024)S(1)} %reshape.61.shift_ref, s32[1]{0:T(128)} %bitcast.6.place_ref, bf16[64,17408]{1,0:T(8,128)(2,1)S(1)} %copy-done, ...), custom_call_target="tpu_custom_call" | custom-call | flops 1000 | bytes 1000 | tf_op jit(solution)/shard_map/pallas_call | solution.py:311
  26.7 1.6 %collective-permute-start = (f32[64,32,128]{2,1,0:T(8,128)S(1)}, f32[64,32,128]{2,1,0:T(8,128)S(1)}, u32[]{:S(2)}, u32[]{:S(2)}) collective-permute-start(f32[64,32,128]{2,1,0:T(8,128)S(1)} %slice.65), channel_id=1, source_target_pairs={{0,2},{2,0},{4,6},{6,4},{8,10},{10,8},{12,14},{14,12},{16,18},{18,... | collective-permute-start | bytes 3145736 | tf_op jit(solution)/shard_map/ppermute | solution.py:325
  28.3 2.3 %collective-permute-done = f32[64,32,128]{2,1,0:T(8,128)S(1)} collective-permute-done((f32[64,32,128]{2,1,0:T(8,128)S(1)}, f32[64,32,128]{2,1,0:T(8,128)S(1)}, u32[]{:S(2)}, u32[]{:S(2)}) %collective-permute-start) | collective-permute-done | bytes 1048608 | tf_op jit(solution)/shard_map/ppermute | solution.py:325
  30.6 0.2 slice_add_fusion
  30.8 5.0 %collective-permute-start.1 = (f32[32,32,128]{2,1,0:T(8,128)S(1)}, f32[32,32,128]{2,1,0:T(8,128)S(1)}, u32[]{:S(2)}, u32[]{:S(2)}) collective-permute-start(f32[32,32,128]{2,1,0:T(8,128)S(1)} %slice.67), channel_id=1, source_target_pairs={{0,128},{2,130},{4,132},{6,134},{8,136},{10,138},{12,140},{14,142}... | collective-permute-start | bytes 1572872 | tf_op jit(solution)/shard_map/ppermute | solution.py:325
  35.9 20.7 %collective-permute-done.1 = f32[32,32,128]{2,1,0:T(8,128)S(1)} collective-permute-done((f32[32,32,128]{2,1,0:T(8,128)S(1)}, f32[32,32,128]{2,1,0:T(8,128)S(1)}, u32[]{:S(2)}, u32[]{:S(2)}) %collective-permute-start.1) | collective-permute-done | bytes 524320 | tf_op jit(solution)/shard_map/ppermute | solution.py:325
  56.6 0.1 slice_add_fusion.1
  56.7 2.1 %all-to-all-done.got_ref = bf16[128,48,128]{2,1,0:T(8,128)(2,1)} async-done(((bf16[128,48,128]{2,1,0:T(8,128)(2,1)}), bf16[128,48,128]{2,1,0:T(8,128)(2,1)}, u32[]{:S(2)}, u32[]{:S(2)}) %all-to-all-start) | async-done | bytes 1572896 | tf_op jit(solution)/shard_map/all_to_all | solution.py:382
  58.8 2.8 %collective-permute-start.2 = (f32[8,32,128]{2,1,0:T(8,128)S(1)}, f32[8,32,128]{2,1,0:T(8,128)S(1)}, u32[]{:S(2)}, u32[]{:S(2)}) collective-permute-start(f32[8,32,128]{2,1,0:T(8,128)S(1)} %get-tuple-element.23), channel_id=1, source_target_pairs={{0,32},{2,34},{4,36},{6,38},{8,40},{10,42},{12,44},{14,46},{16,48}... | collective-permute-start | bytes 393224 | tf_op jit(solution)/shard_map/ppermute | solution.py:334
  61.6 0.4 collective-permute-start.4
  62.1 0.3 collective-permute-start.3
  62.4 11.6 %shard_map.70 = (bf16[128,2,32,128]{3,2,1,0:T(8,128)(2,1)}, bf16[64,512]{1,0:T(8,128)(2,1)S(1)}) custom-call(s32[1]{0:T(128)} %bitcast.owner_ref, bf16[128,48,128]{2,1,0:T(8,128)(2,1)} %all-to-all-done.got_ref), custom_call_target="tpu_custom_call" | custom-call | flops 4000000 | bytes 30000000 | tf_op jit(solution)/shard_map/pallas_call | solution.py:311
  74.1 14.1 %all-to-all-start.1 = ((bf16[256,32,128]{2,1,0:T(8,128)(2,1)}), bf16[256,32,128]{2,1,0:T(8,128)(2,1)S(1)}, u32[]{:S(2)}, u32[]{:S(2)}) async-start(bf16[256,32,128]{2,1,0:T(8,128)(2,1)} %bitcast.14), calls=%async_computation.1 | async-start | bytes 4194304 | tf_op jit(solution)/shard_map/all_to_all | solution.py:429
  88.2 3.1 %collective-permute-start.5 = (f32[2,32,128]{2,1,0:T(8,128)S(1)}, f32[2,32,128]{2,1,0:T(8,128)S(1)}, u32[]{:S(2)}, u32[]{:S(2)}) collective-permute-start(f32[2,32,128]{2,1,0:T(8,128)S(1)} %get-tuple-element.28), channel_id=1, source_target_pairs={{0,8},{2,10},{4,12},{6,14},{8,0},{10,2},{12,4},{14,6},{16,24},{18,... | collective-permute-start | bytes 98312 | tf_op jit(solution)/shard_map/ppermute | solution.py:334
  91.2 1.2 collective-permute-start.7
  92.4 1.5 %collective-permute-start.8 = (bf16[64,512]{1,0:T(8,128)(2,1)S(1)}, bf16[64,512]{1,0:T(8,128)(2,1)S(1)}, u32[]{:S(2)}, u32[]{:S(2)}) collective-permute-start(bf16[64,512]{1,0:T(8,128)(2,1)S(1)} %get-tuple-element.17), channel_id=1, source_target_pairs={{0,1},{1,0},{2,3},{3,2},{4,5},{5,4},{6,7},{7,6},{8,9},{9,8},{10,11... | collective-permute-start | bytes 196616 | tf_op jit(solution)/shard_map/ppermute | solution.py:430
  93.9 1.2 collective-permute-done.5
  95.1 1.5 %collective-permute-done.7 = f32[2,32,128]{2,1,0:T(8,128)S(1)} collective-permute-done((f32[2,32,128]{2,1,0:T(8,128)S(1)}, f32[2,32,128]{2,1,0:T(8,128)S(1)}, u32[]{:S(2)}, u32[]{:S(2)}) %collective-permute-start.7) | collective-permute-done | bytes 32800 | tf_op jit(solution)/shard_map/ppermute | solution.py:334
  96.7 2.8 %collective-permute-done.8 = bf16[64,512]{1,0:T(8,128)(2,1)S(1)} collective-permute-done((bf16[64,512]{1,0:T(8,128)(2,1)S(1)}, bf16[64,512]{1,0:T(8,128)(2,1)S(1)}, u32[]{:S(2)}, u32[]{:S(2)}) %collective-permute-start.8) | collective-permute-done | bytes 65568 | tf_op jit(solution)/shard_map/ppermute | solution.py:430
  99.5 7.3 %collective-permute-start.9 = (f32[1,32,128]{2,1,0:T(8,128)S(1)}, f32[1,32,128]{2,1,0:T(8,128)S(1)}, u32[]{:S(2)}, u32[]{:S(2)}) collective-permute-start(f32[1,32,128]{2,1,0:T(8,128)S(1)} %slice.63), channel_id=1, source_target_pairs={{0,64},{2,66},{4,68},{6,70},{8,72},{10,74},{12,76},{14,78},{16,80}... | collective-permute-start | bytes 49160 | tf_op jit(solution)/shard_map/ppermute | solution.py:325
  106.9 32.6 %collective-permute-done.9 = f32[1,32,128]{2,1,0:T(8,128)S(1)} collective-permute-done((f32[1,32,128]{2,1,0:T(8,128)S(1)}, f32[1,32,128]{2,1,0:T(8,128)S(1)}, u32[]{:S(2)}, u32[]{:S(2)}) %collective-permute-start.9) | collective-permute-done | bytes 16416 | tf_op jit(solution)/shard_map/ppermute | solution.py:325
  139.4 0.6 multiply_bitcast_fusion
  140.0 2.5 %shard_map.71 = bf16[64,17408]{1,0:T(8,128)(2,1)} custom-call(bf16[256,32,128]{2,1,0:T(8,128)(2,1)S(1)} %all-to-all-done.1.got_ref, bf16[64,512]{1,0:T(8,128)(2,1)S(1)} %get-tuple-element.27.tail_low_ref, bf16[64,512]{1,0:T(8,128)(2,1)S(1)} %get-tuple-element.26.tail_high_ref), custom_call_target="tpu_custom_call" | custom-call | flops 4000000 | bytes 6000000 | tf_op jit(solution)/shard_map/pallas_call | solution.py:311
  (25 shorter events, 0.3 us)
Async XLA Ops:
  0.6 19.9 %copy-start.1 = (bf16[32,30,600]{2,0,1:T(8,128)(2,1)S(1)}, bf16[32,30,600]{2,0,1:T(8,128)(2,1)}, u32[]{:S(2)}) copy-start(bf16[32,30,600]{2,0,1:T(8,128)(2,1)} %param.7) | copy-start | bytes 3456004
  4.2 14.6 %copy-start.2 = (s32[32,30]{1,0:T(8,128)S(1)}, s32[32,30]{1,0:T(8,128)}, u32[]{:S(2)}) copy-start(s32[32,30]{1,0:T(8,128)} %param.8) | copy-start | bytes 11524
  4.2 14.7 %copy-start.3 = (s32[32,30]{1,0:T(8,128)S(1)}, s32[32,30]{1,0:T(8,128)}, u32[]{:S(2)}) copy-start(s32[32,30]{1,0:T(8,128)} %param.9) | copy-start | bytes 11524
  4.2 14.9 %copy-start.4 = (s32[64]{0:T(128)S(1)}, s32[64]{0:T(128)}, u32[]{:S(2)}) copy-start(s32[64]{0:T(128)} %param.6) | copy-start | bytes 772
  4.2 16.3 %copy-start = (bf16[64,17408]{1,0:T(8,128)(2,1)S(1)}, bf16[64,17408]{1,0:T(8,128)(2,1)}, u32[]{:S(2)}) copy-start(bf16[64,17408]{1,0:T(8,128)(2,1)} %archive_ref) | copy-start | bytes 6684676
  4.2 54.6 %all-to-all-start = ((bf16[128,48,128]{2,1,0:T(8,128)(2,1)}), bf16[128,48,128]{2,1,0:T(8,128)(2,1)}, u32[]{:S(2)}, u32[]{:S(2)}) async-start(bf16[128,48,128]{2,1,0:T(8,128)(2,1)} %shard_map.68), calls=%async_computation | async-start | bytes 3145728 | tf_op jit(solution)/shard_map/all_to_all | solution.py:382
  26.7 3.9 %collective-permute-start = (f32[64,32,128]{2,1,0:T(8,128)S(1)}, f32[64,32,128]{2,1,0:T(8,128)S(1)}, u32[]{:S(2)}, u32[]{:S(2)}) collective-permute-start(f32[64,32,128]{2,1,0:T(8,128)S(1)} %slice.65), channel_id=1, source_target_pairs={{0,2},{2,0},{4,6},{6,4},{8,10},{10,8},{12,14},{14,12},{16,18},{18,... | collective-permute-start | bytes 3145736 | tf_op jit(solution)/shard_map/ppermute | solution.py:325
  30.8 25.8 %collective-permute-start.1 = (f32[32,32,128]{2,1,0:T(8,128)S(1)}, f32[32,32,128]{2,1,0:T(8,128)S(1)}, u32[]{:S(2)}, u32[]{:S(2)}) collective-permute-start(f32[32,32,128]{2,1,0:T(8,128)S(1)} %slice.67), channel_id=1, source_target_pairs={{0,128},{2,130},{4,132},{6,134},{8,136},{10,138},{12,140},{14,142}... | collective-permute-start | bytes 1572872 | tf_op jit(solution)/shard_map/ppermute | solution.py:325
  58.8 15.2 %collective-permute-start.2 = (f32[8,32,128]{2,1,0:T(8,128)S(1)}, f32[8,32,128]{2,1,0:T(8,128)S(1)}, u32[]{:S(2)}, u32[]{:S(2)}) collective-permute-start(f32[8,32,128]{2,1,0:T(8,128)S(1)} %get-tuple-element.23), channel_id=1, source_target_pairs={{0,32},{2,34},{4,36},{6,38},{8,40},{10,42},{12,44},{14,46},{16,48}... | collective-permute-start | bytes 393224 | tf_op jit(solution)/shard_map/ppermute | solution.py:334
  61.6 12.4 %collective-permute-start.4 = (f32[8,32,128]{2,1,0:T(8,128)S(1)}, f32[8,32,128]{2,1,0:T(8,128)S(1)}, u32[]{:S(2)}, u32[]{:S(2)}) collective-permute-start(f32[8,32,128]{2,1,0:T(8,128)S(1)} %get-tuple-element.24), channel_id=1, source_target_pairs={{0,48},{2,50},{4,52},{6,54},{8,56},{10,58},{12,60},{14,62},{16,32}... | collective-permute-start | bytes 393224 | tf_op jit(solution)/shard_map/ppermute | solution.py:334
  62.1 12.0 %collective-permute-start.3 = (f32[8,32,128]{2,1,0:T(8,128)S(1)}, f32[8,32,128]{2,1,0:T(8,128)S(1)}, u32[]{:S(2)}, u32[]{:S(2)}) collective-permute-start(f32[8,32,128]{2,1,0:T(8,128)S(1)} %get-tuple-element.25), channel_id=1, source_target_pairs={{0,16},{2,18},{4,20},{6,22},{8,24},{10,26},{12,28},{14,30},{16,0},... | collective-permute-start | bytes 393224 | tf_op jit(solution)/shard_map/ppermute | solution.py:334
  74.1 66.0 %all-to-all-start.1 = ((bf16[256,32,128]{2,1,0:T(8,128)(2,1)}), bf16[256,32,128]{2,1,0:T(8,128)(2,1)S(1)}, u32[]{:S(2)}, u32[]{:S(2)}) async-start(bf16[256,32,128]{2,1,0:T(8,128)(2,1)} %bitcast.14), calls=%async_computation.1 | async-start | bytes 4194304 | tf_op jit(solution)/shard_map/all_to_all | solution.py:429
  88.2 6.9 %collective-permute-start.5 = (f32[2,32,128]{2,1,0:T(8,128)S(1)}, f32[2,32,128]{2,1,0:T(8,128)S(1)}, u32[]{:S(2)}, u32[]{:S(2)}) collective-permute-start(f32[2,32,128]{2,1,0:T(8,128)S(1)} %get-tuple-element.28), channel_id=1, source_target_pairs={{0,8},{2,10},{4,12},{6,14},{8,0},{10,2},{12,4},{14,6},{16,24},{18,... | collective-permute-start | bytes 98312 | tf_op jit(solution)/shard_map/ppermute | solution.py:334
  91.2 5.4 %collective-permute-start.7 = (f32[2,32,128]{2,1,0:T(8,128)S(1)}, f32[2,32,128]{2,1,0:T(8,128)S(1)}, u32[]{:S(2)}, u32[]{:S(2)}) collective-permute-start(f32[2,32,128]{2,1,0:T(8,128)S(1)} %get-tuple-element.29), channel_id=1, source_target_pairs={{0,12},{2,14},{4,8},{6,10},{8,4},{10,6},{12,0},{14,2},{16,28},{18,... | collective-permute-start | bytes 98312 | tf_op jit(solution)/shard_map/ppermute | solution.py:334
  92.4 4.2 %collective-permute-start.6 = (f32[2,32,128]{2,1,0:T(8,128)S(1)}, f32[2,32,128]{2,1,0:T(8,128)S(1)}, u32[]{:S(2)}, u32[]{:S(2)}) collective-permute-start(f32[2,32,128]{2,1,0:T(8,128)S(1)} %get-tuple-element.30), channel_id=1, source_target_pairs={{0,4},{2,6},{4,0},{6,2},{8,12},{10,14},{12,8},{14,10},{16,20},{18,... | collective-permute-start | bytes 98312 | tf_op jit(solution)/shard_map/ppermute | solution.py:334
  92.4 7.1 %collective-permute-start.8 = (bf16[64,512]{1,0:T(8,128)(2,1)S(1)}, bf16[64,512]{1,0:T(8,128)(2,1)S(1)}, u32[]{:S(2)}, u32[]{:S(2)}) collective-permute-start(bf16[64,512]{1,0:T(8,128)(2,1)S(1)} %get-tuple-element.17), channel_id=1, source_target_pairs={{0,1},{1,0},{2,3},{3,2},{4,5},{5,4},{6,7},{7,6},{8,9},{9,8},{10,11... | collective-permute-start | bytes 196616 | tf_op jit(solution)/shard_map/ppermute | solution.py:430
  99.5 39.9 %collective-permute-start.9 = (f32[1,32,128]{2,1,0:T(8,128)S(1)}, f32[1,32,128]{2,1,0:T(8,128)S(1)}, u32[]{:S(2)}, u32[]{:S(2)}) collective-permute-start(f32[1,32,128]{2,1,0:T(8,128)S(1)} %slice.63), channel_id=1, source_target_pairs={{0,64},{2,66},{4,68},{6,70},{8,72},{10,74},{12,76},{14,78},{16,80}... | collective-permute-start | bytes 49160 | tf_op jit(solution)/shard_map/ppermute | solution.py:325

commit v8 on v6

--- a/solution.py
+++ b/solution.py
@@ -13,7 +13,7 @@
 KW = 7
 SPAN = KW * LANES
 MIB = 1024 * 1024
-PARTS = 4
+PARTS = 8
 GROUP = 16
 EARLY = 2
 
@@ -285,9 +285,11 @@
         inside = (lag >= fine) & (lag < fine + length)
         mask = jnp.where(inside, 1.0, 0.0).astype(jnp.bfloat16)
         product = lax.dot_general(windows(line_ref), banded, contract, preferred_element_type=jnp.float32)
-        energy = lax.dot_general(
-            windows(high_ref), mask, contract, preferred_element_type=jnp.float32
-        ) + lax.dot_general(windows(low_ref), mask, contract, preferred_element_type=jnp.float32)
+        both = lax.dot_general(
+            jnp.concatenate([windows(high_ref), windows(low_ref)], axis=0),
+            mask, contract, preferred_element_type=jnp.float32,
+        )
+        energy = both[:blocks] + both[blocks:]
         scale = (energy / length + EPSILON) * (power / length + EPSILON)
         normalized = product / length / jnp.sqrt(scale)
         template = entry % out_ref.shape[1]

time: 140 us -> 140 us (level)
  starting transfers between devices: 48.1 us -> 52.2 us
  waiting for transfers between devices: 61.4 us -> 59.1 us
    ppermute x3, starting transfers between devices: 5.81 us -> 8.48 us  [halve(): return partial[:half] + lax.ppermute(partial[half:], 'stn', pairs)]
    all_to_all x1, waiting for transfers between devices: 3.69 us -> 1.32 us  [shards(): first = lax.all_to_all(packed, 'stn', 0, 0, tiled=True)]
    all_to_all x1, starting transfers between devices: 11.4 us -> 12.9 us  [shards(): second = lax.all_to_all(lines, ('stn', 'tpl'), 0, 0, tiled=True)]
  transfers between devices with their start and end apart: 12 -> 12, of which waited for: 9 -> 9; matrix products, arithmetic and copies ran while one was open for 2% -> 2% of each run, Pallas kernels for 14% -> 13%
where the time goes in v8:
time: 140 us; the launch traced here: 139 us
  waiting for transfers between devices  59.1 us (42%)
  starting transfers between devices  52.2 us (37%)
  Pallas kernels  23.4 us (17%)
  other arithmetic  2.42 us (2%)
    ppermute x6, waiting for transfers between devices, exchange(): lax.ppermute(partial[part], 'stn', [(i, i ^ mask) for i in range(count)])  34.9 us
    pallas_call x4, Pallas kernels, kernel_call(): pl.pallas_call(body, out_shape=outs, in_specs=[SMEM_SPEC] * len(scalars)...  23.4 us
    ppermute x3, waiting for transfers between devices, halve(): return partial[:half] + lax.ppermute(partial[half:], 'stn', pairs)  22.3 us
    ppermute x6, starting transfers between devices, exchange(): lax.ppermute(partial[part], 'stn', [(i, i ^ mask) for i in range(count)])  14.9 us
    all_to_all x1, starting transfers between devices, shards(): first = lax.all_to_all(packed, 'stn', 0, 0, tiled=True)  14.5 us
    all_to_all x1, starting transfers between devices, shards(): second = lax.all_to_all(lines, ('stn', 'tpl'), 0, 0, tiled=True)  12.9 us
    ppermute x3, starting transfers between devices, halve(): return partial[:half] + lax.ppermute(partial[half:], 'stn', pairs)  8.48 us
  transfers between devices with their start and end apart: 12, of which 9 were waited for; matrix products, arithmetic and copies ran while one was open for 2% of the time, Pallas kernels for 13%

profile of v8, /device:TPU:16, one launch (start us, length us, event | category | flops | bytes accessed | tf_op | source)
XLA Modules:
  0.0 138.7 jit_solution(7007565395321741558)
XLA Ops:
  0.6 3.5 %shard_map.68 = bf16[128,48,128]{2,1,0:T(8,128)(2,1)} custom-call(s32[1]{0:T(128)} %bitcast.1.half_ref, s32[1,64]{1,0:T(1,128)} %bitcast.17, bf16[64,17408]{1,0:T(8,128)(2,1)} %archive_ref), custom_call_target="tpu_custom_call" | custom-call | flops 4000000 | bytes 4000000 | tf_op jit(solution)/shard_map/pallas_call | solution.py:312
  4.2 14.5 %all-to-all-start = ((bf16[128,48,128]{2,1,0:T(8,128)(2,1)}), bf16[128,48,128]{2,1,0:T(8,128)(2,1)}, u32[]{:S(2)}, u32[]{:S(2)}) async-start(bf16[128,48,128]{2,1,0:T(8,128)(2,1)} %shard_map.68), calls=%async_computation | async-start | bytes 3145728 | tf_op jit(solution)/shard_map/all_to_all | solution.py:383
  18.7 0.1 copy.9
  18.9 0.1 copy.10
  19.0 0.7 fusion
  19.8 0.2 select_reduce_fusion.1
  20.0 0.5 select_reduce_fusion.entry_ref
  20.5 5.9 %shard_map.69 = f32[128,32,128]{2,1,0:T(8,128)S(1)} custom-call(s32[1]{0:T(128)} %bitcast.4.count_ref, s32[960]{0:T(1024)S(1)} %select_reduce_fusion.entry_ref, s32[960]{0:T(1024)S(1)} %get-tuple-element.20.row_ref, s32[960]{0:T(1024)S(1)} %reshape.61.shift_ref, s32[1]{0:T(128)} %bitcast.6.place_ref, bf16[64,17408]{1,0:T(8,128)(2,1)S(1)} %copy-done, ...), custom_call_target="tpu_custom_call" | custom-call | flops 1000 | bytes 1000 | tf_op jit(solution)/shard_map/pallas_call | solution.py:312
  26.5 3.4 %collective-permute-start = (f32[64,32,128]{2,1,0:T(8,128)S(1)}, f32[64,32,128]{2,1,0:T(8,128)S(1)}, u32[]{:S(2)}, u32[]{:S(2)}) collective-permute-start(f32[64,32,128]{2,1,0:T(8,128)S(1)} %slice.65), channel_id=1, source_target_pairs={{0,2},{2,0},{4,6},{6,4},{8,10},{10,8},{12,14},{14,12},{16,18},{18,... | collective-permute-start | bytes 3145736 | tf_op jit(solution)/shard_map/ppermute | solution.py:326
  29.9 2.3 %collective-permute-done = f32[64,32,128]{2,1,0:T(8,128)S(1)} collective-permute-done((f32[64,32,128]{2,1,0:T(8,128)S(1)}, f32[64,32,128]{2,1,0:T(8,128)S(1)}, u32[]{:S(2)}, u32[]{:S(2)}) %collective-permute-start) | collective-permute-done | bytes 1048608 | tf_op jit(solution)/shard_map/ppermute | solution.py:326
  32.2 0.2 slice_add_fusion
  32.5 4.9 %collective-permute-start.1 = (f32[32,32,128]{2,1,0:T(8,128)S(1)}, f32[32,32,128]{2,1,0:T(8,128)S(1)}, u32[]{:S(2)}, u32[]{:S(2)}) collective-permute-start(f32[32,32,128]{2,1,0:T(8,128)S(1)} %slice.67), channel_id=1, source_target_pairs={{0,128},{2,130},{4,132},{6,134},{8,136},{10,138},{12,140},{14,142}... | collective-permute-start | bytes 1572872 | tf_op jit(solution)/shard_map/ppermute | solution.py:326
  37.4 20.0 %collective-permute-done.1 = f32[32,32,128]{2,1,0:T(8,128)S(1)} collective-permute-done((f32[32,32,128]{2,1,0:T(8,128)S(1)}, f32[32,32,128]{2,1,0:T(8,128)S(1)}, u32[]{:S(2)}, u32[]{:S(2)}) %collective-permute-start.1) | collective-permute-done | bytes 524320 | tf_op jit(solution)/shard_map/ppermute | solution.py:326
  57.4 0.1 slice_add_fusion.1
  57.4 1.3 all-to-all-done.got_ref
  58.8 0.1 collective-permute-start.2
  58.9 11.5 %shard_map.70 = (bf16[128,2,32,128]{3,2,1,0:T(8,128)(2,1)}, bf16[64,512]{1,0:T(8,128)(2,1)S(1)}) custom-call(s32[1]{0:T(128)} %bitcast.owner_ref, bf16[128,48,128]{2,1,0:T(8,128)(2,1)} %all-to-all-done.got_ref), custom_call_target="tpu_custom_call" | custom-call | flops 4000000 | bytes 30000000 | tf_op jit(solution)/shard_map/pallas_call | solution.py:312
  70.5 12.9 %all-to-all-start.1 = ((bf16[256,32,128]{2,1,0:T(8,128)(2,1)}), bf16[256,32,128]{2,1,0:T(8,128)(2,1)S(1)}, u32[]{:S(2)}, u32[]{:S(2)}) async-start(bf16[256,32,128]{2,1,0:T(8,128)(2,1)} %bitcast.14), calls=%async_computation.1 | async-start | bytes 4194304 | tf_op jit(solution)/shard_map/all_to_all | solution.py:430
  83.4 3.1 %collective-permute-start.3 = (f32[4,32,128]{2,1,0:T(8,128)S(1)}, f32[4,32,128]{2,1,0:T(8,128)S(1)}, u32[]{:S(2)}, u32[]{:S(2)}) collective-permute-start(f32[4,32,128]{2,1,0:T(8,128)S(1)} %get-tuple-element.23), channel_id=1, source_target_pairs={{0,8},{2,10},{4,12},{6,14},{8,0},{10,2},{12,4},{14,6},{16,24},{18,... | collective-permute-start | bytes 196616 | tf_op jit(solution)/shard_map/ppermute | solution.py:335
  86.5 1.2 collective-permute-start.5
  87.6 1.5 %collective-permute-start.6 = (bf16[64,512]{1,0:T(8,128)(2,1)S(1)}, bf16[64,512]{1,0:T(8,128)(2,1)S(1)}, u32[]{:S(2)}, u32[]{:S(2)}) collective-permute-start(bf16[64,512]{1,0:T(8,128)(2,1)S(1)} %get-tuple-element.17), channel_id=1, source_target_pairs={{0,1},{1,0},{2,3},{3,2},{4,5},{5,4},{6,7},{7,6},{8,9},{9,8},{10,11... | collective-permute-start | bytes 196616 | tf_op jit(solution)/shard_map/ppermute | solution.py:431
  89.1 2.3 %collective-permute-done.3 = f32[4,32,128]{2,1,0:T(8,128)S(1)} collective-permute-done((f32[4,32,128]{2,1,0:T(8,128)S(1)}, f32[4,32,128]{2,1,0:T(8,128)S(1)}, u32[]{:S(2)}, u32[]{:S(2)}) %collective-permute-start.3) | collective-permute-done | bytes 65568 | tf_op jit(solution)/shard_map/ppermute | solution.py:335
  91.4 2.7 %collective-permute-done.5 = f32[4,32,128]{2,1,0:T(8,128)S(1)} collective-permute-done((f32[4,32,128]{2,1,0:T(8,128)S(1)}, f32[4,32,128]{2,1,0:T(8,128)S(1)}, u32[]{:S(2)}, u32[]{:S(2)}) %collective-permute-start.5) | collective-permute-done | bytes 65568 | tf_op jit(solution)/shard_map/ppermute | solution.py:335
  94.1 0.6 collective-permute-done.6
  94.7 2.7 %collective-permute-start.7 = (f32[1,32,128]{2,1,0:T(8,128)S(1)}, f32[1,32,128]{2,1,0:T(8,128)S(1)}, u32[]{:S(2)}, u32[]{:S(2)}) collective-permute-start(f32[1,32,128]{2,1,0:T(8,128)S(1)} %get-tuple-element.28), channel_id=1, source_target_pairs={{0,32},{2,34},{4,36},{6,38},{8,40},{10,42},{12,44},{14,46},{16,48}... | collective-permute-start | bytes 49160 | tf_op jit(solution)/shard_map/ppermute | solution.py:335
  97.4 6.7 %collective-permute-start.9 = (f32[1,32,128]{2,1,0:T(8,128)S(1)}, f32[1,32,128]{2,1,0:T(8,128)S(1)}, u32[]{:S(2)}, u32[]{:S(2)}) collective-permute-start(f32[1,32,128]{2,1,0:T(8,128)S(1)} %get-tuple-element.29), channel_id=1, source_target_pairs={{0,96},{2,98},{4,100},{6,102},{8,104},{10,106},{12,108},{14,110},{... | collective-permute-start | bytes 49160 | tf_op jit(solution)/shard_map/ppermute | solution.py:335
  104.1 1.3 collective-permute-start.8
  105.4 24.1 %collective-permute-done.7 = f32[1,32,128]{2,1,0:T(8,128)S(1)} collective-permute-done((f32[1,32,128]{2,1,0:T(8,128)S(1)}, f32[1,32,128]{2,1,0:T(8,128)S(1)}, u32[]{:S(2)}, u32[]{:S(2)}) %collective-permute-start.7) | collective-permute-done | bytes 16416 | tf_op jit(solution)/shard_map/ppermute | solution.py:335
  129.5 4.0 %collective-permute-done.9 = f32[1,32,128]{2,1,0:T(8,128)S(1)} collective-permute-done((f32[1,32,128]{2,1,0:T(8,128)S(1)}, f32[1,32,128]{2,1,0:T(8,128)S(1)}, u32[]{:S(2)}, u32[]{:S(2)}) %collective-permute-start.9) | collective-permute-done | bytes 16416 | tf_op jit(solution)/shard_map/ppermute | solution.py:335
  133.5 1.8 %collective-permute-done.8 = f32[1,32,128]{2,1,0:T(8,128)S(1)} collective-permute-done((f32[1,32,128]{2,1,0:T(8,128)S(1)}, f32[1,32,128]{2,1,0:T(8,128)S(1)}, u32[]{:S(2)}, u32[]{:S(2)}) %collective-permute-start.8) | collective-permute-done | bytes 16416 | tf_op jit(solution)/shard_map/ppermute | solution.py:335
  135.4 0.6 multiply_bitcast_fusion
  136.0 2.5 %shard_map.71 = bf16[64,17408]{1,0:T(8,128)(2,1)} custom-call(bf16[256,32,128]{2,1,0:T(8,128)(2,1)S(1)} %all-to-all-done.1.got_ref, bf16[64,512]{1,0:T(8,128)(2,1)S(1)} %get-tuple-element.27.tail_low_ref, bf16[64,512]{1,0:T(8,128)(2,1)S(1)} %get-tuple-element.26.tail_high_ref), custom_call_target="tpu_custom_call" | custom-call | flops 4000000 | bytes 6000000 | tf_op jit(solution)/shard_map/pallas_call | solution.py:312
  (25 shorter events, 0.4 us)
Async XLA Ops:
  0.6 19.9 %copy-start.1 = (bf16[32,30,600]{2,0,1:T(8,128)(2,1)S(1)}, bf16[32,30,600]{2,0,1:T(8,128)(2,1)}, u32[]{:S(2)}) copy-start(bf16[32,30,600]{2,0,1:T(8,128)(2,1)} %param.7) | copy-start | bytes 3456004
  4.1 14.6 %copy-start.2 = (s32[32,30]{1,0:T(8,128)S(1)}, s32[32,30]{1,0:T(8,128)}, u32[]{:S(2)}) copy-start(s32[32,30]{1,0:T(8,128)} %param.8) | copy-start | bytes 11524
  4.2 14.7 %copy-start.3 = (s32[32,30]{1,0:T(8,128)S(1)}, s32[32,30]{1,0:T(8,128)}, u32[]{:S(2)}) copy-start(s32[32,30]{1,0:T(8,128)} %param.9) | copy-start | bytes 11524
  4.2 14.9 %copy-start.4 = (s32[64]{0:T(128)S(1)}, s32[64]{0:T(128)}, u32[]{:S(2)}) copy-start(s32[64]{0:T(128)} %param.6) | copy-start | bytes 772
  4.2 16.3 %copy-start = (bf16[64,17408]{1,0:T(8,128)(2,1)S(1)}, bf16[64,17408]{1,0:T(8,128)(2,1)}, u32[]{:S(2)}) copy-start(bf16[64,17408]{1,0:T(8,128)(2,1)} %archive_ref) | copy-start | bytes 6684676
  4.2 54.6 %all-to-all-start = ((bf16[128,48,128]{2,1,0:T(8,128)(2,1)}), bf16[128,48,128]{2,1,0:T(8,128)(2,1)}, u32[]{:S(2)}, u32[]{:S(2)}) async-start(bf16[128,48,128]{2,1,0:T(8,128)(2,1)} %shard_map.68), calls=%async_computation | async-start | bytes 3145728 | tf_op jit(solution)/shard_map/all_to_all | solution.py:383
  26.5 5.7 %collective-permute-start = (f32[64,32,128]{2,1,0:T(8,128)S(1)}, f32[64,32,128]{2,1,0:T(8,128)S(1)}, u32[]{:S(2)}, u32[]{:S(2)}) collective-permute-start(f32[64,32,128]{2,1,0:T(8,128)S(1)} %slice.65), channel_id=1, source_target_pairs={{0,2},{2,0},{4,6},{6,4},{8,10},{10,8},{12,14},{14,12},{16,18},{18,... | collective-permute-start | bytes 3145736 | tf_op jit(solution)/shard_map/ppermute | solution.py:326
  32.5 24.9 %collective-permute-start.1 = (f32[32,32,128]{2,1,0:T(8,128)S(1)}, f32[32,32,128]{2,1,0:T(8,128)S(1)}, u32[]{:S(2)}, u32[]{:S(2)}) collective-permute-start(f32[32,32,128]{2,1,0:T(8,128)S(1)} %slice.67), channel_id=1, source_target_pairs={{0,128},{2,130},{4,132},{6,134},{8,136},{10,138},{12,140},{14,142}... | collective-permute-start | bytes 1572872 | tf_op jit(solution)/shard_map/ppermute | solution.py:326
  58.8 11.6 %collective-permute-start.2 = (f32[16,32,128]{2,1,0:T(8,128)S(1)}, f32[16,32,128]{2,1,0:T(8,128)S(1)}, u32[]{:S(2)}, u32[]{:S(2)}) collective-permute-start(f32[16,32,128]{2,1,0:T(8,128)S(1)} %slice.55), channel_id=1, source_target_pairs={{0,16},{2,18},{4,20},{6,22},{8,24},{10,26},{12,28},{14,30},{16,0},... | collective-permute-start | bytes 786440 | tf_op jit(solution)/shard_map/ppermute | solution.py:326
  70.5 65.5 %all-to-all-start.1 = ((bf16[256,32,128]{2,1,0:T(8,128)(2,1)}), bf16[256,32,128]{2,1,0:T(8,128)(2,1)S(1)}, u32[]{:S(2)}, u32[]{:S(2)}) async-start(bf16[256,32,128]{2,1,0:T(8,128)(2,1)} %bitcast.14), calls=%async_computation.1 | async-start | bytes 4194304 | tf_op jit(solution)/shard_map/all_to_all | solution.py:430
  83.4 8.0 %collective-permute-start.3 = (f32[4,32,128]{2,1,0:T(8,128)S(1)}, f32[4,32,128]{2,1,0:T(8,128)S(1)}, u32[]{:S(2)}, u32[]{:S(2)}) collective-permute-start(f32[4,32,128]{2,1,0:T(8,128)S(1)} %get-tuple-element.23), channel_id=1, source_target_pairs={{0,8},{2,10},{4,12},{6,14},{8,0},{10,2},{12,4},{14,6},{16,24},{18,... | collective-permute-start | bytes 196616 | tf_op jit(solution)/shard_map/ppermute | solution.py:335
  86.5 7.6 %collective-permute-start.5 = (f32[4,32,128]{2,1,0:T(8,128)S(1)}, f32[4,32,128]{2,1,0:T(8,128)S(1)}, u32[]{:S(2)}, u32[]{:S(2)}) collective-permute-start(f32[4,32,128]{2,1,0:T(8,128)S(1)} %get-tuple-element.24), channel_id=1, source_target_pairs={{0,12},{2,14},{4,8},{6,10},{8,4},{10,6},{12,0},{14,2},{16,28},{18,... | collective-permute-start | bytes 196616 | tf_op jit(solution)/shard_map/ppermute | solution.py:335
  87.6 6.5 %collective-permute-start.4 = (f32[4,32,128]{2,1,0:T(8,128)S(1)}, f32[4,32,128]{2,1,0:T(8,128)S(1)}, u32[]{:S(2)}, u32[]{:S(2)}) collective-permute-start(f32[4,32,128]{2,1,0:T(8,128)S(1)} %get-tuple-element.25), channel_id=1, source_target_pairs={{0,4},{2,6},{4,0},{6,2},{8,12},{10,14},{12,8},{14,10},{16,20},{18,... | collective-permute-start | bytes 196616 | tf_op jit(solution)/shard_map/ppermute | solution.py:335
  87.6 7.1 %collective-permute-start.6 = (bf16[64,512]{1,0:T(8,128)(2,1)S(1)}, bf16[64,512]{1,0:T(8,128)(2,1)S(1)}, u32[]{:S(2)}, u32[]{:S(2)}) collective-permute-start(bf16[64,512]{1,0:T(8,128)(2,1)S(1)} %get-tuple-element.17), channel_id=1, source_target_pairs={{0,1},{1,0},{2,3},{3,2},{4,5},{5,4},{6,7},{7,6},{8,9},{9,8},{10,11... | collective-permute-start | bytes 196616 | tf_op jit(solution)/shard_map/ppermute | solution.py:431
  94.7 34.8 %collective-permute-start.7 = (f32[1,32,128]{2,1,0:T(8,128)S(1)}, f32[1,32,128]{2,1,0:T(8,128)S(1)}, u32[]{:S(2)}, u32[]{:S(2)}) collective-permute-start(f32[1,32,128]{2,1,0:T(8,128)S(1)} %get-tuple-element.28), channel_id=1, source_target_pairs={{0,32},{2,34},{4,36},{6,38},{8,40},{10,42},{12,44},{14,46},{16,48}... | collective-permute-start | bytes 49160 | tf_op jit(solution)/shard_map/ppermute | solution.py:335
  97.4 36.1 %collective-permute-start.9 = (f32[1,32,128]{2,1,0:T(8,128)S(1)}, f32[1,32,128]{2,1,0:T(8,128)S(1)}, u32[]{:S(2)}, u32[]{:S(2)}) collective-permute-start(f32[1,32,128]{2,1,0:T(8,128)S(1)} %get-tuple-element.29), channel_id=1, source_target_pairs={{0,96},{2,98},{4,100},{6,102},{8,104},{10,106},{12,108},{14,110},{... | collective-permute-start | bytes 49160 | tf_op jit(solution)/shard_map/ppermute | solution.py:335
  104.1 31.2 %collective-permute-start.8 = (f32[1,32,128]{2,1,0:T(8,128)S(1)}, f32[1,32,128]{2,1,0:T(8,128)S(1)}, u32[]{:S(2)}, u32[]{:S(2)}) collective-permute-start(f32[1,32,128]{2,1,0:T(8,128)S(1)} %get-tuple-element.30), channel_id=1, source_target_pairs={{0,64},{2,66},{4,68},{6,70},{8,72},{10,74},{12,76},{14,78},{16,80}... | collective-permute-start | bytes 49160 | tf_op jit(solution)/shard_map/ppermute | solution.py:335
